TPU v7x, 32 devices: a whole 2x2x4 slice. The times are simulated.
32 devices in a mesh: tm: 8 (over z, y), space: 4 (over x, core).
Axes of the slice: x: 2, y: 2, z: 4, core: 2. Of those that a mesh axis runs over, the one named last changes fastest.
Arguments:
- frames: bfloat16 [128, 16, 64, 384], P('tm', 'space'), may hold values from -6 to 6
- token_ids: int32 [1, 128, 16, 64], P(None, 'tm', 'space'), may hold values from 0 to 1023
- action_ids: int32 [128], P('tm'), may hold values from 0 to 7
- token_table: bfloat16 [1024, 384], replicated, may hold values from -6 to 6
- action_table: bfloat16 [8, 384], replicated, may hold values from -3 to 3
- conv_weight: bfloat16 [3, 3, 384], replicated, may hold values from -1.796875 to 1.796875
- norm_gain: bfloat16 [384], replicated, may hold values from 0.5 to 1.5
- w_query: bfloat16 [384, 384], replicated, may hold values from -12 to 12
- w_key: bfloat16 [384, 384], replicated, may hold values from -12 to 12
- w_value: bfloat16 [384, 384], replicated, may hold values from -0.3125 to 0.3125
- w_out: bfloat16 [384, 384], replicated, may hold values from -0.625 to 0.625
Outputs:
- final_frames: bfloat16 [128, 16, 64, 384], P('tm', 'space')
All inputs are finite; a program needn't handle non-finite values.
Results may differ from a plain program's by a relative error of at most 0.0057.
Values may be sent and summed in bfloat16 or wider, within the bound.
A program may use at most 192 MiB of HBM per device.

v0:
```python
import jax
import jax.numpy as jnp
from jax import lax
from jax.experimental import pallas as pl
from jax.experimental.pallas import tpu as pltpu
from jax.sharding import PartitionSpec as P

HEADS = 6
ACTIONS = 8
WINDOW = 16
ANCHORS = 4
GROUP = 16
F32 = jnp.float32
BF16 = jnp.bfloat16
NT = (((1,), (1,)), ((), ()))
VMEM_LIMIT = 48 * 1024 * 1024


def shift_cols(y, by):
    cols = y.shape[0]
    rolled = pltpu.roll(y, by % cols, 0)
    at = lax.broadcasted_iota(jnp.int32, y.shape, 0)
    edge = 0 if by == 1 else cols - 1
    return jnp.where(at == edge, 0.0, rolled)


def conv_norm(above, here, below, conv, gain):
    rows = [r.astype(F32) for r in (above, here, below)]
    sums = []
    for j in range(3):
        sums.append(
            rows[0] * conv[j : j + 1]
            + rows[1] * conv[3 + j : 4 + j]
            + rows[2] * conv[6 + j : 7 + j]
        )
    mixed = rows[1] + sums[1] + shift_cols(sums[0], 1) + shift_cols(sums[2], -1)
    scale = lax.rsqrt(jnp.mean(mixed * mixed, axis=-1, keepdims=True) + 1e-06)
    return mixed, (mixed * scale * gain).astype(BF16)


def embed_kernel(
    ids, frames, actions, table, conv_ref, gain_ref, emb, top, bottom, mixed, normed
):
    f = pl.program_id(0)
    row_count, cols, width = frames.shape[1:]
    vocab = table.shape[0]
    action = actions[pl.ds(f, 1), :]
    codes = lax.broadcasted_iota(jnp.int32, (cols, vocab), 1)
    rows = []
    for r in range(row_count):
        onehot = jnp.where(codes == ids[r * cols : (r + 1) * cols, :], 1.0, 0.0).astype(BF16)
        token = jnp.dot(onehot, table[...], preferred_element_type=F32)
        row = (frames[0, r].astype(F32) + token + action).astype(BF16)
        emb[0, r] = row
        rows.append(row)
    top[0] = rows[0]
    bottom[0] = rows[-1]
    conv = conv_ref[...]
    gain = gain_ref[...]
    for r in range(1, row_count - 1):
        m, n = conv_norm(rows[r - 1], rows[r], rows[r + 1], conv, gain)
        mixed[0, (r - 1) * cols : r * cols, :] = m
        normed[0, (r - 1) * cols : r * cols, :] = n


def edge_kernel(emb, before, after, conv_ref, gain_ref, mixed, normed):
    row_count, cols = emb.shape[1:3]
    conv = conv_ref[...]
    gain = gain_ref[...]
    m, n = conv_norm(before[0], emb[0, 0], emb[0, 1], conv, gain)
    mixed[0, :cols, :] = m
    normed[0, :cols, :] = n
    m, n = conv_norm(emb[0, row_count - 2], emb[0, row_count - 1], after[0], conv, gain)
    mixed[0, cols:, :] = m
    normed[0, cols:, :] = n


def attend_kernel(
    tm_ref, own, prev_lo, prev_hi, anchors, mixed, w_qkv, w_out, *rest
):
    out = rest[-1]
    tm = tm_ref[0]
    frame_count, group, width = own.shape
    rows = frame_count * group
    anchor_rows = ANCHORS * group
    x = own[...].reshape(rows, width)
    before = jnp.concatenate([prev_lo[...], prev_hi[...]], axis=0).reshape(rows, width)
    first = anchors[...].reshape(anchor_rows, width)
    qkv = jnp.dot(x, w_qkv[...], preferred_element_type=F32)
    q = (qkv[:, :width].astype(BF16) * 0.125).astype(BF16)
    kv_own = qkv[:, width:].astype(BF16)
    kv_prev = jnp.dot(before, w_qkv[:, width:], preferred_element_type=F32).astype(BF16)
    kv_anchor = jnp.dot(first, w_qkv[:, width:], preferred_element_type=F32).astype(BF16)

    at_q = lax.broadcasted_iota(jnp.int32, (rows, rows), 0)
    at_k = lax.broadcasted_iota(jnp.int32, (rows, rows), 1)
    causal = at_k // group <= at_q // group
    same = at_k % group == at_q % group
    bias = jnp.where(same & (causal | (tm > 0)), 0.0, -1e30)
    at_q = lax.broadcasted_iota(jnp.int32, (rows, anchor_rows), 0)
    at_k = lax.broadcasted_iota(jnp.int32, (rows, anchor_rows), 1)
    limit = tm * frame_count + at_q // group - (WINDOW - 1)
    seen = (at_k % group == at_q % group) & (at_k // group < limit)
    anchor_bias = jnp.where(seen, 0.0, -1e30)

    lane = lax.broadcasted_iota(jnp.int32, (rows, 128), 1)
    parts = []
    for pair in range(width // 128):
        at = slice(pair * 128, (pair + 1) * 128)
        at_v = slice(width + pair * 128, width + (pair + 1) * 128)
        halves = []
        for half in range(2):
            mine = (lane < 64) if half == 0 else (lane >= 64)
            qh = jnp.where(mine, q[:, at], jnp.zeros((), BF16))
            s_own = lax.dot_general(qh, kv_own[:, at], NT, preferred_element_type=F32)
            s_prev = lax.dot_general(qh, kv_prev[:, at], NT, preferred_element_type=F32)
            s_first = lax.dot_general(qh, kv_anchor[:, at], NT, preferred_element_type=F32)
            s = jnp.where(causal, s_own, s_prev) + bias
            s_first = s_first + anchor_bias
            top = jnp.maximum(
                jnp.max(s, axis=-1, keepdims=True), jnp.max(s_first, axis=-1, keepdims=True)
            )
            e = jnp.exp(s - top)
            e_first = jnp.exp(s_first - top)
            total = jnp.sum(e, axis=-1, keepdims=True) + jnp.sum(
                e_first, axis=-1, keepdims=True
            )
            e_own = jnp.where(causal, e, 0.0).astype(BF16)
            e_prev = jnp.where(causal, 0.0, e).astype(BF16)
            o = jnp.dot(e_own, kv_own[:, at_v], preferred_element_type=F32)
            o += jnp.dot(e_prev, kv_prev[:, at_v], preferred_element_type=F32)
            o += jnp.dot(
                e_first.astype(BF16), kv_anchor[:, at_v], preferred_element_type=F32
            )
            halves.append(o / total)
        parts.append(jnp.where(lane < 64, halves[0], halves[1]).astype(BF16))
    attended = jnp.concatenate(parts, axis=1)
    result = jnp.dot(attended, w_out[...], preferred_element_type=F32)
    result = result.reshape(frame_count, group, width) + mixed[...]
    out[...] = result.astype(BF16).reshape(out.shape)


def params():
    return pltpu.CompilerParams(vmem_limit_bytes=VMEM_LIMIT)


def embed(ids, frames, actions, table, conv, gain):
    count, row_count, cols, width = frames.shape
    strip = jax.ShapeDtypeStruct((count, cols, width), BF16)
    inner = (row_count - 2) * cols
    strip_spec = pl.BlockSpec((1, cols, width), lambda f: (f, 0, 0))
    inner_spec = pl.BlockSpec((1, inner, width), lambda f: (f, 0, 0))
    frame_spec = pl.BlockSpec((1, row_count, cols, width), lambda f: (f, 0, 0, 0))

    def whole(a):
        return pl.BlockSpec(a.shape, lambda f: (0,) * a.ndim)

    return pl.pallas_call(
        embed_kernel,
        grid=(count,),
        in_specs=[
            pl.BlockSpec((row_count * cols, 1), lambda f: (f, 0)),
            frame_spec,
            whole(actions),
            whole(table),
            whole(conv),
            whole(gain),
        ],
        out_specs=[frame_spec, strip_spec, strip_spec, inner_spec, inner_spec],
        out_shape=[
            jax.ShapeDtypeStruct(frames.shape, BF16),
            strip,
            strip,
            jax.ShapeDtypeStruct((count, inner, width), F32),
            jax.ShapeDtypeStruct((count, inner, width), BF16),
        ],
        compiler_params=params(),
        cost_estimate=pl.CostEstimate(
            flops=2 * ids.shape[0] * table.shape[0] * width,
            bytes_accessed=16 * 1024 * 1024,
            transcendentals=0,
        ),
        name="embed",
    )(ids, frames, actions, table, conv, gain)


def edge(emb, before, after, conv, gain):
    count, row_count, cols, width = emb.shape
    strip_spec = pl.BlockSpec((1, cols, width), lambda f: (f, 0, 0))
    edge_spec = pl.BlockSpec((1, 2 * cols, width), lambda f: (f, 0, 0))
    frame_spec = pl.BlockSpec((1, row_count, cols, width), lambda f: (f, 0, 0, 0))

    def whole(a):
        return pl.BlockSpec(a.shape, lambda f: (0,) * a.ndim)

    return pl.pallas_call(
        edge_kernel,
        grid=(count,),
        in_specs=[frame_spec, strip_spec, strip_spec, whole(conv), whole(gain)],
        out_specs=[edge_spec, edge_spec],
        out_shape=[
            jax.ShapeDtypeStruct((count, 2 * cols, width), F32),
            jax.ShapeDtypeStruct((count, 2 * cols, width), BF16),
        ],
        compiler_params=params(),
        cost_estimate=pl.CostEstimate(
            flops=20 * emb.size, bytes_accessed=16 * 1024 * 1024, transcendentals=0
        ),
        name="edge",
    )(emb, before, after, conv, gain)


def attend(tm, own, prev_lo, prev_hi, anchors, mixed, w_qkv, w_out, out, shape, row_of):
    count, positions, width = own.shape
    cols = shape[2]
    per_row = cols // GROUP

    def block(a):
        return pl.BlockSpec((a.shape[0], GROUP, width), lambda g: (0, g, 0))

    def whole(a):
        return pl.BlockSpec(a.shape, lambda g: (0, 0))

    args = [tm, own, prev_lo, prev_hi, anchors, mixed, w_qkv, w_out]
    specs = [pl.BlockSpec(memory_space=pltpu.SMEM)]
    specs += [block(a) for a in args[1:6]] + [whole(w_qkv), whole(w_out)]
    aliases = {}
    if out is not None:
        aliases = {len(args): 0}
        args.append(out)
        specs.append(pl.BlockSpec(memory_space=pl.ANY))
    return pl.pallas_call(
        attend_kernel,
        grid=(positions // GROUP,),
        in_specs=specs,
        out_specs=pl.BlockSpec(
            (count, 1, GROUP, width), lambda g: (0, row_of(g // per_row), g % per_row, 0)
        ),
        out_shape=jax.ShapeDtypeStruct(shape, BF16),
        input_output_aliases=aliases,
        compiler_params=params(),
        cost_estimate=pl.CostEstimate(
            flops=16_000_000_000, bytes_accessed=16 * 1024 * 1024, transcendentals=0
        ),
        name="attend",
    )(*args)


def send(x, by):
    count = lax.axis_size("tm")
    return lax.ppermute(x, "tm", [(i, i + by) for i in range(count - by)])


def window_of(normed, tm):
    count = lax.axis_size("tm")
    lo = send(normed[:ANCHORS], 1)
    hi = send(normed[ANCHORS:], 1)
    anchors = jnp.where(tm == 0, normed[:ANCHORS], lo)
    by = count // 2
    while by >= 2:
        pairs = [(i, i + by) for i in range(count - by) if i % (2 * by) < 2]
        got = lax.ppermute(anchors, "tm", pairs)
        place = tm % (2 * by)
        anchors = jnp.where((place == by) | (place == by + 1), got, anchors)
        by //= 2
    return lo, hi, anchors


def on_device(
    frames,
    token_ids,
    action_ids,
    token_table,
    action_table,
    conv_weight,
    norm_gain,
    w_query,
    w_key,
    w_value,
    w_out,
):
    shape = frames.shape
    width = shape[3]
    tm = lax.axis_index("tm")
    tm_arg = tm.astype(jnp.int32).reshape(1)
    ids = token_ids[0].reshape(-1, 1)
    onehot = (action_ids[:, None] == jnp.arange(ACTIONS, dtype=jnp.int32)[None, :]).astype(BF16)
    actions = jnp.dot(onehot, action_table, preferred_element_type=F32)
    conv = conv_weight.reshape(9, width).astype(F32)
    gain = norm_gain.reshape(1, width).astype(F32)
    w_qkv = jnp.concatenate([w_query, w_key, w_value], axis=1)

    emb, top, bottom, mixed_in, normed_in = embed(ids, frames, actions, token_table, conv, gain)
    strips = lax.axis_size("space")
    up = [(i, i + 1) for i in range(strips - 1)]
    before = lax.ppermute(bottom, "space", up)
    after = lax.ppermute(top, "space", [(j, i) for i, j in up])
    sent_in = window_of(normed_in, tm)
    mixed_edge, normed_edge = edge(emb, before, after, conv, gain)
    sent_edge = window_of(normed_edge, tm)
    last = shape[1] - 1
    out = attend(
        tm_arg, normed_in, *sent_in, mixed_in, w_qkv, w_out, None, shape, lambda r: r + 1
    )
    return attend(
        tm_arg, normed_edge, *sent_edge, mixed_edge, w_qkv, w_out, out, shape, lambda r: r * last
    )


def solution(mesh):
    in_specs = (
        P("tm", "space", None, None),
        P(None, "tm", "space", None),
        P("tm"),
        P(),
        P(),
        P(),
        P(),
        P(),
        P(),
        P(),
        P(),
    )
    out_specs = P("tm", "space", None, None)
    return jax.shard_map(
        on_device, mesh=mesh, in_specs=in_specs, out_specs=out_specs, check_vma=False
    )
```

profile of v0, /device:TPU:13, one launch (start us, length us, event | category | flops | bytes accessed | tf_op | source)
XLA Modules:
  0.0 176.3 jit_solution(7748855565779063900)
XLA Ops:
  1.5 4.2 %reshape_squeeze.4.ids = s32[4096,1]{1,0:T(8,128)} reshape(s32[1,16,4,64]{3,2,1,0:T(4,128)} %param.12) | data formatting | bytes 32768 | tf_op jit(solution)/shard_map/reshape;squeeze | solution.py:286
  5.9 1.6 copy-done.1
  7.5 15.7 %embed.1 = (bf16[16,4,64,384]{3,2,1,0:T(8,128)(2,1)}, bf16[16,64,384]{2,1,0:T(8,128)(2,1)}, bf16[16,64,384]{2,1,0:T(8,128)(2,1)}, f32[16,128,384]{2,1,0:T(8,128)}, bf16[16,128,384]{2,1,0:T(8,128)(2,1)S(1)}) custom-call(s32[4096,1]{1,0:T(8,128)S(1)} %copy-done.1, bf16[16,4,64,384]{3,2,1,0:T(8,128)(2,1)} %frames.1, f32[16,384]{1,0:T(8,128)S(1)} %fusion.actions, ...), custom_call_target="tpu_custom_call" | custom-call | flops 3221225472 | bytes 16777216 | tf_op jit(solution)/shard_map/embed/pallas_call | solution.py:158
  24.0 3.1 %collective-permute-start.6 = (bf16[4,128,384]{2,1,0:T(8,128)(2,1)}, bf16[4,128,384]{2,1,0:T(8,128)(2,1)S(1)}, u32[]{:S(2)}, u32[]{:S(2)}) collective-permute-start(bf16[4,128,384]{2,1,0:T(8,128)(2,1)} %slice.16), channel_id=1, source_target_pairs={{0,4},{4,8},{8,12},{12,16},{16,20},{20,24},{24,28},{1,5},{5,9},{9,... | collective-permute-start | bytes 1179656 | tf_op jit(solution)/shard_map/ppermute | solution.py:251
  27.1 4.0 %collective-permute-start = (bf16[16,64,384]{2,1,0:T(8,128)(2,1)}, bf16[16,64,384]{2,1,0:T(8,128)(2,1)S(1)}, u32[]{:S(2)}, u32[]{:S(2)}) collective-permute-start(bf16[16,64,384]{2,1,0:T(8,128)(2,1)} %get-tuple-element.13), channel_id=1, source_target_pairs={{0,1},{1,2},{2,3},{4,5},{5,6},{6,7},{8,9},{9,10},{10,11},{12,13},{... | collective-permute-start | bytes 2359304 | tf_op jit(solution)/shard_map/ppermute | solution.py:296
  31.1 1.9 %collective-permute-start.1 = (bf16[16,64,384]{2,1,0:T(8,128)(2,1)}, bf16[16,64,384]{2,1,0:T(8,128)(2,1)S(1)}, u32[]{:S(2)}, u32[]{:S(2)}) collective-permute-start(bf16[16,64,384]{2,1,0:T(8,128)(2,1)} %get-tuple-element.14), channel_id=1, source_target_pairs={{1,0},{2,1},{3,2},{5,4},{6,5},{7,6},{9,8},{10,9},{11,10},{13,12},{... | collective-permute-start | bytes 2359304 | tf_op jit(solution)/shard_map/ppermute | solution.py:297
  33.0 3.0 %collective-permute-done.6.prev_lo = bf16[4,128,384]{2,1,0:T(8,128)(2,1)S(1)} collective-permute-done((bf16[4,128,384]{2,1,0:T(8,128)(2,1)}, bf16[4,128,384]{2,1,0:T(8,128)(2,1)S(1)}, u32[]{:S(2)}, u32[]{:S(2)}) %collective-permute-start.6) | collective-permute-done | bytes 393248 | tf_op jit(solution)/shard_map/ppermute | solution.py:251
  36.9 1.4 collective-permute-start.8
  38.3 2.0 %collective-permute-done.before = bf16[16,64,384]{2,1,0:T(8,128)(2,1)S(1)} collective-permute-done((bf16[16,64,384]{2,1,0:T(8,128)(2,1)}, bf16[16,64,384]{2,1,0:T(8,128)(2,1)S(1)}, u32[]{:S(2)}, u32[]{:S(2)}) %collective-permute-start) | collective-permute-done | bytes 786464 | tf_op jit(solution)/shard_map/ppermute | solution.py:296
  40.3 0.9 copy-done.2
  41.2 3.4 %collective-permute-done.1.after = bf16[16,64,384]{2,1,0:T(8,128)(2,1)S(1)} collective-permute-done((bf16[16,64,384]{2,1,0:T(8,128)(2,1)}, bf16[16,64,384]{2,1,0:T(8,128)(2,1)S(1)}, u32[]{:S(2)}, u32[]{:S(2)}) %collective-permute-start.1) | collective-permute-done | bytes 786464 | tf_op jit(solution)/shard_map/ppermute | solution.py:297
  44.6 0.9 copy-done.4
  45.5 1.1 copy-done.3
  46.6 1.1 copy-done.5
  48.5 11.0 %edge.1 = (f32[16,128,384]{2,1,0:T(8,128)}, bf16[16,128,384]{2,1,0:T(8,128)(2,1)S(1)}) custom-call(bf16[16,4,64,384]{3,2,1,0:T(8,128)(2,1)} %get-tuple-element.12.emb, bf16[16,64,384]{2,1,0:T(8,128)(2,1)S(1)} %copy-done.3, bf16[16,64,384]{2,1,0:T(8,128)(2,1)S(1)} %copy-done.5, f32[9,384]{1,0:T(8,128)S(1)} %copy-done.7, f32[1,384]{1,0:T(1,128)S(1)} %reshape.12.gain_ref), custom_call_target="tpu_custom_call" | custom-call | flops 31457280 | bytes 16777216 | tf_op jit(solution)/shard_map/edge/pallas_call | solution.py:196
  60.3 3.1 %collective-permute-start.2 = (bf16[4,128,384]{2,1,0:T(8,128)(2,1)}, bf16[4,128,384]{2,1,0:T(8,128)(2,1)}, u32[]{:S(2)}, u32[]{:S(2)}) collective-permute-start(bf16[4,128,384]{2,1,0:T(8,128)(2,1)} %slice.14), channel_id=1, source_target_pairs={{0,4},{4,8},{8,12},{12,16},{16,20},{20,24},{24,28},{1,5},{5,9},{9,... | collective-permute-start | bytes 1179656 | tf_op jit(solution)/shard_map/ppermute | solution.py:251
  63.4 1.1 slice.17
  64.6 3.5 %collective-permute-start.7 = (bf16[12,128,384]{2,1,0:T(8,128)(2,1)}, bf16[12,128,384]{2,1,0:T(8,128)(2,1)}, u32[]{:S(2)}, u32[]{:S(2)}) collective-permute-start(bf16[12,128,384]{2,1,0:T(8,128)(2,1)} %slice.17), channel_id=1, source_target_pairs={{0,4},{4,8},{8,12},{12,16},{16,20},{20,24},{24,28},{1,5},{5,9},{9,... | collective-permute-start | bytes 3538952 | tf_op jit(solution)/shard_map/ppermute | solution.py:251
  68.2 1.8 %constant_dynamic-update-slice_fusion.2 = bf16[384,1152]{1,0:T(8,128)(2,1)} fusion(bf16[384,384]{1,0:T(8,128)(2,1)} %param.18), kind=kLoop, calls=%fused_computation.8 | loop fusion | bytes 589824
  70.0 1.8 %broadcast_select_fusion.2 = bf16[4,128,384]{2,1,0:T(8,128)(2,1)} fusion(bf16[4,128,384]{2,1,0:T(8,128)(2,1)} %collective-permute-done.8, bf16[4,128,384]{2,1,0:T(8,128)(2,1)} %broadcast_select_fusion, pred[]{:T(512)S(6)} %or.9), kind=kLoop, calls=%fused_computation.2 | loop fusion | flops 196608 | bytes 1179649 | tf_op jit(solution)/shard_map/jit(_where)/select_n | solution.py:264
  71.8 1.3 collective-permute-start.9
  73.2 1.8 %broadcast_select_fusion.1 = bf16[4,128,384]{2,1,0:T(8,128)(2,1)} fusion(bf16[4,128,384]{2,1,0:T(8,128)(2,1)} %collective-permute-done.2.prev_lo, pred[]{:T(512)S(6)} %eq.45, bf16[16,128,384]{2,1,0:T(8,128)(2,1)S(1)} %get-tuple-element.15.own), kind=kLoop, calls=%fused_computation.1 | loop fusion | flops 196608 | bytes 1179649 | tf_op jit(solution)/shard_map/jit(_where)/select_n | solution.py:258
  75.0 1.4 collective-permute-start.4
  77.3 1.8 %constant_dynamic-update-slice_fusion.w_qkv = bf16[384,1152]{1,0:T(8,128)(2,1)} fusion(bf16[384,1152]{1,0:T(8,128)(2,1)} %constant_dynamic-update-slice_fusion.1, bf16[384,384]{1,0:T(8,128)(2,1)} %param.20), kind=kLoop, calls=%fused_computation.6 | loop fusion | bytes 589824 | tf_op jit(solution)/shard_map/concatenate | solution.py:291
  79.2 4.5 %collective-permute-start.3 = (bf16[12,128,384]{2,1,0:T(8,128)(2,1)S(1)}, bf16[12,128,384]{2,1,0:T(8,128)(2,1)S(1)}, u32[]{:S(2)}, u32[]{:S(2)}) collective-permute-start(bf16[12,128,384]{2,1,0:T(8,128)(2,1)S(1)} %slice.15), channel_id=1, source_target_pairs={{0,4},{4,8},{8,12},{12,16},{16,20},{20,24},{24,28},{1,5},{5,9},{9,... | collective-permute-start | bytes 3538952 | tf_op jit(solution)/shard_map/ppermute | solution.py:251
  83.7 23.4 %collective-permute-done.9 = bf16[4,128,384]{2,1,0:T(8,128)(2,1)} collective-permute-done((bf16[4,128,384]{2,1,0:T(8,128)(2,1)}, bf16[4,128,384]{2,1,0:T(8,128)(2,1)}, u32[]{:S(2)}, u32[]{:S(2)}) %collective-permute-start.9) | collective-permute-done | bytes 393248 | tf_op jit(solution)/shard_map/ppermute | solution.py:262
  107.2 1.0 broadcast_select_fusion.4.anchors
  108.2 1.1 broadcast_select_fusion.3
  109.3 1.3 collective-permute-start.5
  110.6 28.3 %attend.2.rest_0_ = bf16[16,4,64,384]{3,2,1,0:T(8,128)(2,1)} custom-call(s32[1]{0:T(128)} %bitcast.tm_ref, bf16[16,128,384]{2,1,0:T(8,128)(2,1)S(1)} %get-tuple-element.17.own, bf16[4,128,384]{2,1,0:T(8,128)(2,1)S(1)} %collective-permute-done.6.prev_lo, bf16[12,128,384]{2,1,0:T(8,128)(2,1)} %collective-permute-done.7.prev_hi, ...), custom_call_target="tpu_custom_call" | custom-call | flops 16000000000 | bytes 16777216 | tf_op jit(solution)/shard_map/attend/pallas_call | solution.py:232
  138.9 9.1 %collective-permute-done.5 = bf16[4,128,384]{2,1,0:T(8,128)(2,1)S(1)} collective-permute-done((bf16[4,128,384]{2,1,0:T(8,128)(2,1)S(1)}, bf16[4,128,384]{2,1,0:T(8,128)(2,1)S(1)}, u32[]{:S(2)}, u32[]{:S(2)}) %collective-permute-start.5) | collective-permute-done | bytes 393248 | tf_op jit(solution)/shard_map/ppermute | solution.py:262
  148.0 28.3 %attend.3 = bf16[16,4,64,384]{3,2,1,0:T(8,128)(2,1)} custom-call(s32[1]{0:T(128)} %bitcast.tm_ref, bf16[16,128,384]{2,1,0:T(8,128)(2,1)S(1)} %get-tuple-element.15.own, bf16[4,128,384]{2,1,0:T(8,128)(2,1)} %collective-permute-done.2.prev_lo, bf16[12,128,384]{2,1,0:T(8,128)(2,1)S(1)} %collective-permute-done.3.prev_hi, ...), custom_call_target="tpu_custom_call", output_to_operand_aliasing={{}: (8, {})} | custom-call | flops 16000000000 | bytes 16777216 | tf_op jit(solution)/shard_map/attend/pallas_call | solution.py:232
  (33 shorter events, 6.0 us)
Async XLA Ops:
  0.0 5.7 %copy-start = (bf16[8,384]{1,0:T(8,128)(2,1)S(1)}, bf16[8,384]{1,0:T(8,128)(2,1)}, u32[]{:S(2)}) copy-start(bf16[8,384]{1,0:T(8,128)(2,1)} %param.15) | copy-start | bytes 18436
  0.0 5.7 %copy-start.11 = (s32[16]{0:T(128)S(1)}, s32[16]{0:T(128)}, u32[]{:S(2)}) copy-start(s32[16]{0:T(128)} %param.13) | copy-start | bytes 196
  0.0 5.9 %copy-start.8 = (bf16[1024,384]{1,0:T(8,128)(2,1)S(1)}, bf16[1024,384]{1,0:T(8,128)(2,1)}, u32[]{:S(2)}) copy-start(bf16[1024,384]{1,0:T(8,128)(2,1)} %table.1) | copy-start | bytes 2359300
  0.8 22.4 %copy-start.6 = (f32[9,384]{1,0:T(8,128)}, f32[9,384]{1,0:T(8,128)S(1)}, u32[]{:S(2)}) copy-start(f32[9,384]{1,0:T(8,128)S(1)} %reshape.11.conv_ref) | copy-start | bytes 41476
  5.9 1.6 copy-start.1
  24.0 12.1 %collective-permute-start.6 = (bf16[4,128,384]{2,1,0:T(8,128)(2,1)}, bf16[4,128,384]{2,1,0:T(8,128)(2,1)S(1)}, u32[]{:S(2)}, u32[]{:S(2)}) collective-permute-start(bf16[4,128,384]{2,1,0:T(8,128)(2,1)} %slice.16), channel_id=1, source_target_pairs={{0,4},{4,8},{8,12},{12,16},{16,20},{20,24},{24,28},{1,5},{5,9},{9,... | collective-permute-start | bytes 1179656 | tf_op jit(solution)/shard_map/ppermute | solution.py:251
  27.1 13.2 %collective-permute-start = (bf16[16,64,384]{2,1,0:T(8,128)(2,1)}, bf16[16,64,384]{2,1,0:T(8,128)(2,1)S(1)}, u32[]{:S(2)}, u32[]{:S(2)}) collective-permute-start(bf16[16,64,384]{2,1,0:T(8,128)(2,1)} %get-tuple-element.13), channel_id=1, source_target_pairs={{0,1},{1,2},{2,3},{4,5},{5,6},{6,7},{8,9},{9,10},{10,11},{12,13},{... | collective-permute-start | bytes 2359304 | tf_op jit(solution)/shard_map/ppermute | solution.py:296
  31.1 13.5 %collective-permute-start.1 = (bf16[16,64,384]{2,1,0:T(8,128)(2,1)}, bf16[16,64,384]{2,1,0:T(8,128)(2,1)S(1)}, u32[]{:S(2)}, u32[]{:S(2)}) collective-permute-start(bf16[16,64,384]{2,1,0:T(8,128)(2,1)} %get-tuple-element.14), channel_id=1, source_target_pairs={{1,0},{2,1},{3,2},{5,4},{6,5},{7,6},{9,8},{10,9},{11,10},{13,12},{... | collective-permute-start | bytes 2359304 | tf_op jit(solution)/shard_map/ppermute | solution.py:297
  36.9 33.1 %collective-permute-start.8 = (bf16[4,128,384]{2,1,0:T(8,128)(2,1)}, bf16[4,128,384]{2,1,0:T(8,128)(2,1)}, u32[]{:S(2)}, u32[]{:S(2)}) collective-permute-start(bf16[4,128,384]{2,1,0:T(8,128)(2,1)} %broadcast_select_fusion), channel_id=1, source_target_pairs={{0,16},{4,20},{1,17},{5,21},{2,18},{6,22},{3,19},{7,23}} | collective-permute-start | bytes 1179656 | tf_op jit(solution)/shard_map/ppermute | solution.py:262
  40.3 0.9 copy-start.2
  44.6 0.9 copy-start.4
  45.5 1.1 copy-start.3
  46.6 1.1 copy-start.5
  47.8 0.7 copy-start.7
  60.3 12.9 %collective-permute-start.2 = (bf16[4,128,384]{2,1,0:T(8,128)(2,1)}, bf16[4,128,384]{2,1,0:T(8,128)(2,1)}, u32[]{:S(2)}, u32[]{:S(2)}) collective-permute-start(bf16[4,128,384]{2,1,0:T(8,128)(2,1)} %slice.14), channel_id=1, source_target_pairs={{0,4},{4,8},{8,12},{12,16},{16,20},{20,24},{24,28},{1,5},{5,9},{9,... | collective-permute-start | bytes 1179656 | tf_op jit(solution)/shard_map/ppermute | solution.py:251
  64.6 46.0 %collective-permute-start.7 = (bf16[12,128,384]{2,1,0:T(8,128)(2,1)}, bf16[12,128,384]{2,1,0:T(8,128)(2,1)}, u32[]{:S(2)}, u32[]{:S(2)}) collective-permute-start(bf16[12,128,384]{2,1,0:T(8,128)(2,1)} %slice.17), channel_id=1, source_target_pairs={{0,4},{4,8},{8,12},{12,16},{16,20},{20,24},{24,28},{1,5},{5,9},{9,... | collective-permute-start | bytes 3538952 | tf_op jit(solution)/shard_map/ppermute | solution.py:251
  68.1 8.3 %copy-start.10 = (bf16[384,384]{1,0:T(8,128)(2,1)S(1)}, bf16[384,384]{1,0:T(8,128)(2,1)}, u32[]{:S(2)}) copy-start(bf16[384,384]{1,0:T(8,128)(2,1)} %param.19) | copy-start | bytes 884740
  71.8 35.4 %collective-permute-start.9 = (bf16[4,128,384]{2,1,0:T(8,128)(2,1)}, bf16[4,128,384]{2,1,0:T(8,128)(2,1)}, u32[]{:S(2)}, u32[]{:S(2)}) collective-permute-start(bf16[4,128,384]{2,1,0:T(8,128)(2,1)} %broadcast_select_fusion.2), channel_id=1, source_target_pairs={{0,8},{4,12},{16,24},{20,28},{1,9},{5,13},{17,25},{21,29},{2,10},{... | collective-permute-start | bytes 1179656 | tf_op jit(solution)/shard_map/ppermute | solution.py:262
  75.0 33.2 %collective-permute-start.4 = (bf16[4,128,384]{2,1,0:T(8,128)(2,1)}, bf16[4,128,384]{2,1,0:T(8,128)(2,1)}, u32[]{:S(2)}, u32[]{:S(2)}) collective-permute-start(bf16[4,128,384]{2,1,0:T(8,128)(2,1)} %broadcast_select_fusion.1), channel_id=1, source_target_pairs={{0,16},{4,20},{1,17},{5,21},{2,18},{6,22},{3,19},{7,23}} | collective-permute-start | bytes 1179656 | tf_op jit(solution)/shard_map/ppermute | solution.py:262
  79.2 31.4 %copy-start.9 = (bf16[384,384]{1,0:T(8,128)(2,1)S(1)}, bf16[384,384]{1,0:T(8,128)(2,1)}, u32[]{:S(2)}) copy-start(bf16[384,384]{1,0:T(8,128)(2,1)} %w_out.3) | copy-start | bytes 884740
  79.2 68.8 %collective-permute-start.3 = (bf16[12,128,384]{2,1,0:T(8,128)(2,1)S(1)}, bf16[12,128,384]{2,1,0:T(8,128)(2,1)S(1)}, u32[]{:S(2)}, u32[]{:S(2)}) collective-permute-start(bf16[12,128,384]{2,1,0:T(8,128)(2,1)S(1)} %slice.15), channel_id=1, source_target_pairs={{0,4},{4,8},{8,12},{12,16},{16,20},{20,24},{24,28},{1,5},{5,9},{9,... | collective-permute-start | bytes 3538952 | tf_op jit(solution)/shard_map/ppermute | solution.py:251
  109.3 38.7 %collective-permute-start.5 = (bf16[4,128,384]{2,1,0:T(8,128)(2,1)S(1)}, bf16[4,128,384]{2,1,0:T(8,128)(2,1)S(1)}, u32[]{:S(2)}, u32[]{:S(2)}) collective-permute-start(bf16[4,128,384]{2,1,0:T(8,128)(2,1)S(1)} %broadcast_select_fusion.3), channel_id=1, source_target_pairs={{0,8},{4,12},{16,24},{20,28},{1,9},{5,13},{17,25},{21,29},{2,10},{... | collective-permute-start | bytes 1179656 | tf_op jit(solution)/shard_map/ppermute | solution.py:262
where the time goes:
time: 178 us; the launch traced here: 176 us
  Pallas kernels  83.3 us (47%)
  waiting for transfers between devices  41.2 us (23%)
  starting transfers between devices  25.6 us (14%)
  local copies, waits for them, and re-layouts  19.3 us (11%)
  other arithmetic  6.56 us (4%)
    pallas_call x2, Pallas kernels, attend(): pl.pallas_call(attend_kernel, grid=(positions // GROUP,), in_specs=specs,...  56.6 us
    ppermute x4, waiting for transfers between devices, window_of(): got = lax.ppermute(anchors, 'tm', pairs)  32.5 us
    pallas_call x1, Pallas kernels, embed(): pl.pallas_call(embed_kernel, grid=(count,), in_specs=[pl.BlockSpec((row_c...  15.7 us
    ppermute x4, starting transfers between devices, send(): return lax.ppermute(x, 'tm', [(i, i + by) for i in range(count - by)])  14.3 us
    pallas_call x1, Pallas kernels, edge(): pl.pallas_call(edge_kernel, grid=(count,), in_specs=[frame_spec, strip_sp...  11 us
    unnamed x26, local copies, waits for them, and re-layouts  9.06 us
    ppermute x4, starting transfers between devices, window_of(): got = lax.ppermute(anchors, 'tm', pairs)  5.42 us
    another operation x1, local copies, waits for them, and re-layouts, on_device(): ids = token_ids[0].reshape(-1, 1)  4.17 us
  transfers between devices with their start and end apart: 10, of which 6 were waited for; matrix products, arithmetic and copies ran while one was open for 7% of the time, Pallas kernels for 22%

commit v1 on v0

v1 whole, which is shorter than its diff:
```python
import jax
import jax.numpy as jnp
from jax import lax
from jax.experimental import pallas as pl
from jax.experimental.pallas import tpu as pltpu
from jax.sharding import PartitionSpec as P

HEADS = 6
ACTIONS = 8
WINDOW = 16
ANCHORS = 4
GROUP = 8
F32 = jnp.float32
BF16 = jnp.bfloat16
NT = (((1,), (1,)), ((), ()))
TN = (((0,), (0,)), ((), ()))
VMEM_LIMIT = 48 * 1024 * 1024


def shift_cols(y, by):
    cols = y.shape[0]
    rolled = pltpu.roll(y, by % cols, 0)
    at = lax.broadcasted_iota(jnp.int32, y.shape, 0)
    edge = 0 if by == 1 else cols - 1
    return jnp.where(at == edge, 0.0, rolled)


def conv_norm(above, here, below, conv, gain):
    rows = [r.astype(F32) for r in (above, here, below)]
    sums = []
    for j in range(3):
        sums.append(
            rows[0] * conv[j : j + 1]
            + rows[1] * conv[3 + j : 4 + j]
            + rows[2] * conv[6 + j : 7 + j]
        )
    mixed = rows[1] + sums[1] + shift_cols(sums[0], 1) + shift_cols(sums[2], -1)
    scale = lax.rsqrt(jnp.mean(mixed * mixed, axis=-1, keepdims=True) + 1e-06)
    return mixed, mixed * scale * gain


def grouped(first, second):
    width = first.shape[-1]
    first = first.reshape(-1, GROUP, width)
    second = second.reshape(-1, GROUP, width)
    return jnp.concatenate([first, second], axis=1)


def put_rows(results, mixed, normed, rolled):
    frame = pl.program_id(0) * 2
    turned = []
    for k in range(2):
        n = results[k][1].reshape(-1, GROUP, results[k][1].shape[-1])
        turned.append(pltpu.roll(n, lax.rem(frame + k, GROUP), 1))
    mixed[...] = grouped(results[0][0], results[1][0])
    normed[...] = grouped(results[0][1], results[1][1]).astype(BF16)
    rolled[...] = jnp.concatenate(turned, axis=1).astype(BF16)


def embed_kernel(
    ids, frames, actions, table, conv_ref, gain_ref, emb, top, bottom, mixed, normed, rolled
):
    step = pl.program_id(0)
    row_count, cols, width = frames.shape[1:]
    vocab = table.shape[0]
    count = 2 * row_count * cols
    row_ids = ids[0].astype(F32)
    codes = jnp.transpose(jnp.broadcast_to(row_ids, (128, count)), (1, 0))
    lane = lax.broadcasted_iota(jnp.int32, (count, 128), 1).astype(F32)
    onehot = [
        jnp.where(codes == lane + 128.0 * k, 1.0, 0.0).astype(BF16) for k in range(vocab // 128)
    ]
    tokens = jnp.dot(jnp.concatenate(onehot, axis=1), table[...], preferred_element_type=F32)
    conv = conv_ref[...]
    gain = gain_ref[...]
    results = []
    for k in range(2):
        action = actions[pl.ds(step * 2 + k, 1), :]
        rows = []
        for r in range(row_count):
            at = (k * row_count + r) * cols
            row = frames[k, r].astype(F32) + tokens[at : at + cols] + action
            row = row.astype(BF16)
            emb[k, r] = row
            rows.append(row)
        top[k] = rows[0]
        bottom[k] = rows[-1]
        done = [
            conv_norm(rows[r - 1], rows[r], rows[r + 1], conv, gain)
            for r in range(1, row_count - 1)
        ]
        results.append([jnp.concatenate(part, axis=0) for part in zip(*done)])
    put_rows(results, mixed, normed, rolled)


def edge_kernel(emb, before, after, conv_ref, gain_ref, mixed, normed, rolled):
    row_count = emb.shape[1]
    conv = conv_ref[...]
    gain = gain_ref[...]
    results = []
    for k in range(2):
        done = [
            conv_norm(before[k], emb[k, 0], emb[k, 1], conv, gain),
            conv_norm(emb[k, row_count - 2], emb[k, row_count - 1], after[k], conv, gain),
        ]
        results.append([jnp.concatenate(part, axis=0) for part in zip(*done)])
    put_rows(results, mixed, normed, rolled)


def attend_kernel(
    tm_ref, x_ref, own, lo, hi, anchors, mixed, wq_t, wk, wv_t, w_out, *rest
):
    out, mask = rest[-2:]
    tm = tm_ref[0]
    width = x_ref.shape[-1]
    queries = WINDOW * GROUP
    lanes = 2 * queries
    slabs = 2 * WINDOW + ANCHORS

    @pl.when(pl.program_id(0) == 0)
    def _():
        row = lax.broadcasted_iota(jnp.int32, (slabs * GROUP, lanes), 0)
        lane = lax.broadcasted_iota(jnp.int32, (slabs * GROUP, lanes), 1)
        u = row // GROUP
        t = (lane % queries) // GROUP
        met = (row - lane + lanes) % GROUP
        mine = (u < WINDOW) & (u % GROUP == met) & (u <= t)
        past = (u >= WINDOW) & (u < 2 * WINDOW) & (u % GROUP == met) & (u - WINDOW > t)
        first = (u >= 2 * WINDOW) & (u - 2 * WINDOW == met)
        mask[...] = jnp.where(mine | past | first, 1.0, 0.0).astype(BF16)

    sub = lax.broadcasted_iota(jnp.int32, (GROUP, lanes), 0)
    lane = lax.broadcasted_iota(jnp.int32, (GROUP, lanes), 1)
    t = (lane % queries) // GROUP
    met = (sub - lane + lanes) % GROUP
    places = []
    for b in range(WINDOW // GROUP):
        u = met + b * GROUP
        places.append(jnp.where(u <= t, u, u + WINDOW))
    open_window = [(c < WINDOW) | (tm > 0) for c in places]
    open_anchor = (met < ANCHORS) & (met < tm * WINDOW + t - (WINDOW - 1))

    x = x_ref[...].reshape(-1, width)
    q_t = lax.dot_general(wq_t[...], x, NT, preferred_element_type=F32).astype(BF16)
    q_t = (q_t * 0.125).astype(BF16)
    anchor_rows = ANCHORS * GROUP
    va_t = lax.dot_general(
        wv_t[...], anchors[...].reshape(2 * anchor_rows, width), NT, preferred_element_type=F32
    ).astype(BF16)
    blank = jnp.zeros((64, queries), BF16)
    no_rows = jnp.zeros((anchor_rows, lanes), BF16)
    results = []
    for i in range(2):
        window = jnp.concatenate([own[i], lo[i], hi[i]], axis=0)
        keys = jnp.concatenate([window, anchors[i]], axis=0)
        k = jnp.dot(keys, wk[...], preferred_element_type=F32).astype(BF16)
        v_t = lax.dot_general(wv_t[...], window, NT, preferred_element_type=F32).astype(BF16)
        parts = []
        for pair in range(width // 128):
            at = pair * 128
            across = slice(i * queries, (i + 1) * queries)
            left = jnp.concatenate([q_t[at : at + 64, across], blank], axis=0)
            right = jnp.concatenate([blank, q_t[at + 64 : at + 128, across]], axis=0)
            s = jnp.dot(
                k[:, at : at + 128],
                jnp.concatenate([left, right], axis=1),
                preferred_element_type=F32,
            )
            s = [s[j * GROUP : (j + 1) * GROUP] for j in range(slabs)]
            merged = []
            for b in range(WINDOW // GROUP):
                w = s[b * GROUP]
                for d in range(GROUP):
                    u = b * GROUP + d
                    if d > 0:
                        w = jnp.where(places[b] == u, s[u], w)
                    w = jnp.where(places[b] == WINDOW + u, s[WINDOW + u], w)
                merged.append(jnp.where(open_window[b], w, -1e30))
            w = s[2 * WINDOW]
            for u in range(1, ANCHORS):
                w = jnp.where(met == u, s[2 * WINDOW + u], w)
            merged.append(jnp.where(open_anchor, w, -1e30))
            top = jnp.max(
                jnp.maximum(jnp.maximum(merged[0], merged[1]), merged[2]), axis=0, keepdims=True
            )
            e = [jnp.exp(w - top) for w in merged]
            total = jnp.sum(e[0] + e[1] + e[2], axis=0, keepdims=True)
            over = 1.0 / total
            p = [w * over for w in e]
            p = [jnp.concatenate([w, w], axis=0).astype(BF16) for w in p]
            spread = []
            for j in range(slabs // 2):
                b = (2 * j % WINDOW) // GROUP if j < WINDOW else 2
                spread.append(p[b] * mask[j * 16 : (j + 1) * 16, :])
            p_window = jnp.concatenate(spread[:WINDOW], axis=0)
            p_first = jnp.concatenate(spread[WINDOW:], axis=0)
            p_first = [p_first, no_rows] if i == 0 else [no_rows, p_first]
            o = jnp.dot(v_t[at : at + 128], p_window, preferred_element_type=F32)
            o += jnp.dot(
                va_t[at : at + 128],
                jnp.concatenate(p_first, axis=0),
                preferred_element_type=F32,
            )
            parts += [o[:64, :queries], o[64:, queries:]]
        attended = jnp.concatenate(parts, axis=0).astype(BF16)
        result = lax.dot_general(attended, w_out[...], TN, preferred_element_type=F32)
        results.append((result + mixed[i]).reshape(WINDOW, GROUP, width))
    out[...] = jnp.concatenate(results, axis=1).astype(BF16).reshape(out.shape)


def params():
    return pltpu.CompilerParams(vmem_limit_bytes=VMEM_LIMIT)


def small():
    return pl.CostEstimate(flops=1000, bytes_accessed=1000, transcendentals=0)


def whole(a):
    return pl.BlockSpec(a.shape, lambda f: (0,) * a.ndim)


def row_outputs(count, positions, width):
    groups = positions // GROUP
    spec = pl.BlockSpec((groups, 2 * GROUP, width), lambda f: (0, f, 0))
    shapes = [
        jax.ShapeDtypeStruct((groups, count * GROUP, width), dtype) for dtype in (F32, BF16, BF16)
    ]
    return [spec] * 3, shapes


def embed(ids, frames, actions, table, conv, gain):
    count, row_count, cols, width = frames.shape
    strip = jax.ShapeDtypeStruct((count, cols, width), BF16)
    strip_spec = pl.BlockSpec((2, cols, width), lambda f: (f, 0, 0))
    frame_spec = pl.BlockSpec((2, row_count, cols, width), lambda f: (f, 0, 0, 0))
    specs, shapes = row_outputs(count, (row_count - 2) * cols, width)
    return pl.pallas_call(
        embed_kernel,
        grid=(count // 2,),
        in_specs=[
            pl.BlockSpec((1, 1, 2 * row_count * cols), lambda f: (f, 0, 0)),
            frame_spec,
            whole(actions),
            whole(table),
            whole(conv),
            whole(gain),
        ],
        out_specs=[frame_spec, strip_spec, strip_spec] + specs,
        out_shape=[jax.ShapeDtypeStruct(frames.shape, BF16), strip, strip] + shapes,
        compiler_params=params(),
        cost_estimate=small(),
        name="embed",
    )(ids, frames, actions, table, conv, gain)


def edge(emb, before, after, conv, gain):
    count, row_count, cols, width = emb.shape
    strip_spec = pl.BlockSpec((2, cols, width), lambda f: (f, 0, 0))
    frame_spec = pl.BlockSpec((2, row_count, cols, width), lambda f: (f, 0, 0, 0))
    specs, shapes = row_outputs(count, 2 * cols, width)
    return pl.pallas_call(
        edge_kernel,
        grid=(count // 2,),
        in_specs=[frame_spec, strip_spec, strip_spec, whole(conv), whole(gain)],
        out_specs=specs,
        out_shape=shapes,
        compiler_params=params(),
        cost_estimate=small(),
        name="edge",
    )(emb, before, after, conv, gain)


def attend(tm, blocks, weights, out, shape, row_of):
    count, _, cols, width = shape
    positions = blocks[0].shape[0] * GROUP
    per_row = cols // (2 * GROUP)

    def block(a):
        return pl.BlockSpec((2,) + a.shape[1:], lambda g: (g, 0, 0))

    args = [tm, *blocks, *weights]
    specs = [pl.BlockSpec(memory_space=pltpu.SMEM)]
    specs += [block(a) for a in blocks] + [whole(w) for w in weights]
    aliases = {}
    if out is not None:
        aliases = {len(args): 0}
        args.append(out)
        specs.append(pl.BlockSpec(memory_space=pl.ANY))
    return pl.pallas_call(
        attend_kernel,
        grid=(positions // (2 * GROUP),),
        in_specs=specs,
        out_specs=pl.BlockSpec(
            (count, 1, 2 * GROUP, width), lambda g: (0, row_of(g // per_row), g % per_row, 0)
        ),
        out_shape=jax.ShapeDtypeStruct(shape, BF16),
        scratch_shapes=[
            pltpu.VMEM(((2 * WINDOW + ANCHORS) * GROUP, 2 * WINDOW * GROUP), BF16)
        ],
        input_output_aliases=aliases,
        compiler_params=params(),
        cost_estimate=small(),
        name="attend",
    )(*args)


def send(x, by):
    count = lax.axis_size("tm")
    return lax.ppermute(x, "tm", [(i, i + by) for i in range(count - by)])


def window_of(normed, tm, after=None):
    count = lax.axis_size("tm")
    first = normed[:, : ANCHORS * GROUP]
    if after is not None:
        first, after = lax.optimization_barrier((first, after))
    lo = send(first, 1)
    hi = send(normed[:, ANCHORS * GROUP :], 1)
    anchors = jnp.where(tm == 0, first, lo)
    by = count // 2
    while by >= 2:
        pairs = [(i, i + by) for i in range(count - by) if i % (2 * by) < 2]
        got = lax.ppermute(anchors, "tm", pairs)
        place = tm % (2 * by)
        anchors = jnp.where((place == by) | (place == by + 1), got, anchors)
        by //= 2
    return lo, hi, anchors


def on_device(
    frames,
    token_ids,
    action_ids,
    token_table,
    action_table,
    conv_weight,
    norm_gain,
    w_query,
    w_key,
    w_value,
    w_out,
):
    shape = frames.shape
    width = shape[3]
    tm = lax.axis_index("tm")
    tm_arg = tm.astype(jnp.int32).reshape(1)
    ids = token_ids.reshape(shape[0] // 2, 1, -1)
    onehot = (action_ids[:, None] == jnp.arange(ACTIONS, dtype=jnp.int32)[None, :]).astype(BF16)
    actions = jnp.dot(onehot, action_table, preferred_element_type=F32)
    conv = conv_weight.reshape(9, width).astype(F32)
    gain = norm_gain.reshape(1, width).astype(F32)
    weights = [w_query.T, w_key, w_value.T, w_out]

    emb, top, bottom, mixed, normed, rolled = embed(ids, frames, actions, token_table, conv, gain)
    strips = lax.axis_size("space")
    up = [(i, i + 1) for i in range(strips - 1)]
    before = lax.ppermute(bottom, "space", up)
    after = lax.ppermute(top, "space", [(j, i) for i, j in up])
    lo, hi, anchors = window_of(rolled, tm)
    inner = [normed, rolled, lo, hi, anchors, mixed]
    mixed, normed, rolled = edge(emb, before, after, conv, gain)
    outer = [normed, rolled, *window_of(rolled, tm, hi), mixed]
    last = shape[1] - 1
    out = attend(tm_arg, inner, weights, None, shape, lambda r: r + 1)
    return attend(tm_arg, outer, weights, out, shape, lambda r: r * last)


def solution(mesh):
    in_specs = (
        P("tm", "space", None, None),
        P(None, "tm", "space", None),
        P("tm"),
        P(),
        P(),
        P(),
        P(),
        P(),
        P(),
        P(),
        P(),
    )
    out_specs = P("tm", "space", None, None)
    return jax.shard_map(
        on_device, mesh=mesh, in_specs=in_specs, out_specs=out_specs, check_vma=False
    )
```

time: 178 us -> 163 us (0.916); the launches traced: 176 us -> 160 us
  Pallas kernels: 83.3 us -> 64.5 us
  waiting for transfers between devices: 41.2 us -> 53 us
  local copies, waits for them, and re-layouts: 19.3 us -> 10.9 us
    pallas_call x4, Pallas kernels: 83.3 us -> 64.5 us  [the longest x2 44.5 us: attend(): pl.pallas_call(attend_kernel, grid=(positions // (2 * GROUP),), in_specs=...]
    ppermute x4, waiting for transfers between devices: 3.21 us -> 9.47 us  [send(): return lax.ppermute(x, 'tm', [(i, i + by) for i in range(count - by)])]
    another operation x1 -> x0, local copies, waits for them, and re-layouts: 4.17 us -> none  [on_device(): ids = token_ids[0].reshape(-1, 1)]
    unnamed x26 -> x30, local copies, waits for them, and re-layouts: 9.06 us -> 5.67 us
    ppermute x4, waiting for transfers between devices: 32.5 us -> 35.8 us  [window_of(): got = lax.ppermute(anchors, 'tm', pairs)]
  transfers between devices with their start and end apart: 10 -> 10, of which waited for: 6 -> 5; matrix products, arithmetic and copies ran while one was open for 7% -> 7% of each run, Pallas kernels for 22% -> 19%
where the time goes in v1:
time: 163 us; the launch traced here: 160 us
  Pallas kernels  64.5 us (40%)
  waiting for transfers between devices  53 us (33%)
  starting transfers between devices  24.1 us (15%)
  local copies, waits for them, and re-layouts  10.9 us (7%)
  other arithmetic  5.88 us (4%)
    pallas_call x2, Pallas kernels, attend(): pl.pallas_call(attend_kernel, grid=(positions // (2 * GROUP),), in_specs=...  44.5 us
    ppermute x4, waiting for transfers between devices, window_of(): got = lax.ppermute(anchors, 'tm', pairs)  35.8 us
    ppermute x4, starting transfers between devices, send(): return lax.ppermute(x, 'tm', [(i, i + by) for i in range(count - by)])  13.4 us
    pallas_call x1, Pallas kernels, embed(): pl.pallas_call(embed_kernel, grid=(count // 2,), in_specs=[pl.BlockSpec((...  12.2 us
    ppermute x4, waiting for transfers between devices, send(): return lax.ppermute(x, 'tm', [(i, i + by) for i in range(count - by)])  9.47 us
    pallas_call x1, Pallas kernels, edge(): pl.pallas_call(edge_kernel, grid=(count // 2,), in_specs=[frame_spec, str...  7.81 us
    unnamed x30, local copies, waits for them, and re-layouts  5.67 us
    ppermute x4, starting transfers between devices, window_of(): got = lax.ppermute(anchors, 'tm', pairs)  4.81 us
  transfers between devices with their start and end apart: 10, of which 5 were waited for; matrix products, arithmetic and copies ran while one was open for 7% of the time, Pallas kernels for 19%

profile of v1, /device:TPU:13, one launch (start us, length us, event | category | flops | bytes accessed | tf_op | source)
XLA Modules:
  0.0 159.5 jit_solution(5504349553403954728)
XLA Ops:
  0.7 0.9 reshape.14.ids
  2.3 0.8 fusion.actions
  3.1 1.1 copy-done.11
  4.3 12.2 %embed.1 = (bf16[16,4,64,384]{3,2,1,0:T(8,128)(2,1)}, bf16[16,64,384]{2,1,0:T(8,128)(2,1)S(1)}, bf16[16,64,384]{2,1,0:T(8,128)(2,1)S(1)}, f32[16,128,384]{2,1,0:...) custom-call(s32[8,1,512]{2,1,0:T(1,128)S(1)} %reshape.14.ids, ...), custom_call_target="tpu_custom_call" | custom-call | flops 1000 | bytes 1000 | tf_op jit(solution)/shard_map/embed/pallas_call | solution.py:238
  16.6 3.1 %collective-permute-start.2 = (bf16[16,96,384]{2,1,0:T(8,128)(2,1)S(1)}, bf16[16,96,384]{2,1,0:T(8,128)(2,1)S(1)}, u32[]{:S(2)}, u32[]{:S(2)}) collective-permute-start(bf16[16,96,384]{2,1,0:T(8,128)(2,1)S(1)} %slice.13), channel_id=1, source_target_pairs={{0,4},{4,8},{8,12},{12,16},{16,20},{20,24},{24,28},{1,5},{5,9},{9,... | collective-permute-start | bytes 3538952 | tf_op jit(solution)/shard_map/ppermute | solution.py:310
  19.7 4.0 %collective-permute-start = (bf16[16,64,384]{2,1,0:T(8,128)(2,1)S(1)}, bf16[16,64,384]{2,1,0:T(8,128)(2,1)S(1)}, u32[]{:S(2)}, u32[]{:S(2)}) collective-permute-start(bf16[16,64,384]{2,1,0:T(8,128)(2,1)S(1)} %get-tuple-element.16), channel_id=1, source_target_pairs={{0,1},{1,2},{2,3},{4,5},{5,6},{6,7},{8,9},{9,10},{10,11},{12,13},{... | collective-permute-start | bytes 2359304 | tf_op jit(solution)/shard_map/ppermute | solution.py:358
  23.7 1.9 %collective-permute-start.1 = (bf16[16,64,384]{2,1,0:T(8,128)(2,1)S(1)}, bf16[16,64,384]{2,1,0:T(8,128)(2,1)S(1)}, u32[]{:S(2)}, u32[]{:S(2)}) collective-permute-start(bf16[16,64,384]{2,1,0:T(8,128)(2,1)S(1)} %get-tuple-element.17), channel_id=1, source_target_pairs={{1,0},{2,1},{3,2},{5,4},{6,5},{7,6},{9,8},{10,9},{11,10},{13,12},{... | collective-permute-start | bytes 2359304 | tf_op jit(solution)/shard_map/ppermute | solution.py:359
  25.6 0.8 slice.15
  26.5 3.1 %collective-permute-start.7 = (bf16[16,32,384]{2,1,0:T(8,128)(2,1)}, bf16[16,32,384]{2,1,0:T(8,128)(2,1)S(1)}, u32[]{:S(2)}, u32[]{:S(2)}) collective-permute-start(bf16[16,32,384]{2,1,0:T(8,128)(2,1)} %slice.15), channel_id=1, source_target_pairs={{0,4},{4,8},{8,12},{12,16},{16,20},{20,24},{24,28},{1,5},{5,9},{9,... | collective-permute-start | bytes 1179656 | tf_op jit(solution)/shard_map/ppermute | solution.py:310
  29.6 3.0 %collective-permute-done.before = bf16[16,64,384]{2,1,0:T(8,128)(2,1)S(1)} collective-permute-done((bf16[16,64,384]{2,1,0:T(8,128)(2,1)S(1)}, bf16[16,64,384]{2,1,0:T(8,128)(2,1)S(1)}, u32[]{:S(2)}, u32[]{:S(2)}) %collective-permute-start) | collective-permute-done | bytes 786464 | tf_op jit(solution)/shard_map/ppermute | solution.py:358
  32.6 4.7 %collective-permute-done.1.after = bf16[16,64,384]{2,1,0:T(8,128)(2,1)S(1)} collective-permute-done((bf16[16,64,384]{2,1,0:T(8,128)(2,1)S(1)}, bf16[16,64,384]{2,1,0:T(8,128)(2,1)S(1)}, u32[]{:S(2)}, u32[]{:S(2)}) %collective-permute-start.1) | collective-permute-done | bytes 786464 | tf_op jit(solution)/shard_map/ppermute | solution.py:359
  37.3 7.8 %edge.1 = (f32[16,128,384]{2,1,0:T(8,128)}, bf16[16,128,384]{2,1,0:T(8,128)(2,1)S(1)}, bf16[16,128,384]{2,1,0:T(8,128)(2,1)S(1)}) custom-call(bf16[16,4,64,384]{3,2,1,0:T(8,128)(2,1)} %get-tuple-element.15.emb, bf16[16,64,384]{2,1,0:T(8,128)(2,1)S(1)} %collective-permute-done.before, bf16[16,64,384]{2,1,0:T(8,128)(2,1)S(1)} %collective-permute-done.1.after, ...), custom_call_target="tpu_custom_call" | custom-call | flops 1000 | bytes 1000 | tf_op jit(solution)/shard_map/edge/pallas_call | solution.py:262
  45.1 1.1 copy-done.5
  46.3 0.9 slice.12
  47.1 1.0 copy-done.7
  48.2 3.1 %collective-permute-start.3 = (bf16[16,32,384]{2,1,0:T(8,128)(2,1)}, bf16[16,32,384]{2,1,0:T(8,128)(2,1)}, u32[]{:S(2)}, u32[]{:S(2)}) collective-permute-start(bf16[16,32,384]{2,1,0:T(8,128)(2,1)} %slice.12), channel_id=1, source_target_pairs={{0,4},{4,8},{8,12},{12,16},{16,20},{20,24},{24,28},{1,5},{5,9},{9,... | collective-permute-start | bytes 1179656 | tf_op jit(solution)/shard_map/ppermute | solution.py:310
  51.3 2.4 %collective-permute-done.7.lo = bf16[16,32,384]{2,1,0:T(8,128)(2,1)S(1)} collective-permute-done((bf16[16,32,384]{2,1,0:T(8,128)(2,1)}, bf16[16,32,384]{2,1,0:T(8,128)(2,1)S(1)}, u32[]{:S(2)}, u32[]{:S(2)}) %collective-permute-start.7) | collective-permute-done | bytes 393248 | tf_op jit(solution)/shard_map/ppermute | solution.py:310
  55.2 7.0 %collective-permute-done.3.lo = bf16[16,32,384]{2,1,0:T(8,128)(2,1)} collective-permute-done((bf16[16,32,384]{2,1,0:T(8,128)(2,1)}, bf16[16,32,384]{2,1,0:T(8,128)(2,1)}, u32[]{:S(2)}, u32[]{:S(2)}) %collective-permute-start.3) | collective-permute-done | bytes 393248 | tf_op jit(solution)/shard_map/ppermute | solution.py:310
  62.3 1.0 broadcast_select_fusion.1
  63.3 1.4 collective-permute-start.5
  64.8 1.2 slice.14
  65.9 4.0 %collective-permute-start.4 = (bf16[16,96,384]{2,1,0:T(8,128)(2,1)}, bf16[16,96,384]{2,1,0:T(8,128)(2,1)}, u32[]{:S(2)}, u32[]{:S(2)}) collective-permute-start(bf16[16,96,384]{2,1,0:T(8,128)(2,1)} %slice.14), channel_id=1, source_target_pairs={{0,4},{4,8},{8,12},{12,16},{16,20},{20,24},{24,28},{1,5},{5,9},{9,... | collective-permute-start | bytes 3538952 | tf_op jit(solution)/shard_map/ppermute | solution.py:310
  70.0 1.8 %broadcast_select_fusion.2 = bf16[16,32,384]{2,1,0:T(8,128)(2,1)} fusion(bf16[16,32,384]{2,1,0:T(8,128)(2,1)S(1)} %collective-permute-done.8, bf16[16,32,384]{2,1,0:T(8,128)(2,1)} %broadcast_select_fusion, pred[]{:T(512)S(6)} %or.9), kind=kLoop, calls=%fused_computation.2 | loop fusion | flops 196608 | bytes 1179649 | tf_op jit(solution)/shard_map/jit(_where)/select_n | solution.py:326
  71.8 1.4 collective-permute-start.9
  73.3 1.3 collective-permute-start.6
  74.6 1.2 copy.13
  75.8 1.2 copy.14
  77.0 35.8 %collective-permute-done.9 = bf16[16,32,384]{2,1,0:T(8,128)(2,1)} collective-permute-done((bf16[16,32,384]{2,1,0:T(8,128)(2,1)}, bf16[16,32,384]{2,1,0:T(8,128)(2,1)}, u32[]{:S(2)}, u32[]{:S(2)}) %collective-permute-start.9) | collective-permute-done | bytes 393248 | tf_op jit(solution)/shard_map/ppermute | solution.py:324
  112.8 1.0 broadcast_select_fusion.4.anchors
  113.9 22.2 %attend.2.rest_0_ = bf16[16,4,64,384]{3,2,1,0:T(8,128)(2,1)} custom-call(s32[1]{0:T(128)} %bitcast.tm_ref, bf16[16,128,384]{2,1,0:T(8,128)(2,1)S(1)} %copy-done.4, bf16[16,128,384]{2,1,0:T(8,128)(2,1)} %copy-done.1, bf16[16,32,384]{2,1,0:T(8,128)(2,1)S(1)} %collective-permute-done.7.lo, bf16[16,96,384]{2,1,0:T(8,128)(2,1)S(1)} %copy-done.8, ...), custom_call_target="tpu_custom_call" | custom-call | flops 1000 | bytes 1000 | tf_op jit(solution)/shard_map/attend/pallas_call | solution.py:290
  136.2 1.1 broadcast_select_fusion.5.anchors
  137.2 22.3 %attend.3 = bf16[16,4,64,384]{3,2,1,0:T(8,128)(2,1)} custom-call(s32[1]{0:T(128)} %bitcast.tm_ref, bf16[16,128,384]{2,1,0:T(8,128)(2,1)S(1)} %copy-done.6, bf16[16,128,384]{2,1,0:T(8,128)(2,1)} %copy-done.2, bf16[16,32,384]{2,1,0:T(8,128)(2,1)} %collective-permute-done.3.lo, ...), custom_call_target="tpu_custom_call", output_to_operand_aliasing={{}: (11, {})} | custom-call | flops 1000 | bytes 1000 | tf_op jit(solution)/shard_map/attend/pallas_call | solution.py:290
  (36 shorter events, 3.2 us)
Async XLA Ops:
  0.0 2.3 %copy-start = (bf16[8,384]{1,0:T(8,128)(2,1)S(1)}, bf16[8,384]{1,0:T(8,128)(2,1)}, u32[]{:S(2)}) copy-start(bf16[8,384]{1,0:T(8,128)(2,1)} %param.15) | copy-start | bytes 18436
  2.3 14.2 %copy-start.12 = (f32[9,384]{1,0:T(8,128)}, f32[9,384]{1,0:T(8,128)S(1)}, u32[]{:S(2)}) copy-start(f32[9,384]{1,0:T(8,128)S(1)} %reshape.15.conv_ref) | copy-start | bytes 41476
  3.1 1.1 copy-start.11
  16.4 10.0 %copy-start.3 = (bf16[16,128,384]{2,1,0:T(8,128)(2,1)}, bf16[16,128,384]{2,1,0:T(8,128)(2,1)S(1)}, u32[]{:S(2)}) copy-start(bf16[16,128,384]{2,1,0:T(8,128)(2,1)S(1)} %get-tuple-element.23.x_ref) | copy-start | bytes 4718596
  16.4 37.3 %copy-start.1 = (bf16[16,128,384]{2,1,0:T(8,128)(2,1)}, bf16[16,128,384]{2,1,0:T(8,128)(2,1)S(1)}, u32[]{:S(2)}) copy-start(bf16[16,128,384]{2,1,0:T(8,128)(2,1)S(1)} %get-tuple-element.20.own) | copy-start | bytes 4718596
  16.4 20.9 %copy-start.13 = (f32[9,384]{1,0:T(8,128)S(1)}, f32[9,384]{1,0:T(8,128)}, u32[]{:S(2)}) copy-start(f32[9,384]{1,0:T(8,128)} %copy-done.12) | copy-start | bytes 41476
  16.6 30.6 %collective-permute-start.2 = (bf16[16,96,384]{2,1,0:T(8,128)(2,1)S(1)}, bf16[16,96,384]{2,1,0:T(8,128)(2,1)S(1)}, u32[]{:S(2)}, u32[]{:S(2)}) collective-permute-start(bf16[16,96,384]{2,1,0:T(8,128)(2,1)S(1)} %slice.13), channel_id=1, source_target_pairs={{0,4},{4,8},{8,12},{12,16},{16,20},{20,24},{24,28},{1,5},{5,9},{9,... | collective-permute-start | bytes 3538952 | tf_op jit(solution)/shard_map/ppermute | solution.py:310
  19.7 12.9 %collective-permute-start = (bf16[16,64,384]{2,1,0:T(8,128)(2,1)S(1)}, bf16[16,64,384]{2,1,0:T(8,128)(2,1)S(1)}, u32[]{:S(2)}, u32[]{:S(2)}) collective-permute-start(bf16[16,64,384]{2,1,0:T(8,128)(2,1)S(1)} %get-tuple-element.16), channel_id=1, source_target_pairs={{0,1},{1,2},{2,3},{4,5},{5,6},{6,7},{8,9},{9,10},{10,11},{12,13},{... | collective-permute-start | bytes 2359304 | tf_op jit(solution)/shard_map/ppermute | solution.py:358
  23.7 13.6 %collective-permute-start.1 = (bf16[16,64,384]{2,1,0:T(8,128)(2,1)S(1)}, bf16[16,64,384]{2,1,0:T(8,128)(2,1)S(1)}, u32[]{:S(2)}, u32[]{:S(2)}) collective-permute-start(bf16[16,64,384]{2,1,0:T(8,128)(2,1)S(1)} %get-tuple-element.17), channel_id=1, source_target_pairs={{1,0},{2,1},{3,2},{5,4},{6,5},{7,6},{9,8},{10,9},{11,10},{13,12},{... | collective-permute-start | bytes 2359304 | tf_op jit(solution)/shard_map/ppermute | solution.py:359
  26.5 27.3 %collective-permute-start.7 = (bf16[16,32,384]{2,1,0:T(8,128)(2,1)}, bf16[16,32,384]{2,1,0:T(8,128)(2,1)S(1)}, u32[]{:S(2)}, u32[]{:S(2)}) collective-permute-start(bf16[16,32,384]{2,1,0:T(8,128)(2,1)} %slice.15), channel_id=1, source_target_pairs={{0,4},{4,8},{8,12},{12,16},{16,20},{20,24},{24,28},{1,5},{5,9},{9,... | collective-permute-start | bytes 1179656 | tf_op jit(solution)/shard_map/ppermute | solution.py:310
  45.1 1.1 copy-start.5
  46.3 18.5 %copy-start.2 = (bf16[16,128,384]{2,1,0:T(8,128)(2,1)}, bf16[16,128,384]{2,1,0:T(8,128)(2,1)S(1)}, u32[]{:S(2)}) copy-start(bf16[16,128,384]{2,1,0:T(8,128)(2,1)S(1)} %get-tuple-element.19.own) | copy-start | bytes 4718596
  47.1 1.0 copy-start.7
  48.2 14.1 %collective-permute-start.3 = (bf16[16,32,384]{2,1,0:T(8,128)(2,1)}, bf16[16,32,384]{2,1,0:T(8,128)(2,1)}, u32[]{:S(2)}, u32[]{:S(2)}) collective-permute-start(bf16[16,32,384]{2,1,0:T(8,128)(2,1)} %slice.12), channel_id=1, source_target_pairs={{0,4},{4,8},{8,12},{12,16},{16,20},{20,24},{24,28},{1,5},{5,9},{9,... | collective-permute-start | bytes 1179656 | tf_op jit(solution)/shard_map/ppermute | solution.py:310
  54.6 15.4 %collective-permute-start.8 = (bf16[16,32,384]{2,1,0:T(8,128)(2,1)}, bf16[16,32,384]{2,1,0:T(8,128)(2,1)S(1)}, u32[]{:S(2)}, u32[]{:S(2)}) collective-permute-start(bf16[16,32,384]{2,1,0:T(8,128)(2,1)} %broadcast_select_fusion), channel_id=1, source_target_pairs={{0,16},{4,20},{1,17},{5,21},{2,18},{6,22},{3,19},{7,23}} | collective-permute-start | bytes 1179656 | tf_op jit(solution)/shard_map/ppermute | solution.py:324
  63.3 9.9 %collective-permute-start.5 = (bf16[16,32,384]{2,1,0:T(8,128)(2,1)S(1)}, bf16[16,32,384]{2,1,0:T(8,128)(2,1)}, u32[]{:S(2)}, u32[]{:S(2)}) collective-permute-start(bf16[16,32,384]{2,1,0:T(8,128)(2,1)S(1)} %broadcast_select_fusion.1), channel_id=1, source_target_pairs={{0,16},{4,20},{1,17},{5,21},{2,18},{6,22},{3,19},{7,23}} | collective-permute-start | bytes 1179656 | tf_op jit(solution)/shard_map/ppermute | solution.py:324
  65.9 71.3 %collective-permute-start.4 = (bf16[16,96,384]{2,1,0:T(8,128)(2,1)}, bf16[16,96,384]{2,1,0:T(8,128)(2,1)}, u32[]{:S(2)}, u32[]{:S(2)}) collective-permute-start(bf16[16,96,384]{2,1,0:T(8,128)(2,1)} %slice.14), channel_id=1, source_target_pairs={{0,4},{4,8},{8,12},{12,16},{16,20},{20,24},{24,28},{1,5},{5,9},{9,... | collective-permute-start | bytes 3538952 | tf_op jit(solution)/shard_map/ppermute | solution.py:310
  71.8 42.1 %copy-start.4 = (bf16[16,128,384]{2,1,0:T(8,128)(2,1)S(1)}, bf16[16,128,384]{2,1,0:T(8,128)(2,1)}, u32[]{:S(2)}) copy-start(bf16[16,128,384]{2,1,0:T(8,128)(2,1)} %copy-done.3) | copy-start | bytes 4718596
  71.8 42.1 %copy-start.9 = (bf16[384,384]{1,0:T(8,128)(2,1)S(1)}, bf16[384,384]{1,0:T(8,128)(2,1)}, u32[]{:S(2)}) copy-start(bf16[384,384]{1,0:T(8,128)(2,1)} %wk.3) | copy-start | bytes 884740
  71.8 42.1 %copy-start.10 = (bf16[384,384]{1,0:T(8,128)(2,1)S(1)}, bf16[384,384]{1,0:T(8,128)(2,1)}, u32[]{:S(2)}) copy-start(bf16[384,384]{1,0:T(8,128)(2,1)} %w_out.3) | copy-start | bytes 884740
  71.8 41.0 %collective-permute-start.9 = (bf16[16,32,384]{2,1,0:T(8,128)(2,1)}, bf16[16,32,384]{2,1,0:T(8,128)(2,1)}, u32[]{:S(2)}, u32[]{:S(2)}) collective-permute-start(bf16[16,32,384]{2,1,0:T(8,128)(2,1)} %broadcast_select_fusion.2), channel_id=1, source_target_pairs={{0,8},{4,12},{16,24},{20,28},{1,9},{5,13},{17,25},{21,29},{2,10},{... | collective-permute-start | bytes 1179656 | tf_op jit(solution)/shard_map/ppermute | solution.py:324
  73.3 62.8 %collective-permute-start.6 = (bf16[16,32,384]{2,1,0:T(8,128)(2,1)S(1)}, bf16[16,32,384]{2,1,0:T(8,128)(2,1)}, u32[]{:S(2)}, u32[]{:S(2)}) collective-permute-start(bf16[16,32,384]{2,1,0:T(8,128)(2,1)S(1)} %broadcast_select_fusion.3), channel_id=1, source_target_pairs={{0,8},{4,12},{16,24},{20,28},{1,9},{5,13},{17,25},{21,29},{2,10},{... | collective-permute-start | bytes 1179656 | tf_op jit(solution)/shard_map/ppermute | solution.py:324
  77.0 36.9 %copy-start.8 = (bf16[16,96,384]{2,1,0:T(8,128)(2,1)S(1)}, bf16[16,96,384]{2,1,0:T(8,128)(2,1)}, u32[]{:S(2)}) copy-start(bf16[16,96,384]{2,1,0:T(8,128)(2,1)} %copy-done.7) | copy-start | bytes 3538948
  113.9 23.3 %copy-start.6 = (bf16[16,128,384]{2,1,0:T(8,128)(2,1)S(1)}, bf16[16,128,384]{2,1,0:T(8,128)(2,1)}, u32[]{:S(2)}) copy-start(bf16[16,128,384]{2,1,0:T(8,128)(2,1)} %copy-done.5) | copy-start | bytes 4718596

commit v2 on v1

--- a/solution.py
+++ b/solution.py
@@ -1,3 +1,5 @@
+import functools
+
 import jax
 import jax.numpy as jnp
 from jax import lax
@@ -10,6 +12,7 @@
 WINDOW = 16
 ANCHORS = 4
 GROUP = 8
+STEP = 4
 F32 = jnp.float32
 BF16 = jnp.bfloat16
 NT = (((1,), (1,)), ((), ()))
@@ -46,8 +49,8 @@
     return jnp.concatenate([first, second], axis=1)
 
 
-def put_rows(results, mixed, normed, rolled):
-    frame = pl.program_id(0) * 2
+def put_rows(first, results, mixed, normed, rolled):
+    frame = pl.program_id(0) * 2 + first
     turned = []
     for k in range(2):
         n = results[k][1].reshape(-1, GROUP, results[k][1].shape[-1])
@@ -58,9 +61,9 @@
 
 
 def embed_kernel(
-    ids, frames, actions, table, conv_ref, gain_ref, emb, top, bottom, mixed, normed, rolled
+    first, ids, frames, actions, table, conv_ref, gain_ref, emb, top, bottom, mixed, normed, rolled
 ):
-    step = pl.program_id(0)
+    frame = pl.program_id(0) * 2 + first
     row_count, cols, width = frames.shape[1:]
     vocab = table.shape[0]
     count = 2 * row_count * cols
@@ -75,7 +78,7 @@
     gain = gain_ref[...]
     results = []
     for k in range(2):
-        action = actions[pl.ds(step * 2 + k, 1), :]
+        action = actions[pl.ds(frame + k, 1), :]
         rows = []
         for r in range(row_count):
             at = (k * row_count + r) * cols
@@ -90,10 +93,10 @@
             for r in range(1, row_count - 1)
         ]
         results.append([jnp.concatenate(part, axis=0) for part in zip(*done)])
-    put_rows(results, mixed, normed, rolled)
-
-
-def edge_kernel(emb, before, after, conv_ref, gain_ref, mixed, normed, rolled):
+    put_rows(first, results, mixed, normed, rolled)
+
+
+def edge_kernel(first, emb, before, after, conv_ref, gain_ref, mixed, normed, rolled):
     row_count = emb.shape[1]
     conv = conv_ref[...]
     gain = gain_ref[...]
@@ -104,15 +107,15 @@
             conv_norm(emb[k, row_count - 2], emb[k, row_count - 1], after[k], conv, gain),
         ]
         results.append([jnp.concatenate(part, axis=0) for part in zip(*done)])
-    put_rows(results, mixed, normed, rolled)
+    put_rows(first, results, mixed, normed, rolled)
 
 
 def attend_kernel(
-    tm_ref, x_ref, own, lo, hi, anchors, mixed, wq_t, wk, wv_t, w_out, *rest
+    tm_ref, x_lo, x_hi, own_lo, own_hi, lo, hi, anchors, m_lo, m_hi, wq_t, wk, wv_t, w_out, *rest
 ):
     out, mask = rest[-2:]
     tm = tm_ref[0]
-    width = x_ref.shape[-1]
+    width = x_lo.shape[-1]
     queries = WINDOW * GROUP
     lanes = 2 * queries
     slabs = 2 * WINDOW + ANCHORS
@@ -140,21 +143,28 @@
     open_window = [(c < WINDOW) | (tm > 0) for c in places]
     open_anchor = (met < ANCHORS) & (met < tm * WINDOW + t - (WINDOW - 1))
 
-    x = x_ref[...].reshape(-1, width)
+    anchor_rows = ANCHORS * GROUP
+    window_rows = 2 * queries
+    x = jnp.concatenate([ref[i] for i in range(STEP) for ref in (x_lo, x_hi)], axis=0)
+    window = [ref[i] for i in range(STEP) for ref in (own_lo, own_hi, lo, hi)]
+    window = jnp.concatenate(window, axis=0)
+    first = anchors[...].reshape(STEP * anchor_rows, width)
     q_t = lax.dot_general(wq_t[...], x, NT, preferred_element_type=F32).astype(BF16)
     q_t = (q_t * 0.125).astype(BF16)
-    anchor_rows = ANCHORS * GROUP
-    va_t = lax.dot_general(
-        wv_t[...], anchors[...].reshape(2 * anchor_rows, width), NT, preferred_element_type=F32
+    k_all = jnp.dot(
+        jnp.concatenate([window, first], axis=0), wk[...], preferred_element_type=F32
     ).astype(BF16)
+    v_all = lax.dot_general(wv_t[...], window, NT, preferred_element_type=F32).astype(BF16)
+    va_t = lax.dot_general(wv_t[...], first, NT, preferred_element_type=F32).astype(BF16)
     blank = jnp.zeros((64, queries), BF16)
     no_rows = jnp.zeros((anchor_rows, lanes), BF16)
-    results = []
-    for i in range(2):
-        window = jnp.concatenate([own[i], lo[i], hi[i]], axis=0)
-        keys = jnp.concatenate([window, anchors[i]], axis=0)
-        k = jnp.dot(keys, wk[...], preferred_element_type=F32).astype(BF16)
-        v_t = lax.dot_general(wv_t[...], window, NT, preferred_element_type=F32).astype(BF16)
+    columns = []
+    for i in range(STEP):
+        at = STEP * window_rows + i * anchor_rows
+        k = jnp.concatenate(
+            [k_all[i * window_rows : (i + 1) * window_rows], k_all[at : at + anchor_rows]], axis=0
+        )
+        v_t = v_all[:, i * window_rows : (i + 1) * window_rows]
         parts = []
         for pair in range(width // 128):
             at = pair * 128
@@ -194,7 +204,7 @@
                 spread.append(p[b] * mask[j * 16 : (j + 1) * 16, :])
             p_window = jnp.concatenate(spread[:WINDOW], axis=0)
             p_first = jnp.concatenate(spread[WINDOW:], axis=0)
-            p_first = [p_first, no_rows] if i == 0 else [no_rows, p_first]
+            p_first = [p_first if n == i else no_rows for n in range(STEP)]
             o = jnp.dot(v_t[at : at + 128], p_window, preferred_element_type=F32)
             o += jnp.dot(
                 va_t[at : at + 128],
@@ -202,9 +212,14 @@
                 preferred_element_type=F32,
             )
             parts += [o[:64, :queries], o[64:, queries:]]
-        attended = jnp.concatenate(parts, axis=0).astype(BF16)
-        result = lax.dot_general(attended, w_out[...], TN, preferred_element_type=F32)
-        results.append((result + mixed[i]).reshape(WINDOW, GROUP, width))
+        columns.append(jnp.concatenate(parts, axis=0).astype(BF16))
+    attended = jnp.concatenate(columns, axis=1)
+    result = lax.dot_general(attended, w_out[...], TN, preferred_element_type=F32)
+    results = []
+    for i in range(STEP):
+        mixed = jnp.concatenate([m_lo[i], m_hi[i]], axis=0)
+        total = result[i * queries : (i + 1) * queries] + mixed
+        results.append(total.reshape(WINDOW, GROUP, width))
     out[...] = jnp.concatenate(results, axis=1).astype(BF16).reshape(out.shape)
 
 
@@ -229,38 +244,44 @@
     return [spec] * 3, shapes
 
 
-def embed(ids, frames, actions, table, conv, gain):
-    count, row_count, cols, width = frames.shape
+def embed(first, count, ids, frames, actions, table, conv, gain):
+    _, row_count, cols, width = frames.shape
     strip = jax.ShapeDtypeStruct((count, cols, width), BF16)
     strip_spec = pl.BlockSpec((2, cols, width), lambda f: (f, 0, 0))
-    frame_spec = pl.BlockSpec((2, row_count, cols, width), lambda f: (f, 0, 0, 0))
+    block = (2, row_count, cols, width)
+    skip = first // 2
     specs, shapes = row_outputs(count, (row_count - 2) * cols, width)
     return pl.pallas_call(
-        embed_kernel,
+        functools.partial(embed_kernel, first),
         grid=(count // 2,),
         in_specs=[
-            pl.BlockSpec((1, 1, 2 * row_count * cols), lambda f: (f, 0, 0)),
-            frame_spec,
+            pl.BlockSpec((1, 1, 2 * row_count * cols), lambda f: (f + skip, 0, 0)),
+            pl.BlockSpec(block, lambda f: (f + skip, 0, 0, 0)),
             whole(actions),
             whole(table),
             whole(conv),
             whole(gain),
         ],
-        out_specs=[frame_spec, strip_spec, strip_spec] + specs,
-        out_shape=[jax.ShapeDtypeStruct(frames.shape, BF16), strip, strip] + shapes,
+        out_specs=[pl.BlockSpec(block, lambda f: (f, 0, 0, 0)), strip_spec, strip_spec] + specs,
+        out_shape=[
+            jax.ShapeDtypeStruct((count, row_count, cols, width), BF16),
+            strip,
+            strip,
+        ]
+        + shapes,
         compiler_params=params(),
         cost_estimate=small(),
         name="embed",
     )(ids, frames, actions, table, conv, gain)
 
 
-def edge(emb, before, after, conv, gain):
+def edge(first, emb, before, after, conv, gain):
     count, row_count, cols, width = emb.shape
     strip_spec = pl.BlockSpec((2, cols, width), lambda f: (f, 0, 0))
     frame_spec = pl.BlockSpec((2, row_count, cols, width), lambda f: (f, 0, 0, 0))
     specs, shapes = row_outputs(count, 2 * cols, width)
     return pl.pallas_call(
-        edge_kernel,
+        functools.partial(edge_kernel, first),
         grid=(count // 2,),
         in_specs=[frame_spec, strip_spec, strip_spec, whole(conv), whole(gain)],
         out_specs=specs,
@@ -271,17 +292,16 @@
     )(emb, before, after, conv, gain)
 
 
-def attend(tm, blocks, weights, out, shape, row_of):
+def attend(tm, blocks, weights, out, shape, positions, row_of):
     count, _, cols, width = shape
-    positions = blocks[0].shape[0] * GROUP
-    per_row = cols // (2 * GROUP)
-
-    def block(a):
-        return pl.BlockSpec((2,) + a.shape[1:], lambda g: (g, 0, 0))
-
-    args = [tm, *blocks, *weights]
+    per_row = cols // (STEP * GROUP)
+
+    def block(a, start):
+        return pl.BlockSpec((STEP,) + a.shape[1:], lambda g: (g + start // STEP, 0, 0))
+
+    args = [tm, *[a for a, _ in blocks], *weights]
     specs = [pl.BlockSpec(memory_space=pltpu.SMEM)]
-    specs += [block(a) for a in blocks] + [whole(w) for w in weights]
+    specs += [block(a, start) for a, start in blocks] + [whole(w) for w in weights]
     aliases = {}
     if out is not None:
         aliases = {len(args): 0}
@@ -289,10 +309,11 @@
         specs.append(pl.BlockSpec(memory_space=pl.ANY))
     return pl.pallas_call(
         attend_kernel,
-        grid=(positions // (2 * GROUP),),
+        grid=(positions // (STEP * GROUP),),
         in_specs=specs,
         out_specs=pl.BlockSpec(
-            (count, 1, 2 * GROUP, width), lambda g: (0, row_of(g // per_row), g % per_row, 0)
+            (count, 1, STEP * GROUP, width),
+            lambda g: (0, row_of(g // per_row), g % per_row, 0),
         ),
         out_shape=jax.ShapeDtypeStruct(shape, BF16),
         scratch_shapes=[
@@ -310,13 +331,8 @@
     return lax.ppermute(x, "tm", [(i, i + by) for i in range(count - by)])
 
 
-def window_of(normed, tm, after=None):
+def anchors_of(first, lo, tm):
     count = lax.axis_size("tm")
-    first = normed[:, : ANCHORS * GROUP]
-    if after is not None:
-        first, after = lax.optimization_barrier((first, after))
-    lo = send(first, 1)
-    hi = send(normed[:, ANCHORS * GROUP :], 1)
     anchors = jnp.where(tm == 0, first, lo)
     by = count // 2
     while by >= 2:
@@ -325,7 +341,13 @@
         place = tm % (2 * by)
         anchors = jnp.where((place == by) | (place == by + 1), got, anchors)
         by //= 2
-    return lo, hi, anchors
+    return anchors
+
+
+def halo(top, bottom):
+    strips = lax.axis_size("space")
+    up = [(i, i + 1) for i in range(strips - 1)]
+    return lax.ppermute(bottom, "space", up), lax.ppermute(top, "space", [(j, i) for i, j in up])
 
 
 def on_device(
@@ -352,18 +374,56 @@
     gain = norm_gain.reshape(1, width).astype(F32)
     weights = [w_query.T, w_key, w_value.T, w_out]
 
-    emb, top, bottom, mixed, normed, rolled = embed(ids, frames, actions, token_table, conv, gain)
-    strips = lax.axis_size("space")
-    up = [(i, i + 1) for i in range(strips - 1)]
-    before = lax.ppermute(bottom, "space", up)
-    after = lax.ppermute(top, "space", [(j, i) for i, j in up])
-    lo, hi, anchors = window_of(rolled, tm)
-    inner = [normed, rolled, lo, hi, anchors, mixed]
-    mixed, normed, rolled = edge(emb, before, after, conv, gain)
-    outer = [normed, rolled, *window_of(rolled, tm, hi), mixed]
-    last = shape[1] - 1
-    out = attend(tm_arg, inner, weights, None, shape, lambda r: r + 1)
-    return attend(tm_arg, outer, weights, out, shape, lambda r: r * last)
+    cols = shape[2]
+    inner = (shape[1] - 2) * cols // GROUP
+    row = cols // GROUP
+    shared = (ids, frames, actions, token_table, conv, gain)
+
+    emb, top, bottom, mixed_a, normed_a, rolled_a = embed(0, ANCHORS, *shared)
+    mixed_b, normed_b, rolled_b = edge(0, emb, *halo(top, bottom), conv, gain)
+    first = jnp.concatenate([rolled_a, rolled_b], axis=0)
+    lo = send(first, 1)
+    emb, top, bottom, mixed_c, normed_c, rolled_c = embed(ANCHORS, shape[0] - ANCHORS, *shared)
+    lo, _ = lax.optimization_barrier((lo, rolled_c))
+    anchors = anchors_of(first, lo, tm)
+    hi = send(rolled_c, 1)
+    mixed_d, normed_d, rolled_d = edge(ANCHORS, emb, *halo(top, bottom), conv, gain)
+
+    def blocks(x_lo, x_hi, own_hi, hi, m_lo, m_hi, start, at, hi_at):
+        return [
+            (x_lo, at),
+            (x_hi, at),
+            (first, start + at),
+            (own_hi, at),
+            (lo, start + at),
+            (hi, hi_at),
+            (anchors, start + at),
+            (m_lo, at),
+            (m_hi, at),
+        ]
+
+    out = attend(
+        tm_arg,
+        blocks(normed_a, normed_c, rolled_c, hi, mixed_a, mixed_c, 0, 0, 0),
+        weights,
+        None,
+        shape,
+        inner * GROUP,
+        lambda r: r + 1,
+    )
+    to_send, _ = lax.optimization_barrier((rolled_d, hi))
+    later = [send(to_send[r * row : (r + 1) * row], 1) for r in range(2)]
+    for r in range(2):
+        out = attend(
+            tm_arg,
+            blocks(normed_b, normed_d, rolled_d, later[r], mixed_b, mixed_d, inner, r * row, 0),
+            weights,
+            out,
+            shape,
+            cols,
+            lambda _, r=r: r * (shape[1] - 1),
+        )
+    return out
 
 
 def solution(mesh):

time: 163 us -> 158 us (0.969); the launches traced: 160 us -> 157 us
  waiting for transfers between devices: 53 us -> 42 us
  local copies, waits for them, and re-layouts: 10.9 us -> 14.9 us
  Pallas kernels: 64.5 us -> 68.2 us
  starting transfers between devices: 24.1 us -> 26.6 us
    ppermute x6, waiting for transfers between devices: 43.5 us -> 21.5 us  [the longest x2 10.6 us: anchors_of(): got = lax.ppermute(anchors, 'tm', pairs)]
    ppermute x4, waiting for transfers between devices: 9.47 us -> 20.5 us  [send(): return lax.ppermute(x, 'tm', [(i, i + by) for i in range(count - by)])]
    unnamed x30 -> x45, local copies, waits for them, and re-layouts: 5.67 us -> 11.5 us
    pallas_call x4 -> x7, Pallas kernels: 64.5 us -> 68.2 us  [the longest x3 48.8 us: attend(): pl.pallas_call(attend_kernel, grid=(positions // (STEP * GROUP),), in_spe...]
    ppermute x6, starting transfers between devices: 10.7 us -> 12.9 us  [the longest x2 5.84 us: halo(): lax.ppermute(bottom, 'space', up)]
    slice x4 -> x1, local copies, waits for them, and re-layouts: 2.99 us -> 1.14 us  [on_device(): later = [send(to_send[r * row:(r + 1) * row], 1) for r in range(2)]]
    select_n x6 -> x3, other arithmetic: 5.88 us -> 4.33 us  [the longest x2 3.36 us: anchors_of(): anchors = jnp.where((place == by) | (place == by + 1), got, anchors)]
  transfers between devices with their start and end apart: 10 -> 10, of which waited for: 5 -> 7; matrix products, arithmetic and copies ran while one was open for 7% -> 4% of each run, Pallas kernels for 19% -> 32%
where the time goes in v2:
time: 158 us; the launch traced here: 157 us
  Pallas kernels  68.2 us (43%)
  waiting for transfers between devices  42 us (27%)
  starting transfers between devices  26.6 us (17%)
  local copies, waits for them, and re-layouts  14.9 us (9%)
  other arithmetic  4.33 us (3%)
    pallas_call x3, Pallas kernels, attend(): pl.pallas_call(attend_kernel, grid=(positions // (STEP * GROUP),), in_spe...  48.8 us
    ppermute x4, waiting for transfers between devices, send(): return lax.ppermute(x, 'tm', [(i, i + by) for i in range(count - by)])  20.5 us
    ppermute x4, starting transfers between devices, send(): return lax.ppermute(x, 'tm', [(i, i + by) for i in range(count - by)])  13.7 us
    pallas_call x2, Pallas kernels, embed(): pl.pallas_call(functools.partial(embed_kernel, first), grid=(count // 2,)...  13.3 us
    unnamed x45, local copies, waits for them, and re-layouts  11.5 us
    ppermute x2, waiting for transfers between devices, anchors_of(): got = lax.ppermute(anchors, 'tm', pairs)  10.6 us
    ppermute x2, waiting for transfers between devices, halo(): lax.ppermute(top, 'space', [(j, i) for i, j in up])  8.88 us
    pallas_call x2, Pallas kernels, edge(): pl.pallas_call(functools.partial(edge_kernel, first), grid=(count // 2,),...  6.2 us
  transfers between devices with their start and end apart: 10, of which 7 were waited for; matrix products, arithmetic and copies ran while one was open for 4% of the time, Pallas kernels for 32%

profile of v2, /device:TPU:13, one launch (start us, length us, event | category | flops | bytes accessed | tf_op | source)
XLA Modules:
  0.0 157.3 jit_solution(16005806761843938985)
XLA Ops:
  3.1 1.1 copy-done.6
  4.3 3.6 %embed.2 = (bf16[4,4,64,384]{3,2,1,0:T(8,128)(2,1)S(1)}, bf16[4,64,384]{2,1,0:T(8,128)(2,1)S(1)}, bf16[4,64,384]{2,1,0:T(8,128)(2,1)S(1)}, f32[16,32,384]{2,1,0:...) custom-call(s32[8,1,512]{2,1,0:T(1,128)S(1)} %reshape.14.ids, ...), custom_call_target="tpu_custom_call" | custom-call | flops 1000 | bytes 1000 | tf_op jit(solution)/shard_map/embed/pallas_call | solution.py:254
  8.6 3.8 %collective-permute-start = (bf16[4,64,384]{2,1,0:T(8,128)(2,1)S(1)}, bf16[4,64,384]{2,1,0:T(8,128)(2,1)S(1)}, u32[]{:S(2)}, u32[]{:S(2)}) collective-permute-start(bf16[4,64,384]{2,1,0:T(8,128)(2,1)S(1)} %get-tuple-element.26), channel_id=1, source_target_pairs={{0,1},{1,2},{2,3},{4,5},{5,6},{6,7},{8,9},{9,10},{10,11},{12,13},{... | collective-permute-start | bytes 589832 | tf_op jit(solution)/shard_map/ppermute | solution.py:350
  12.4 1.9 %collective-permute-start.1 = (bf16[4,64,384]{2,1,0:T(8,128)(2,1)S(1)}, bf16[4,64,384]{2,1,0:T(8,128)(2,1)S(1)}, u32[]{:S(2)}, u32[]{:S(2)}) collective-permute-start(bf16[4,64,384]{2,1,0:T(8,128)(2,1)S(1)} %get-tuple-element.27), channel_id=1, source_target_pairs={{1,0},{2,1},{3,2},{5,4},{6,5},{7,6},{9,8},{10,9},{11,10},{13,12},{... | collective-permute-start | bytes 589832 | tf_op jit(solution)/shard_map/ppermute | solution.py:350
  15.0 4.4 %collective-permute-done.1.after = bf16[4,64,384]{2,1,0:T(8,128)(2,1)S(1)} collective-permute-done((bf16[4,64,384]{2,1,0:T(8,128)(2,1)S(1)}, bf16[4,64,384]{2,1,0:T(8,128)(2,1)S(1)}, u32[]{:S(2)}, u32[]{:S(2)}) %collective-permute-start.1) | collective-permute-done | bytes 196640 | tf_op jit(solution)/shard_map/ppermute | solution.py:350
  19.4 1.1 edge.2
  22.1 3.1 %collective-permute-start.4 = (bf16[32,32,384]{2,1,0:T(8,128)(2,1)S(1)}, bf16[32,32,384]{2,1,0:T(8,128)(2,1)S(1)}, u32[]{:S(2)}, u32[]{:S(2)}) collective-permute-start(bf16[32,32,384]{2,1,0:T(8,128)(2,1)S(1)} %constant_dynamic-update-slice_fusion.own_lo), channel_id=1, source_target_pairs={{0,4},{4,8},{8,12},{12,16},{16,20},{20,24},{24,28},{1,5},{5,9},{9,... | collective-permute-start | bytes 2359304 | tf_op jit(solution)/shard_map/ppermute | solution.py:331
  25.3 9.6 %embed.3 = (bf16[12,4,64,384]{3,2,1,0:T(8,128)(2,1)}, bf16[12,64,384]{2,1,0:T(8,128)(2,1)S(1)}, bf16[12,64,384]{2,1,0:T(8,128)(2,1)}, f32[16,96,384]{2,1,0:T(8,1...) custom-call(s32[8,1,512]{2,1,0:T(1,128)S(1)} %reshape.14.ids, bf16[16,4,64,384]{3,2,1,0:T(8,128)(2,1)} %frames.3, ...), custom_call_target="tpu_custom_call" | custom-call | flops 1000 | bytes 1000 | tf_op jit(solution)/shard_map/embed/pallas_call | solution.py:254
  35.9 4.2 %collective-permute-done.4.lo = bf16[32,32,384]{2,1,0:T(8,128)(2,1)S(1)} collective-permute-done((bf16[32,32,384]{2,1,0:T(8,128)(2,1)S(1)}, bf16[32,32,384]{2,1,0:T(8,128)(2,1)S(1)}, u32[]{:S(2)}, u32[]{:S(2)}) %collective-permute-start.4) | collective-permute-done | bytes 786464 | tf_op jit(solution)/shard_map/ppermute | solution.py:331
  41.1 1.5 collective-permute-start.7
  42.6 3.8 %collective-permute-start.5 = (bf16[16,96,384]{2,1,0:T(8,128)(2,1)}, bf16[16,96,384]{2,1,0:T(8,128)(2,1)}, u32[]{:S(2)}, u32[]{:S(2)}) collective-permute-start(bf16[16,96,384]{2,1,0:T(8,128)(2,1)} %get-tuple-element.36.own_hi), channel_id=1, source_target_pairs={{0,4},{4,8},{8,12},{12,16},{16,20},{20,24},{24,28},{1,5},{5,9},{9,... | collective-permute-start | bytes 3538952 | tf_op jit(solution)/shard_map/ppermute | solution.py:331
  46.4 2.0 %collective-permute-start.2 = (bf16[12,64,384]{2,1,0:T(8,128)(2,1)}, bf16[12,64,384]{2,1,0:T(8,128)(2,1)S(1)}, u32[]{:S(2)}, u32[]{:S(2)}) collective-permute-start(bf16[12,64,384]{2,1,0:T(8,128)(2,1)} %get-tuple-element.30), channel_id=1, source_target_pairs={{0,1},{1,2},{2,3},{4,5},{5,6},{6,7},{8,9},{9,10},{10,11},{12,13},{... | collective-permute-start | bytes 1769480 | tf_op jit(solution)/shard_map/ppermute | solution.py:350
  48.5 2.3 %collective-permute-start.3 = (bf16[12,64,384]{2,1,0:T(8,128)(2,1)S(1)}, bf16[12,64,384]{2,1,0:T(8,128)(2,1)S(1)}, u32[]{:S(2)}, u32[]{:S(2)}) collective-permute-start(bf16[12,64,384]{2,1,0:T(8,128)(2,1)S(1)} %get-tuple-element.31), channel_id=1, source_target_pairs={{1,0},{2,1},{3,2},{5,4},{6,5},{7,6},{9,8},{10,9},{11,10},{13,12},{... | collective-permute-start | bytes 1769480 | tf_op jit(solution)/shard_map/ppermute | solution.py:350
  50.8 2.1 %broadcast_select_fusion.1 = bf16[32,32,384]{2,1,0:T(8,128)(2,1)} fusion(bf16[32,32,384]{2,1,0:T(8,128)(2,1)} %collective-permute-done.7, bf16[32,32,384]{2,1,0:T(8,128)(2,1)} %broadcast_select_fusion, pred[]{:T(512)S(6)} %or.7), kind=kLoop, calls=%fused_computation.1 | loop fusion | flops 393216 | bytes 2359297 | tf_op jit(solution)/shard_map/jit(_where)/select_n | solution.py:342
  52.9 1.3 collective-permute-start.8
  54.2 1.4 collective-permute-done.2.before
  55.6 4.5 %collective-permute-done.3.after = bf16[12,64,384]{2,1,0:T(8,128)(2,1)S(1)} collective-permute-done((bf16[12,64,384]{2,1,0:T(8,128)(2,1)S(1)}, bf16[12,64,384]{2,1,0:T(8,128)(2,1)S(1)}, u32[]{:S(2)}, u32[]{:S(2)}) %collective-permute-start.3) | collective-permute-done | bytes 589856 | tf_op jit(solution)/shard_map/ppermute | solution.py:350
  60.9 1.1 copy-done.17
  61.9 5.1 %edge.3 = (f32[16,96,384]{2,1,0:T(8,128)S(1)}, bf16[16,96,384]{2,1,0:T(8,128)(2,1)S(1)}, bf16[16,96,384]{2,1,0:T(8,128)(2,1)S(1)}) custom-call(bf16[12,4,64,384]{3,2,1,0:T(8,128)(2,1)} %get-tuple-element.29.emb, bf16[12,64,384]{2,1,0:T(8,128)(2,1)S(1)} %collective-permute-done.2.before, bf16[12,64,384]{2,1,0:T(8,128)(2,1)S(1)} %copy-done.17, ...), custom_call_target="tpu_custom_call" | custom-call | flops 1000 | bytes 1000 | tf_op jit(solution)/shard_map/edge/pallas_call | solution.py:283
  67.1 1.4 copy-done.2
  68.5 1.1 copy-done.3
  69.6 16.4 %collective-permute-done.5.hi = bf16[16,96,384]{2,1,0:T(8,128)(2,1)} collective-permute-done((bf16[16,96,384]{2,1,0:T(8,128)(2,1)}, bf16[16,96,384]{2,1,0:T(8,128)(2,1)}, u32[]{:S(2)}, u32[]{:S(2)}) %collective-permute-start.5) | collective-permute-done | bytes 1179680 | tf_op jit(solution)/shard_map/ppermute | solution.py:331
  86.0 1.1 fusion.2
  87.2 4.9 %collective-permute-start.9 = (bf16[8,96,384]{2,1,0:T(8,128)(2,1)}, bf16[8,96,384]{2,1,0:T(8,128)(2,1)}, u32[]{:S(2)}, u32[]{:S(2)}) collective-permute-start(bf16[8,96,384]{2,1,0:T(8,128)(2,1)} %get-tuple-element.45), channel_id=1, source_target_pairs={{0,4},{4,8},{8,12},{12,16},{16,20},{20,24},{24,28},{1,5},{5,9},{9,... | collective-permute-start | bytes 1769480 | tf_op jit(solution)/shard_map/ppermute | solution.py:331
  92.0 1.9 %collective-permute-start.6 = (bf16[8,96,384]{2,1,0:T(8,128)(2,1)}, bf16[8,96,384]{2,1,0:T(8,128)(2,1)}, u32[]{:S(2)}, u32[]{:S(2)}) collective-permute-start(bf16[8,96,384]{2,1,0:T(8,128)(2,1)} %get-tuple-element.46), channel_id=1, source_target_pairs={{0,4},{4,8},{8,12},{12,16},{16,20},{20,24},{24,28},{1,5},{5,9},{9,... | collective-permute-start | bytes 1769480 | tf_op jit(solution)/shard_map/ppermute | solution.py:331
  94.2 1.2 copy.15
  95.5 10.6 %collective-permute-done.8 = bf16[32,32,384]{2,1,0:T(8,128)(2,1)} collective-permute-done((bf16[32,32,384]{2,1,0:T(8,128)(2,1)}, bf16[32,32,384]{2,1,0:T(8,128)(2,1)}, u32[]{:S(2)}, u32[]{:S(2)}) %collective-permute-start.8) | collective-permute-done | bytes 786464 | tf_op jit(solution)/shard_map/ppermute | solution.py:340
  106.1 1.2 broadcast_select_fusion.2.anchors
  107.4 1.1 copy-done.15
  108.5 23.3 %attend.3.rest_0_ = bf16[16,4,64,384]{3,2,1,0:T(8,128)(2,1)} custom-call(s32[1]{0:T(128)} %bitcast.tm_ref, bf16[16,32,384]{2,1,0:T(8,128)(2,1)S(1)} %copy-done.19, bf16[16,96,384]{2,1,0:T(8,128)(2,1)S(1)} %copy-done.13, bf16[32,32,384]{2,1,0:T(8,128)(2,1)S(1)} %constant_dynamic-update-slice_fusion.own_lo, bf16[16,96,384]{2,1,0:T(8,128)(2,1)} %get-tuple-element.36.own_hi, ...), custom_call_target="tpu_custom_call" | custom-call | flops 1000 | bytes 1000 | tf_op jit(solution)/shard_map/attend/pallas_call | solution.py:310
  131.8 12.7 %attend.4.rest_0_ = bf16[16,4,64,384]{3,2,1,0:T(8,128)(2,1)} custom-call(s32[1]{0:T(128)} %bitcast.tm_ref, bf16[16,32,384]{2,1,0:T(8,128)(2,1)S(1)} %copy-done.11, bf16[16,96,384]{2,1,0:T(8,128)(2,1)} %copy-done.3, bf16[32,32,384]{2,1,0:T(8,128)(2,1)S(1)} %constant_dynamic-update-slice_fusion.own_lo, ...), custom_call_target="tpu_custom_call", output_to_operand_aliasing={{}: (14, {})} | custom-call | flops 1000 | bytes 1000 | tf_op jit(solution)/shard_map/attend/pallas_call | solution.py:310
  144.5 12.7 %attend.5 = bf16[16,4,64,384]{3,2,1,0:T(8,128)(2,1)} custom-call(s32[1]{0:T(128)} %bitcast.tm_ref, bf16[16,32,384]{2,1,0:T(8,128)(2,1)S(1)} %copy-done.11, bf16[16,96,384]{2,1,0:T(8,128)(2,1)} %copy-done.3, bf16[32,32,384]{2,1,0:T(8,128)(2,1)S(1)} %constant_dynamic-update-slice_fusion.own_lo, ...), custom_call_target="tpu_custom_call", output_to_operand_aliasing={{}: (14, {})} | custom-call | flops 1000 | bytes 1000 | tf_op jit(solution)/shard_map/attend/pallas_call | solution.py:310
  (49 shorter events, 9.2 us)
Async XLA Ops:
  0.0 2.3 %copy-start = (bf16[8,384]{1,0:T(8,128)(2,1)S(1)}, bf16[8,384]{1,0:T(8,128)(2,1)}, u32[]{:S(2)}) copy-start(bf16[8,384]{1,0:T(8,128)(2,1)} %param.15) | copy-start | bytes 18436
  3.1 1.1 copy-start.6
  7.9 0.7 copy-start.18
  8.6 10.8 %copy-start.14 = (f32[16,32,384]{2,1,0:T(8,128)}, f32[16,32,384]{2,1,0:T(8,128)S(1)}, u32[]{:S(2)}) copy-start(f32[16,32,384]{2,1,0:T(8,128)S(1)} %get-tuple-element.43.m_lo) | copy-start | bytes 2359300
  8.6 16.6 %copy-start.7 = (bf16[1024,384]{1,0:T(8,128)(2,1)S(1)}, bf16[1024,384]{1,0:T(8,128)(2,1)}, u32[]{:S(2)}) copy-start(bf16[1024,384]{1,0:T(8,128)(2,1)} %table.3) | copy-start | bytes 2359300
  8.6 6.4 %collective-permute-start = (bf16[4,64,384]{2,1,0:T(8,128)(2,1)S(1)}, bf16[4,64,384]{2,1,0:T(8,128)(2,1)S(1)}, u32[]{:S(2)}, u32[]{:S(2)}) collective-permute-start(bf16[4,64,384]{2,1,0:T(8,128)(2,1)S(1)} %get-tuple-element.26), channel_id=1, source_target_pairs={{0,1},{1,2},{2,3},{4,5},{5,6},{6,7},{8,9},{9,10},{10,11},{12,13},{... | collective-permute-start | bytes 589832 | tf_op jit(solution)/shard_map/ppermute | solution.py:350
  12.4 7.0 %collective-permute-start.1 = (bf16[4,64,384]{2,1,0:T(8,128)(2,1)S(1)}, bf16[4,64,384]{2,1,0:T(8,128)(2,1)S(1)}, u32[]{:S(2)}, u32[]{:S(2)}) collective-permute-start(bf16[4,64,384]{2,1,0:T(8,128)(2,1)S(1)} %get-tuple-element.27), channel_id=1, source_target_pairs={{1,0},{2,1},{3,2},{5,4},{6,5},{7,6},{9,8},{10,9},{11,10},{13,12},{... | collective-permute-start | bytes 589832 | tf_op jit(solution)/shard_map/ppermute | solution.py:350
  20.5 0.7 copy-start.10
  21.2 0.9 copy-start.4
  22.1 18.0 %collective-permute-start.4 = (bf16[32,32,384]{2,1,0:T(8,128)(2,1)S(1)}, bf16[32,32,384]{2,1,0:T(8,128)(2,1)S(1)}, u32[]{:S(2)}, u32[]{:S(2)}) collective-permute-start(bf16[32,32,384]{2,1,0:T(8,128)(2,1)S(1)} %constant_dynamic-update-slice_fusion.own_lo), channel_id=1, source_target_pairs={{0,4},{4,8},{8,12},{12,16},{16,20},{20,24},{24,28},{1,5},{5,9},{9,... | collective-permute-start | bytes 2359304 | tf_op jit(solution)/shard_map/ppermute | solution.py:331
  34.9 1.0 copy-start.12
  41.1 9.7 %collective-permute-start.7 = (bf16[32,32,384]{2,1,0:T(8,128)(2,1)}, bf16[32,32,384]{2,1,0:T(8,128)(2,1)}, u32[]{:S(2)}, u32[]{:S(2)}) collective-permute-start(bf16[32,32,384]{2,1,0:T(8,128)(2,1)} %broadcast_select_fusion), channel_id=1, source_target_pairs={{0,16},{4,20},{1,17},{5,21},{2,18},{6,22},{3,19},{7,23}} | collective-permute-start | bytes 2359304 | tf_op jit(solution)/shard_map/ppermute | solution.py:340
  42.6 43.4 %collective-permute-start.5 = (bf16[16,96,384]{2,1,0:T(8,128)(2,1)}, bf16[16,96,384]{2,1,0:T(8,128)(2,1)}, u32[]{:S(2)}, u32[]{:S(2)}) collective-permute-start(bf16[16,96,384]{2,1,0:T(8,128)(2,1)} %get-tuple-element.36.own_hi), channel_id=1, source_target_pairs={{0,4},{4,8},{8,12},{12,16},{16,20},{20,24},{24,28},{1,5},{5,9},{9,... | collective-permute-start | bytes 3538952 | tf_op jit(solution)/shard_map/ppermute | solution.py:331
  46.4 9.2 %collective-permute-start.2 = (bf16[12,64,384]{2,1,0:T(8,128)(2,1)}, bf16[12,64,384]{2,1,0:T(8,128)(2,1)S(1)}, u32[]{:S(2)}, u32[]{:S(2)}) collective-permute-start(bf16[12,64,384]{2,1,0:T(8,128)(2,1)} %get-tuple-element.30), channel_id=1, source_target_pairs={{0,1},{1,2},{2,3},{4,5},{5,6},{6,7},{8,9},{9,10},{10,11},{12,13},{... | collective-permute-start | bytes 1769480 | tf_op jit(solution)/shard_map/ppermute | solution.py:350
  48.5 11.6 %collective-permute-start.3 = (bf16[12,64,384]{2,1,0:T(8,128)(2,1)S(1)}, bf16[12,64,384]{2,1,0:T(8,128)(2,1)S(1)}, u32[]{:S(2)}, u32[]{:S(2)}) collective-permute-start(bf16[12,64,384]{2,1,0:T(8,128)(2,1)S(1)} %get-tuple-element.31), channel_id=1, source_target_pairs={{1,0},{2,1},{3,2},{5,4},{6,5},{7,6},{9,8},{10,9},{11,10},{13,12},{... | collective-permute-start | bytes 1769480 | tf_op jit(solution)/shard_map/ppermute | solution.py:350
  52.9 53.1 %collective-permute-start.8 = (bf16[32,32,384]{2,1,0:T(8,128)(2,1)}, bf16[32,32,384]{2,1,0:T(8,128)(2,1)}, u32[]{:S(2)}, u32[]{:S(2)}) collective-permute-start(bf16[32,32,384]{2,1,0:T(8,128)(2,1)} %broadcast_select_fusion.1), channel_id=1, source_target_pairs={{0,8},{4,12},{16,24},{20,28},{1,9},{5,13},{17,25},{21,29},{2,10},{... | collective-permute-start | bytes 2359304 | tf_op jit(solution)/shard_map/ppermute | solution.py:340
  60.1 0.8 copy-start.16
  60.9 1.1 copy-start.17
  67.1 1.4 copy-start.2
  68.5 1.1 copy-start.3
  69.6 37.7 %copy-start.1 = (bf16[16,96,384]{2,1,0:T(8,128)(2,1)}, bf16[16,96,384]{2,1,0:T(8,128)(2,1)S(1)}, u32[]{:S(2)}) copy-start(bf16[16,96,384]{2,1,0:T(8,128)(2,1)S(1)} %get-tuple-element.38.own_hi) | copy-start | bytes 3538948
  69.6 24.3 %copy-start.20 = (bf16[384,384]{1,0:T(8,128)(2,1)S(1)}, bf16[384,384]{1,0:T(8,128)(2,1)}, u32[]{:S(2)}) copy-start(bf16[384,384]{1,0:T(8,128)(2,1)} %param.18) | copy-start | bytes 884740
  87.2 44.6 %collective-permute-start.9 = (bf16[8,96,384]{2,1,0:T(8,128)(2,1)}, bf16[8,96,384]{2,1,0:T(8,128)(2,1)}, u32[]{:S(2)}, u32[]{:S(2)}) collective-permute-start(bf16[8,96,384]{2,1,0:T(8,128)(2,1)} %get-tuple-element.45), channel_id=1, source_target_pairs={{0,4},{4,8},{8,12},{12,16},{16,20},{20,24},{24,28},{1,5},{5,9},{9,... | collective-permute-start | bytes 1769480 | tf_op jit(solution)/shard_map/ppermute | solution.py:331
  92.0 52.5 %collective-permute-start.6 = (bf16[8,96,384]{2,1,0:T(8,128)(2,1)}, bf16[8,96,384]{2,1,0:T(8,128)(2,1)}, u32[]{:S(2)}, u32[]{:S(2)}) collective-permute-start(bf16[8,96,384]{2,1,0:T(8,128)(2,1)} %get-tuple-element.46), channel_id=1, source_target_pairs={{0,4},{4,8},{8,12},{12,16},{16,20},{20,24},{24,28},{1,5},{5,9},{9,... | collective-permute-start | bytes 1769480 | tf_op jit(solution)/shard_map/ppermute | solution.py:331
  95.4 11.9 %copy-start.8 = (bf16[384,384]{1,0:T(8,128)(2,1)S(1)}, bf16[384,384]{1,0:T(8,128)(2,1)}, u32[]{:S(2)}) copy-start(bf16[384,384]{1,0:T(8,128)(2,1)} %wk.5) | copy-start | bytes 884740
  95.4 11.9 %copy-start.9 = (bf16[384,384]{1,0:T(8,128)(2,1)S(1)}, bf16[384,384]{1,0:T(8,128)(2,1)}, u32[]{:S(2)}) copy-start(bf16[384,384]{1,0:T(8,128)(2,1)} %w_out.5) | copy-start | bytes 884740
  95.4 11.9 %copy-start.13 = (bf16[16,96,384]{2,1,0:T(8,128)(2,1)S(1)}, bf16[16,96,384]{2,1,0:T(8,128)(2,1)}, u32[]{:S(2)}) copy-start(bf16[16,96,384]{2,1,0:T(8,128)(2,1)} %copy-done.12) | copy-start | bytes 3538948
  95.5 11.9 %copy-start.19 = (bf16[16,32,384]{2,1,0:T(8,128)(2,1)S(1)}, bf16[16,32,384]{2,1,0:T(8,128)(2,1)}, u32[]{:S(2)}) copy-start(bf16[16,32,384]{2,1,0:T(8,128)(2,1)} %copy-done.18) | copy-start | bytes 1179652
  107.4 1.1 copy-start.15
  108.5 23.3 %copy-start.5 = (f32[16,32,384]{2,1,0:T(8,128)S(1)}, f32[16,32,384]{2,1,0:T(8,128)}, u32[]{:S(2)}) copy-start(f32[16,32,384]{2,1,0:T(8,128)} %copy-done.4) | copy-start | bytes 2359300
  108.5 23.3 %copy-start.11 = (bf16[16,32,384]{2,1,0:T(8,128)(2,1)S(1)}, bf16[16,32,384]{2,1,0:T(8,128)(2,1)}, u32[]{:S(2)}) copy-start(bf16[16,32,384]{2,1,0:T(8,128)(2,1)} %copy-done.10) | copy-start | bytes 1179652

commit v3 on v2

--- a/solution.py
+++ b/solution.py
@@ -113,38 +113,29 @@
 def attend_kernel(
     tm_ref, x_lo, x_hi, own_lo, own_hi, lo, hi, anchors, m_lo, m_hi, wq_t, wk, wv_t, w_out, *rest
 ):
-    out, mask = rest[-2:]
+    out, mask, scores, spread, spread_first = rest[-5:]
     tm = tm_ref[0]
     width = x_lo.shape[-1]
     queries = WINDOW * GROUP
-    lanes = 2 * queries
+    pairs = width // 128
+    columns = STEP * pairs * 2
     slabs = 2 * WINDOW + ANCHORS
+    anchor_rows = ANCHORS * GROUP
+    window_rows = 2 * queries
 
     @pl.when(pl.program_id(0) == 0)
     def _():
-        row = lax.broadcasted_iota(jnp.int32, (slabs * GROUP, lanes), 0)
-        lane = lax.broadcasted_iota(jnp.int32, (slabs * GROUP, lanes), 1)
+        row = lax.broadcasted_iota(jnp.int32, (slabs * GROUP, queries), 0)
+        lane = lax.broadcasted_iota(jnp.int32, (slabs * GROUP, queries), 1)
         u = row // GROUP
-        t = (lane % queries) // GROUP
-        met = (row - lane + lanes) % GROUP
+        t = lane // GROUP
+        met = (row - lane + queries) % GROUP
         mine = (u < WINDOW) & (u % GROUP == met) & (u <= t)
         past = (u >= WINDOW) & (u < 2 * WINDOW) & (u % GROUP == met) & (u - WINDOW > t)
         first = (u >= 2 * WINDOW) & (u - 2 * WINDOW == met)
         mask[...] = jnp.where(mine | past | first, 1.0, 0.0).astype(BF16)
-
-    sub = lax.broadcasted_iota(jnp.int32, (GROUP, lanes), 0)
-    lane = lax.broadcasted_iota(jnp.int32, (GROUP, lanes), 1)
-    t = (lane % queries) // GROUP
-    met = (sub - lane + lanes) % GROUP
-    places = []
-    for b in range(WINDOW // GROUP):
-        u = met + b * GROUP
-        places.append(jnp.where(u <= t, u, u + WINDOW))
-    open_window = [(c < WINDOW) | (tm > 0) for c in places]
-    open_anchor = (met < ANCHORS) & (met < tm * WINDOW + t - (WINDOW - 1))
-
-    anchor_rows = ANCHORS * GROUP
-    window_rows = 2 * queries
+        spread_first[...] = jnp.zeros(spread_first.shape, BF16)
+
     x = jnp.concatenate([ref[i] for i in range(STEP) for ref in (x_lo, x_hi)], axis=0)
     window = [ref[i] for i in range(STEP) for ref in (own_lo, own_hi, lo, hi)]
     window = jnp.concatenate(window, axis=0)
@@ -154,66 +145,91 @@
     k_all = jnp.dot(
         jnp.concatenate([window, first], axis=0), wk[...], preferred_element_type=F32
     ).astype(BF16)
-    v_all = lax.dot_general(wv_t[...], window, NT, preferred_element_type=F32).astype(BF16)
+    v_t = lax.dot_general(wv_t[...], window, NT, preferred_element_type=F32).astype(BF16)
     va_t = lax.dot_general(wv_t[...], first, NT, preferred_element_type=F32).astype(BF16)
+
     blank = jnp.zeros((64, queries), BF16)
-    no_rows = jnp.zeros((anchor_rows, lanes), BF16)
-    columns = []
     for i in range(STEP):
         at = STEP * window_rows + i * anchor_rows
         k = jnp.concatenate(
             [k_all[i * window_rows : (i + 1) * window_rows], k_all[at : at + anchor_rows]], axis=0
         )
-        v_t = v_all[:, i * window_rows : (i + 1) * window_rows]
-        parts = []
-        for pair in range(width // 128):
+        for pair in range(pairs):
             at = pair * 128
             across = slice(i * queries, (i + 1) * queries)
             left = jnp.concatenate([q_t[at : at + 64, across], blank], axis=0)
             right = jnp.concatenate([blank, q_t[at + 64 : at + 128, across]], axis=0)
-            s = jnp.dot(
+            column = (i * pairs + pair) * 2 * queries
+            scores[:, column : column + 2 * queries] = jnp.dot(
                 k[:, at : at + 128],
                 jnp.concatenate([left, right], axis=1),
                 preferred_element_type=F32,
             )
-            s = [s[j * GROUP : (j + 1) * GROUP] for j in range(slabs)]
-            merged = []
-            for b in range(WINDOW // GROUP):
-                w = s[b * GROUP]
-                for d in range(GROUP):
-                    u = b * GROUP + d
-                    if d > 0:
-                        w = jnp.where(places[b] == u, s[u], w)
-                    w = jnp.where(places[b] == WINDOW + u, s[WINDOW + u], w)
-                merged.append(jnp.where(open_window[b], w, -1e30))
-            w = s[2 * WINDOW]
-            for u in range(1, ANCHORS):
-                w = jnp.where(met == u, s[2 * WINDOW + u], w)
-            merged.append(jnp.where(open_anchor, w, -1e30))
-            top = jnp.max(
-                jnp.maximum(jnp.maximum(merged[0], merged[1]), merged[2]), axis=0, keepdims=True
-            )
-            e = [jnp.exp(w - top) for w in merged]
-            total = jnp.sum(e[0] + e[1] + e[2], axis=0, keepdims=True)
-            over = 1.0 / total
-            p = [w * over for w in e]
-            p = [jnp.concatenate([w, w], axis=0).astype(BF16) for w in p]
-            spread = []
-            for j in range(slabs // 2):
-                b = (2 * j % WINDOW) // GROUP if j < WINDOW else 2
-                spread.append(p[b] * mask[j * 16 : (j + 1) * 16, :])
-            p_window = jnp.concatenate(spread[:WINDOW], axis=0)
-            p_first = jnp.concatenate(spread[WINDOW:], axis=0)
-            p_first = [p_first if n == i else no_rows for n in range(STEP)]
-            o = jnp.dot(v_t[at : at + 128], p_window, preferred_element_type=F32)
-            o += jnp.dot(
-                va_t[at : at + 128],
-                jnp.concatenate(p_first, axis=0),
+
+    sub = lax.broadcasted_iota(jnp.int32, (GROUP, queries), 0)
+    lane = lax.broadcasted_iota(jnp.int32, (GROUP, queries), 1)
+    t = lane // GROUP
+    met = (sub - lane + queries) % GROUP
+
+    def slab(u, c):
+        return scores[u * GROUP : (u + 1) * GROUP, c * queries : (c + 1) * queries]
+
+    merged = []
+    for b in range(WINDOW // GROUP):
+        u = met + b * GROUP
+        place = jnp.where(u <= t, u, u + WINDOW)
+        w = [slab(b * GROUP, c) for c in range(columns)]
+        for d in range(GROUP):
+            for u in (b * GROUP + d, WINDOW + b * GROUP + d):
+                if u != b * GROUP:
+                    here = place == u
+                    w = [jnp.where(here, slab(u, c), w[c]) for c in range(columns)]
+        seen = (place < WINDOW) | (tm > 0)
+        merged.append([jnp.where(seen, v, -1e30) for v in w])
+    w = [slab(2 * WINDOW, c) for c in range(columns)]
+    for u in range(1, ANCHORS):
+        here = met == u
+        w = [jnp.where(here, slab(2 * WINDOW + u, c), w[c]) for c in range(columns)]
+    seen = (met < ANCHORS) & (met < tm * WINDOW + t - (WINDOW - 1))
+    merged.append([jnp.where(seen, v, -1e30) for v in w])
+
+    merged = [jnp.concatenate(w, axis=1) for w in merged]
+    top = jnp.max(
+        jnp.maximum(jnp.maximum(merged[0], merged[1]), merged[2]), axis=0, keepdims=True
+    )
+    e = [jnp.exp(w - top) for w in merged]
+    over = 1.0 / jnp.sum(e[0] + e[1] + e[2], axis=0, keepdims=True)
+    probs = [w * over for w in e]
+    probs = [jnp.concatenate([w, w], axis=0).astype(BF16) for w in probs]
+
+    for j in range(slabs // 2):
+        b = (2 * j % WINDOW) // GROUP if j < WINDOW else 2
+        here = mask[j * 16 : (j + 1) * 16, :]
+        for c in range(columns):
+            piece = probs[b][:, c * queries : (c + 1) * queries] * here
+            across = slice(c * queries, (c + 1) * queries)
+            if j < WINDOW:
+                spread[j * 16 : (j + 1) * 16, across] = piece
+            else:
+                at = c // (2 * pairs) * anchor_rows + (j - WINDOW) * 16
+                spread_first[at : at + 16, across] = piece
+
+    attended = []
+    for i in range(STEP):
+        parts = []
+        for pair in range(pairs):
+            at = slice(pair * 128, (pair + 1) * 128)
+            column = (i * pairs + pair) * 2 * queries
+            across = slice(column, column + 2 * queries)
+            o = jnp.dot(
+                v_t[at, i * window_rows : (i + 1) * window_rows],
+                spread[:, across],
                 preferred_element_type=F32,
             )
+            o += jnp.dot(va_t[at], spread_first[:, across], preferred_element_type=F32)
             parts += [o[:64, :queries], o[64:, queries:]]
-        columns.append(jnp.concatenate(parts, axis=0).astype(BF16))
-    attended = jnp.concatenate(columns, axis=1)
+        attended.append(jnp.concatenate(parts, axis=0).astype(BF16))
+    attended = jnp.concatenate(attended, axis=1)
     result = lax.dot_general(attended, w_out[...], TN, preferred_element_type=F32)
     results = []
     for i in range(STEP):
@@ -295,6 +311,8 @@
 def attend(tm, blocks, weights, out, shape, positions, row_of):
     count, _, cols, width = shape
     per_row = cols // (STEP * GROUP)
+    keys = (2 * WINDOW + ANCHORS) * GROUP
+    lanes = STEP * (width // 64) * WINDOW * GROUP
 
     def block(a, start):
         return pl.BlockSpec((STEP,) + a.shape[1:], lambda g: (g + start // STEP, 0, 0))
@@ -317,7 +335,10 @@
         ),
         out_shape=jax.ShapeDtypeStruct(shape, BF16),
         scratch_shapes=[
-            pltpu.VMEM(((2 * WINDOW + ANCHORS) * GROUP, 2 * WINDOW * GROUP), BF16)
+            pltpu.VMEM((keys, WINDOW * GROUP), BF16),
+            pltpu.VMEM((keys, lanes), F32),
+            pltpu.VMEM((2 * WINDOW * GROUP, lanes), BF16),
+            pltpu.VMEM((STEP * ANCHORS * GROUP, lanes), BF16),
         ],
         input_output_aliases=aliases,
         compiler_params=params(),
@@ -386,7 +407,7 @@
     emb, top, bottom, mixed_c, normed_c, rolled_c = embed(ANCHORS, shape[0] - ANCHORS, *shared)
     lo, _ = lax.optimization_barrier((lo, rolled_c))
     anchors = anchors_of(first, lo, tm)
-    hi = send(rolled_c, 1)
+    hi = [send(rolled_c[r * row : (r + 1) * row], 1) for r in range(inner // row)]
     mixed_d, normed_d, rolled_d = edge(ANCHORS, emb, *halo(top, bottom), conv, gain)
 
     def blocks(x_lo, x_hi, own_hi, hi, m_lo, m_hi, start, at, hi_at):
@@ -402,16 +423,18 @@
             (m_hi, at),
         ]
 
-    out = attend(
-        tm_arg,
-        blocks(normed_a, normed_c, rolled_c, hi, mixed_a, mixed_c, 0, 0, 0),
-        weights,
-        None,
-        shape,
-        inner * GROUP,
-        lambda r: r + 1,
-    )
-    to_send, _ = lax.optimization_barrier((rolled_d, hi))
+    out = None
+    for r in range(inner // row):
+        out = attend(
+            tm_arg,
+            blocks(normed_a, normed_c, rolled_c, hi[r], mixed_a, mixed_c, 0, r * row, 0),
+            weights,
+            out,
+            shape,
+            cols,
+            lambda _, r=r: r + 1,
+        )
+    to_send, _ = lax.optimization_barrier((rolled_d, hi[0]))
     later = [send(to_send[r * row : (r + 1) * row], 1) for r in range(2)]
     for r in range(2):
         out = attend(

time: 158 us -> 138 us (0.87)
  the two profiles are of different devices: /device:TPU:13 before, /device:TPU:9 now
where the time goes in v3:
time: 138 us; the launch traced here: 137 us
  Pallas kernels  50 us (36%)
  waiting for transfers between devices  36.1 us (26%)
  starting transfers between devices  31.2 us (23%)
  local copies, waits for them, and re-layouts  13.8 us (10%)
  other arithmetic  4.52 us (3%)
    ppermute x5, waiting for transfers between devices, send(): return lax.ppermute(x, 'tm', [(i, i + by) for i in range(count - by)])  31.1 us
    pallas_call x4, Pallas kernels, attend(): pl.pallas_call(attend_kernel, grid=(positions // (STEP * GROUP),), in_spe...  30.3 us
    ppermute x5, starting transfers between devices, send(): return lax.ppermute(x, 'tm', [(i, i + by) for i in range(count - by)])  17.5 us
    pallas_call x2, Pallas kernels, embed(): pl.pallas_call(functools.partial(embed_kernel, first), grid=(count // 2,)...  13.3 us
    unnamed x43, local copies, waits for them, and re-layouts  9.08 us
    pallas_call x2, Pallas kernels, edge(): pl.pallas_call(functools.partial(edge_kernel, first), grid=(count // 2,),...  6.45 us
    ppermute x2, starting transfers between devices, halo(): lax.ppermute(bottom, 'space', up)  5.72 us
    ppermute x2, starting transfers between devices, halo(): lax.ppermute(top, 'space', [(j, i) for i, j in up])  5.12 us
  transfers between devices with their start and end apart: 11, of which 7 were waited for; matrix products, arithmetic and copies ran while one was open for 6% of the time, Pallas kernels for 28%

profile of v3, /device:TPU:9, one launch (start us, length us, event | category | flops | bytes accessed | tf_op | source)
XLA Modules:
  0.0 136.8 jit_solution(12134389701701563735)
XLA Ops:
  3.1 1.1 copy-done.12
  4.3 3.6 %embed.2 = (bf16[4,4,64,384]{3,2,1,0:T(8,128)(2,1)S(1)}, bf16[4,64,384]{2,1,0:T(8,128)(2,1)S(1)}, bf16[4,64,384]{2,1,0:T(8,128)(2,1)S(1)}, f32[16,32,384]{2,1,0:...) custom-call(s32[8,1,512]{2,1,0:T(1,128)S(1)} %reshape.14.ids, ...), custom_call_target="tpu_custom_call" | custom-call | flops 1000 | bytes 1000 | tf_op jit(solution)/shard_map/embed/pallas_call | solution.py:270
  7.9 3.8 %collective-permute-start = (bf16[4,64,384]{2,1,0:T(8,128)(2,1)S(1)}, bf16[4,64,384]{2,1,0:T(8,128)(2,1)S(1)}, u32[]{:S(2)}, u32[]{:S(2)}) collective-permute-start(bf16[4,64,384]{2,1,0:T(8,128)(2,1)S(1)} %get-tuple-element.26), channel_id=1, source_target_pairs={{0,1},{1,2},{2,3},{4,5},{5,6},{6,7},{8,9},{9,10},{10,11},{12,13},{... | collective-permute-start | bytes 589832 | tf_op jit(solution)/shard_map/ppermute | solution.py:371
  11.7 1.9 %collective-permute-start.1 = (bf16[4,64,384]{2,1,0:T(8,128)(2,1)S(1)}, bf16[4,64,384]{2,1,0:T(8,128)(2,1)S(1)}, u32[]{:S(2)}, u32[]{:S(2)}) collective-permute-start(bf16[4,64,384]{2,1,0:T(8,128)(2,1)S(1)} %get-tuple-element.27), channel_id=1, source_target_pairs={{1,0},{2,1},{3,2},{5,4},{6,5},{7,6},{9,8},{10,9},{11,10},{13,12},{... | collective-permute-start | bytes 589832 | tf_op jit(solution)/shard_map/ppermute | solution.py:371
  14.3 4.4 %collective-permute-done.1.after = bf16[4,64,384]{2,1,0:T(8,128)(2,1)S(1)} collective-permute-done((bf16[4,64,384]{2,1,0:T(8,128)(2,1)S(1)}, bf16[4,64,384]{2,1,0:T(8,128)(2,1)S(1)}, u32[]{:S(2)}, u32[]{:S(2)}) %collective-permute-start.1) | collective-permute-done | bytes 196640 | tf_op jit(solution)/shard_map/ppermute | solution.py:371
  21.4 3.1 %collective-permute-start.4 = (bf16[32,32,384]{2,1,0:T(8,128)(2,1)S(1)}, bf16[32,32,384]{2,1,0:T(8,128)(2,1)S(1)}, u32[]{:S(2)}, u32[]{:S(2)}) collective-permute-start(bf16[32,32,384]{2,1,0:T(8,128)(2,1)S(1)} %constant_dynamic-update-slice_fusion.own_lo), channel_id=1, source_target_pairs={{0,4},{4,8},{8,12},{12,16},{16,20},{20,24},{24,28},{1,5},{5,9},{9,... | collective-permute-start | bytes 2359304 | tf_op jit(solution)/shard_map/ppermute | solution.py:352
  24.6 9.7 %embed.3 = (bf16[12,4,64,384]{3,2,1,0:T(8,128)(2,1)}, bf16[12,64,384]{2,1,0:T(8,128)(2,1)}, bf16[12,64,384]{2,1,0:T(8,128)(2,1)}, f32[16,96,384]{2,1,0:T(8,128)}...) custom-call(s32[8,1,512]{2,1,0:T(1,128)S(1)} %reshape.14.ids, bf16[16,4,64,384]{3,2,1,0:T(8,128)(2,1)} %frames.3, ...), custom_call_target="tpu_custom_call" | custom-call | flops 1000 | bytes 1000 | tf_op jit(solution)/shard_map/embed/pallas_call | solution.py:270
  35.3 5.0 %collective-permute-done.4.lo = bf16[32,32,384]{2,1,0:T(8,128)(2,1)S(1)} collective-permute-done((bf16[32,32,384]{2,1,0:T(8,128)(2,1)S(1)}, bf16[32,32,384]{2,1,0:T(8,128)(2,1)S(1)}, u32[]{:S(2)}, u32[]{:S(2)}) %collective-permute-start.4) | collective-permute-done | bytes 786464 | tf_op jit(solution)/shard_map/ppermute | solution.py:352
  41.3 1.5 %collective-permute-start.7 = (bf16[32,32,384]{2,1,0:T(8,128)(2,1)}, bf16[32,32,384]{2,1,0:T(8,128)(2,1)}, u32[]{:S(2)}, u32[]{:S(2)}) collective-permute-start(bf16[32,32,384]{2,1,0:T(8,128)(2,1)} %broadcast_select_fusion), channel_id=1, source_target_pairs={{0,16},{4,20},{1,17},{5,21},{2,18},{6,22},{3,19},{7,23}} | collective-permute-start | bytes 2359304 | tf_op jit(solution)/shard_map/ppermute | solution.py:361
  42.8 1.9 %collective-permute-start.2 = (bf16[12,64,384]{2,1,0:T(8,128)(2,1)}, bf16[12,64,384]{2,1,0:T(8,128)(2,1)}, u32[]{:S(2)}, u32[]{:S(2)}) collective-permute-start(bf16[12,64,384]{2,1,0:T(8,128)(2,1)} %get-tuple-element.30), channel_id=1, source_target_pairs={{0,1},{1,2},{2,3},{4,5},{5,6},{6,7},{8,9},{9,10},{10,11},{12,13},{... | collective-permute-start | bytes 1769480 | tf_op jit(solution)/shard_map/ppermute | solution.py:371
  44.8 3.2 %collective-permute-start.3 = (bf16[12,64,384]{2,1,0:T(8,128)(2,1)}, bf16[12,64,384]{2,1,0:T(8,128)(2,1)}, u32[]{:S(2)}, u32[]{:S(2)}) collective-permute-start(bf16[12,64,384]{2,1,0:T(8,128)(2,1)} %get-tuple-element.31), channel_id=1, source_target_pairs={{1,0},{2,1},{3,2},{5,4},{6,5},{7,6},{9,8},{10,9},{11,10},{13,12},{... | collective-permute-start | bytes 1769480 | tf_op jit(solution)/shard_map/ppermute | solution.py:371
  48.0 1.2 fusion.2
  49.1 2.2 %collective-permute-start.5 = (bf16[8,96,384]{2,1,0:T(8,128)(2,1)}, bf16[8,96,384]{2,1,0:T(8,128)(2,1)S(1)}, u32[]{:S(2)}, u32[]{:S(2)}) collective-permute-start(bf16[8,96,384]{2,1,0:T(8,128)(2,1)} %get-tuple-element.46), channel_id=1, source_target_pairs={{0,4},{4,8},{8,12},{12,16},{16,20},{20,24},{24,28},{1,5},{5,9},{9,... | collective-permute-start | bytes 1769480 | tf_op jit(solution)/shard_map/ppermute | solution.py:352
  51.4 2.1 %broadcast_select_fusion.1 = bf16[32,32,384]{2,1,0:T(8,128)(2,1)} fusion(bf16[32,32,384]{2,1,0:T(8,128)(2,1)} %collective-permute-done.7, bf16[32,32,384]{2,1,0:T(8,128)(2,1)} %broadcast_select_fusion, pred[]{:T(512)S(6)} %or.7), kind=kLoop, calls=%fused_computation.1 | loop fusion | flops 393216 | bytes 2359297 | tf_op jit(solution)/shard_map/jit(_where)/select_n | solution.py:363
  53.6 1.3 collective-permute-start.8
  54.8 3.8 %collective-permute-start.10 = (bf16[8,96,384]{2,1,0:T(8,128)(2,1)}, bf16[8,96,384]{2,1,0:T(8,128)(2,1)}, u32[]{:S(2)}, u32[]{:S(2)}) collective-permute-start(bf16[8,96,384]{2,1,0:T(8,128)(2,1)} %get-tuple-element.45), channel_id=1, source_target_pairs={{0,4},{4,8},{8,12},{12,16},{16,20},{20,24},{24,28},{1,5},{5,9},{9,... | collective-permute-start | bytes 1769480 | tf_op jit(solution)/shard_map/ppermute | solution.py:352
  58.7 5.4 %edge.3 = (f32[16,96,384]{2,1,0:T(8,128)S(1)}, bf16[16,96,384]{2,1,0:T(8,128)(2,1)S(1)}, bf16[16,96,384]{2,1,0:T(8,128)(2,1)S(1)}) custom-call(bf16[12,4,64,384]{3,2,1,0:T(8,128)(2,1)} %get-tuple-element.29.emb, bf16[12,64,384]{2,1,0:T(8,128)(2,1)} %collective-permute-done.2.before, bf16[12,64,384]{2,1,0:T(8,128)(2,1)} %collective-permute-done.3.after, ...), custom_call_target="tpu_custom_call" | custom-call | flops 1000 | bytes 1000 | tf_op jit(solution)/shard_map/edge/pallas_call | solution.py:299
  64.1 1.4 %copy-done.3 = f32[16,96,384]{2,1,0:T(8,128)} copy-done((f32[16,96,384]{2,1,0:T(8,128)}, f32[16,96,384]{2,1,0:T(8,128)S(1)}, u32[]{:S(2)}) %copy-start.3) | copy-done | bytes 2359320
  66.6 9.8 %collective-permute-done.5.hi = bf16[8,96,384]{2,1,0:T(8,128)(2,1)S(1)} collective-permute-done((bf16[8,96,384]{2,1,0:T(8,128)(2,1)}, bf16[8,96,384]{2,1,0:T(8,128)(2,1)S(1)}, u32[]{:S(2)}, u32[]{:S(2)}) %collective-permute-start.5) | collective-permute-done | bytes 589856 | tf_op jit(solution)/shard_map/ppermute | solution.py:352
  76.5 1.2 fusion.3
  77.7 3.9 %collective-permute-start.9 = (bf16[8,96,384]{2,1,0:T(8,128)(2,1)}, bf16[8,96,384]{2,1,0:T(8,128)(2,1)}, u32[]{:S(2)}, u32[]{:S(2)}) collective-permute-start(bf16[8,96,384]{2,1,0:T(8,128)(2,1)} %get-tuple-element.47), channel_id=1, source_target_pairs={{0,4},{4,8},{8,12},{12,16},{16,20},{20,24},{24,28},{1,5},{5,9},{9,... | collective-permute-start | bytes 1769480 | tf_op jit(solution)/shard_map/ppermute | solution.py:352
  81.6 4.4 %collective-permute-start.6 = (bf16[8,96,384]{2,1,0:T(8,128)(2,1)}, bf16[8,96,384]{2,1,0:T(8,128)(2,1)}, u32[]{:S(2)}, u32[]{:S(2)}) collective-permute-start(bf16[8,96,384]{2,1,0:T(8,128)(2,1)} %get-tuple-element.48), channel_id=1, source_target_pairs={{0,4},{4,8},{8,12},{12,16},{16,20},{20,24},{24,28},{1,5},{5,9},{9,... | collective-permute-start | bytes 1769480 | tf_op jit(solution)/shard_map/ppermute | solution.py:352
  86.1 1.2 copy.15
  87.2 1.2 copy.16
  88.5 1.4 %broadcast_select_fusion.2.anchors = bf16[32,32,384]{2,1,0:T(8,128)(2,1)S(1)} fusion(bf16[32,32,384]{2,1,0:T(8,128)(2,1)} %collective-permute-done.8, bf16[32,32,384]{2,1,0:T(8,128)(2,1)} %broadcast_select_fusion.1, pred[]{:T(512)S(6)} %or.6), kind=kLoop, calls=%fused_computation.2 | loop fusion | flops 393216 | bytes 2359297 | tf_op jit(solution)/shard_map/jit(_where)/select_n | solution.py:363
  90.3 7.5 %attend.4.rest_0_ = bf16[16,4,64,384]{3,2,1,0:T(8,128)(2,1)} custom-call(s32[1]{0:T(128)} %bitcast.tm_ref, bf16[16,32,384]{2,1,0:T(8,128)(2,1)S(1)} %copy-done.15, bf16[16,96,384]{2,1,0:T(8,128)(2,1)} %copy-done.4, bf16[32,32,384]{2,1,0:T(8,128)(2,1)S(1)} %constant_dynamic-update-slice_fusion.own_lo, bf16[16,96,384]{2,1,0:T(8,128)(2,1)} %copy-done.1, ...), custom_call_target="tpu_custom_call" | custom-call | flops 1000 | bytes 1000 | tf_op jit(solution)/shard_map/attend/pallas_call | solution.py:328
  97.8 8.6 %collective-permute-done.10.hi = bf16[8,96,384]{2,1,0:T(8,128)(2,1)} collective-permute-done((bf16[8,96,384]{2,1,0:T(8,128)(2,1)}, bf16[8,96,384]{2,1,0:T(8,128)(2,1)}, u32[]{:S(2)}, u32[]{:S(2)}) %collective-permute-start.10) | collective-permute-done | bytes 589856 | tf_op jit(solution)/shard_map/ppermute | solution.py:352
  106.4 7.6 %attend.5.rest_0_ = bf16[16,4,64,384]{3,2,1,0:T(8,128)(2,1)} custom-call(s32[1]{0:T(128)} %bitcast.tm_ref, bf16[16,32,384]{2,1,0:T(8,128)(2,1)S(1)} %copy-done.15, bf16[16,96,384]{2,1,0:T(8,128)(2,1)} %copy-done.4, bf16[32,32,384]{2,1,0:T(8,128)(2,1)S(1)} %constant_dynamic-update-slice_fusion.own_lo, ...), custom_call_target="tpu_custom_call", output_to_operand_aliasing={{}: (14, {})} | custom-call | flops 1000 | bytes 1000 | tf_op jit(solution)/shard_map/attend/pallas_call | solution.py:328
  114.0 5.0 %collective-permute-done.9.hi = bf16[8,96,384]{2,1,0:T(8,128)(2,1)} collective-permute-done((bf16[8,96,384]{2,1,0:T(8,128)(2,1)}, bf16[8,96,384]{2,1,0:T(8,128)(2,1)}, u32[]{:S(2)}, u32[]{:S(2)}) %collective-permute-start.9) | collective-permute-done | bytes 589856 | tf_op jit(solution)/shard_map/ppermute | solution.py:352
  119.0 7.6 %attend.6.rest_0_ = bf16[16,4,64,384]{3,2,1,0:T(8,128)(2,1)} custom-call(s32[1]{0:T(128)} %bitcast.tm_ref, bf16[16,32,384]{2,1,0:T(8,128)(2,1)S(1)} %copy-done.17, bf16[16,96,384]{2,1,0:T(8,128)(2,1)} %copy-done.5, bf16[32,32,384]{2,1,0:T(8,128)(2,1)S(1)} %constant_dynamic-update-slice_fusion.own_lo, ...), custom_call_target="tpu_custom_call", output_to_operand_aliasing={{}: (14, {})} | custom-call | flops 1000 | bytes 1000 | tf_op jit(solution)/shard_map/attend/pallas_call | solution.py:328
  126.6 2.6 %collective-permute-done.6.hi = bf16[8,96,384]{2,1,0:T(8,128)(2,1)} collective-permute-done((bf16[8,96,384]{2,1,0:T(8,128)(2,1)}, bf16[8,96,384]{2,1,0:T(8,128)(2,1)}, u32[]{:S(2)}, u32[]{:S(2)}) %collective-permute-start.6) | collective-permute-done | bytes 589856 | tf_op jit(solution)/shard_map/ppermute | solution.py:352
  129.2 7.6 %attend.7 = bf16[16,4,64,384]{3,2,1,0:T(8,128)(2,1)} custom-call(s32[1]{0:T(128)} %bitcast.tm_ref, bf16[16,32,384]{2,1,0:T(8,128)(2,1)S(1)} %copy-done.17, bf16[16,96,384]{2,1,0:T(8,128)(2,1)} %copy-done.5, bf16[32,32,384]{2,1,0:T(8,128)(2,1)S(1)} %constant_dynamic-update-slice_fusion.own_lo, ...), custom_call_target="tpu_custom_call", output_to_operand_aliasing={{}: (14, {})} | custom-call | flops 1000 | bytes 1000 | tf_op jit(solution)/shard_map/attend/pallas_call | solution.py:328
  (51 shorter events, 10.0 us)
Async XLA Ops:
  0.0 2.3 %copy-start = (bf16[8,384]{1,0:T(8,128)(2,1)S(1)}, bf16[8,384]{1,0:T(8,128)(2,1)}, u32[]{:S(2)}) copy-start(bf16[8,384]{1,0:T(8,128)(2,1)} %param.15) | copy-start | bytes 18436
  3.1 1.1 copy-start.12
  7.9 10.8 %copy-start.10 = (f32[16,32,384]{2,1,0:T(8,128)}, f32[16,32,384]{2,1,0:T(8,128)S(1)}, u32[]{:S(2)}) copy-start(f32[16,32,384]{2,1,0:T(8,128)S(1)} %get-tuple-element.43.m_lo) | copy-start | bytes 2359300
  7.9 12.7 %copy-start.14 = (bf16[16,32,384]{2,1,0:T(8,128)(2,1)}, bf16[16,32,384]{2,1,0:T(8,128)(2,1)S(1)}, u32[]{:S(2)}) copy-start(bf16[16,32,384]{2,1,0:T(8,128)(2,1)S(1)} %get-tuple-element.41.x_lo) | copy-start | bytes 1179652
  7.9 16.7 %copy-start.13 = (bf16[1024,384]{1,0:T(8,128)(2,1)S(1)}, bf16[1024,384]{1,0:T(8,128)(2,1)}, u32[]{:S(2)}) copy-start(bf16[1024,384]{1,0:T(8,128)(2,1)} %table.3) | copy-start | bytes 2359300
  7.9 6.4 %collective-permute-start = (bf16[4,64,384]{2,1,0:T(8,128)(2,1)S(1)}, bf16[4,64,384]{2,1,0:T(8,128)(2,1)S(1)}, u32[]{:S(2)}, u32[]{:S(2)}) collective-permute-start(bf16[4,64,384]{2,1,0:T(8,128)(2,1)S(1)} %get-tuple-element.26), channel_id=1, source_target_pairs={{0,1},{1,2},{2,3},{4,5},{5,6},{6,7},{8,9},{9,10},{10,11},{12,13},{... | collective-permute-start | bytes 589832 | tf_op jit(solution)/shard_map/ppermute | solution.py:371
  11.7 7.0 %collective-permute-start.1 = (bf16[4,64,384]{2,1,0:T(8,128)(2,1)S(1)}, bf16[4,64,384]{2,1,0:T(8,128)(2,1)S(1)}, u32[]{:S(2)}, u32[]{:S(2)}) collective-permute-start(bf16[4,64,384]{2,1,0:T(8,128)(2,1)S(1)} %get-tuple-element.27), channel_id=1, source_target_pairs={{1,0},{2,1},{3,2},{5,4},{6,5},{7,6},{9,8},{10,9},{11,10},{13,12},{... | collective-permute-start | bytes 589832 | tf_op jit(solution)/shard_map/ppermute | solution.py:371
  19.8 0.7 copy-start.16
  20.5 0.9 copy-start.8
  21.4 18.9 %collective-permute-start.4 = (bf16[32,32,384]{2,1,0:T(8,128)(2,1)S(1)}, bf16[32,32,384]{2,1,0:T(8,128)(2,1)S(1)}, u32[]{:S(2)}, u32[]{:S(2)}) collective-permute-start(bf16[32,32,384]{2,1,0:T(8,128)(2,1)S(1)} %constant_dynamic-update-slice_fusion.own_lo), channel_id=1, source_target_pairs={{0,4},{4,8},{8,12},{12,16},{16,20},{20,24},{24,28},{1,5},{5,9},{9,... | collective-permute-start | bytes 2359304 | tf_op jit(solution)/shard_map/ppermute | solution.py:352
  34.3 1.0 copy-start.4
  35.3 13.8 %copy-start.1 = (bf16[16,96,384]{2,1,0:T(8,128)(2,1)}, bf16[16,96,384]{2,1,0:T(8,128)(2,1)S(1)}, u32[]{:S(2)}) copy-start(bf16[16,96,384]{2,1,0:T(8,128)(2,1)S(1)} %get-tuple-element.36.own_hi) | copy-start | bytes 3538948
  41.3 10.1 %collective-permute-start.7 = (bf16[32,32,384]{2,1,0:T(8,128)(2,1)}, bf16[32,32,384]{2,1,0:T(8,128)(2,1)}, u32[]{:S(2)}, u32[]{:S(2)}) collective-permute-start(bf16[32,32,384]{2,1,0:T(8,128)(2,1)} %broadcast_select_fusion), channel_id=1, source_target_pairs={{0,16},{4,20},{1,17},{5,21},{2,18},{6,22},{3,19},{7,23}} | collective-permute-start | bytes 2359304 | tf_op jit(solution)/shard_map/ppermute | solution.py:361
  42.8 15.8 %collective-permute-start.2 = (bf16[12,64,384]{2,1,0:T(8,128)(2,1)}, bf16[12,64,384]{2,1,0:T(8,128)(2,1)}, u32[]{:S(2)}, u32[]{:S(2)}) collective-permute-start(bf16[12,64,384]{2,1,0:T(8,128)(2,1)} %get-tuple-element.30), channel_id=1, source_target_pairs={{0,1},{1,2},{2,3},{4,5},{5,6},{6,7},{8,9},{9,10},{10,11},{12,13},{... | collective-permute-start | bytes 1769480 | tf_op jit(solution)/shard_map/ppermute | solution.py:371
  44.8 13.9 %collective-permute-start.3 = (bf16[12,64,384]{2,1,0:T(8,128)(2,1)}, bf16[12,64,384]{2,1,0:T(8,128)(2,1)}, u32[]{:S(2)}, u32[]{:S(2)}) collective-permute-start(bf16[12,64,384]{2,1,0:T(8,128)(2,1)} %get-tuple-element.31), channel_id=1, source_target_pairs={{1,0},{2,1},{3,2},{5,4},{6,5},{7,6},{9,8},{10,9},{11,10},{13,12},{... | collective-permute-start | bytes 1769480 | tf_op jit(solution)/shard_map/ppermute | solution.py:371
  49.1 27.3 %collective-permute-start.5 = (bf16[8,96,384]{2,1,0:T(8,128)(2,1)}, bf16[8,96,384]{2,1,0:T(8,128)(2,1)S(1)}, u32[]{:S(2)}, u32[]{:S(2)}) collective-permute-start(bf16[8,96,384]{2,1,0:T(8,128)(2,1)} %get-tuple-element.46), channel_id=1, source_target_pairs={{0,4},{4,8},{8,12},{12,16},{16,20},{20,24},{24,28},{1,5},{5,9},{9,... | collective-permute-start | bytes 1769480 | tf_op jit(solution)/shard_map/ppermute | solution.py:352
  53.6 34.9 %collective-permute-start.8 = (bf16[32,32,384]{2,1,0:T(8,128)(2,1)}, bf16[32,32,384]{2,1,0:T(8,128)(2,1)}, u32[]{:S(2)}, u32[]{:S(2)}) collective-permute-start(bf16[32,32,384]{2,1,0:T(8,128)(2,1)} %broadcast_select_fusion.1), channel_id=1, source_target_pairs={{0,8},{4,12},{16,24},{20,28},{1,9},{5,13},{17,25},{21,29},{2,10},{... | collective-permute-start | bytes 2359304 | tf_op jit(solution)/shard_map/ppermute | solution.py:361
  54.8 51.5 %collective-permute-start.10 = (bf16[8,96,384]{2,1,0:T(8,128)(2,1)}, bf16[8,96,384]{2,1,0:T(8,128)(2,1)}, u32[]{:S(2)}, u32[]{:S(2)}) collective-permute-start(bf16[8,96,384]{2,1,0:T(8,128)(2,1)} %get-tuple-element.45), channel_id=1, source_target_pairs={{0,4},{4,8},{8,12},{12,16},{16,20},{20,24},{24,28},{1,5},{5,9},{9,... | collective-permute-start | bytes 1769480 | tf_op jit(solution)/shard_map/ppermute | solution.py:352
  64.1 1.4 %copy-start.3 = (f32[16,96,384]{2,1,0:T(8,128)}, f32[16,96,384]{2,1,0:T(8,128)S(1)}, u32[]{:S(2)}) copy-start(f32[16,96,384]{2,1,0:T(8,128)S(1)} %get-tuple-element.40.m_hi) | copy-start | bytes 7077892
  65.5 1.1 copy-start.5
  66.6 23.2 %copy-start.2 = (bf16[16,96,384]{2,1,0:T(8,128)(2,1)}, bf16[16,96,384]{2,1,0:T(8,128)(2,1)S(1)}, u32[]{:S(2)}) copy-start(bf16[16,96,384]{2,1,0:T(8,128)(2,1)S(1)} %get-tuple-element.38.own_hi) | copy-start | bytes 3538948
  76.5 9.6 %copy-start.18 = (bf16[8,96,384]{2,1,0:T(8,128)(2,1)}, bf16[8,96,384]{2,1,0:T(8,128)(2,1)S(1)}, u32[]{:S(2)}) copy-start(bf16[8,96,384]{2,1,0:T(8,128)(2,1)S(1)} %collective-permute-done.5.hi) | copy-start | bytes 1769476
  77.7 41.3 %collective-permute-start.9 = (bf16[8,96,384]{2,1,0:T(8,128)(2,1)}, bf16[8,96,384]{2,1,0:T(8,128)(2,1)}, u32[]{:S(2)}, u32[]{:S(2)}) collective-permute-start(bf16[8,96,384]{2,1,0:T(8,128)(2,1)} %get-tuple-element.47), channel_id=1, source_target_pairs={{0,4},{4,8},{8,12},{12,16},{16,20},{20,24},{24,28},{1,5},{5,9},{9,... | collective-permute-start | bytes 1769480 | tf_op jit(solution)/shard_map/ppermute | solution.py:352
  81.6 47.6 %collective-permute-start.6 = (bf16[8,96,384]{2,1,0:T(8,128)(2,1)}, bf16[8,96,384]{2,1,0:T(8,128)(2,1)}, u32[]{:S(2)}, u32[]{:S(2)}) collective-permute-start(bf16[8,96,384]{2,1,0:T(8,128)(2,1)} %get-tuple-element.48), channel_id=1, source_target_pairs={{0,4},{4,8},{8,12},{12,16},{16,20},{20,24},{24,28},{1,5},{5,9},{9,... | collective-permute-start | bytes 1769480 | tf_op jit(solution)/shard_map/ppermute | solution.py:352
  88.4 1.5 %copy-start.6 = (bf16[384,384]{1,0:T(8,128)(2,1)S(1)}, bf16[384,384]{1,0:T(8,128)(2,1)}, u32[]{:S(2)}) copy-start(bf16[384,384]{1,0:T(8,128)(2,1)} %wk.7) | copy-start | bytes 884740
  88.4 1.5 %copy-start.7 = (bf16[384,384]{1,0:T(8,128)(2,1)S(1)}, bf16[384,384]{1,0:T(8,128)(2,1)}, u32[]{:S(2)}) copy-start(bf16[384,384]{1,0:T(8,128)(2,1)} %w_out.7) | copy-start | bytes 884740
  88.4 1.5 %copy-start.11 = (f32[16,32,384]{2,1,0:T(8,128)S(1)}, f32[16,32,384]{2,1,0:T(8,128)}, u32[]{:S(2)}) copy-start(f32[16,32,384]{2,1,0:T(8,128)} %copy-done.10) | copy-start | bytes 2359300
  88.5 1.6 %copy-start.15 = (bf16[16,32,384]{2,1,0:T(8,128)(2,1)S(1)}, bf16[16,32,384]{2,1,0:T(8,128)(2,1)}, u32[]{:S(2)}) copy-start(bf16[16,32,384]{2,1,0:T(8,128)(2,1)} %copy-done.14) | copy-start | bytes 1179652
  88.5 1.8 %copy-start.19 = (bf16[8,96,384]{2,1,0:T(8,128)(2,1)S(1)}, bf16[8,96,384]{2,1,0:T(8,128)(2,1)}, u32[]{:S(2)}) copy-start(bf16[8,96,384]{2,1,0:T(8,128)(2,1)} %copy-done.18) | copy-start | bytes 1769476
  97.8 21.3 %copy-start.9 = (f32[16,32,384]{2,1,0:T(8,128)S(1)}, f32[16,32,384]{2,1,0:T(8,128)}, u32[]{:S(2)}) copy-start(f32[16,32,384]{2,1,0:T(8,128)} %copy-done.8) | copy-start | bytes 2359300
  97.8 21.3 %copy-start.17 = (bf16[16,32,384]{2,1,0:T(8,128)(2,1)S(1)}, bf16[16,32,384]{2,1,0:T(8,128)(2,1)}, u32[]{:S(2)}) copy-start(bf16[16,32,384]{2,1,0:T(8,128)(2,1)} %copy-done.16) | copy-start | bytes 1179652

commit v4 on v3

--- a/solution.py
+++ b/solution.py
@@ -356,13 +356,15 @@
     count = lax.axis_size("tm")
     anchors = jnp.where(tm == 0, first, lo)
     by = count // 2
+    early = None
     while by >= 2:
         pairs = [(i, i + by) for i in range(count - by) if i % (2 * by) < 2]
         got = lax.ppermute(anchors, "tm", pairs)
+        early = got if early is None else early
         place = tm % (2 * by)
         anchors = jnp.where((place == by) | (place == by + 1), got, anchors)
         by //= 2
-    return anchors
+    return anchors, early
 
 
 def halo(top, bottom):
@@ -405,9 +407,10 @@
     first = jnp.concatenate([rolled_a, rolled_b], axis=0)
     lo = send(first, 1)
     emb, top, bottom, mixed_c, normed_c, rolled_c = embed(ANCHORS, shape[0] - ANCHORS, *shared)
-    lo, _ = lax.optimization_barrier((lo, rolled_c))
-    anchors = anchors_of(first, lo, tm)
-    hi = [send(rolled_c[r * row : (r + 1) * row], 1) for r in range(inner // row)]
+    hi = [send(rolled_c[:row], 1)]
+    lo, rest, _ = lax.optimization_barrier((lo, rolled_c, hi[0]))
+    hi += [send(rest[r * row : (r + 1) * row], 1) for r in range(1, inner // row)]
+    anchors, early = anchors_of(first, lo, tm)
     mixed_d, normed_d, rolled_d = edge(ANCHORS, emb, *halo(top, bottom), conv, gain)
 
     def blocks(x_lo, x_hi, own_hi, hi, m_lo, m_hi, start, at, hi_at):
@@ -434,7 +437,7 @@
             cols,
             lambda _, r=r: r + 1,
         )
-    to_send, _ = lax.optimization_barrier((rolled_d, hi[0]))
+    to_send, *_ = lax.optimization_barrier((rolled_d, early, *hi[1:]))
     later = [send(to_send[r * row : (r + 1) * row], 1) for r in range(2)]
     for r in range(2):
         out = attend(

time: 138 us -> 140 us (1.014)
  the two profiles are of different devices: /device:TPU:9 before, /device:TPU:13 now
where the time goes in v4:
time: 140 us; the launch traced here: 137 us
  Pallas kernels  50.2 us (36%)
  waiting for transfers between devices  37.2 us (27%)
  starting transfers between devices  31 us (22%)
  local copies, waits for them, and re-layouts  13.1 us (9%)
  other arithmetic  4.51 us (3%)
    pallas_call x4, Pallas kernels, attend(): pl.pallas_call(attend_kernel, grid=(positions // (STEP * GROUP),), in_spe...  30.5 us
    ppermute x5, waiting for transfers between devices, send(): return lax.ppermute(x, 'tm', [(i, i + by) for i in range(count - by)])  23.5 us
    ppermute x5, starting transfers between devices, send(): return lax.ppermute(x, 'tm', [(i, i + by) for i in range(count - by)])  17.4 us
    pallas_call x2, Pallas kernels, embed(): pl.pallas_call(functools.partial(embed_kernel, first), grid=(count // 2,)...  13.3 us
    ppermute x2, waiting for transfers between devices, anchors_of(): got = lax.ppermute(anchors, 'tm', pairs)  8.27 us
    unnamed x45, local copies, waits for them, and re-layouts  7.79 us
    pallas_call x2, Pallas kernels, edge(): pl.pallas_call(functools.partial(edge_kernel, first), grid=(count // 2,),...  6.48 us
    ppermute x2, starting transfers between devices, halo(): lax.ppermute(bottom, 'space', up)  5.72 us
  transfers between devices with their start and end apart: 11, of which 6 were waited for; matrix products, arithmetic and copies ran while one was open for 6% of the time, Pallas kernels for 28%

profile of v4, /device:TPU:13, one launch (start us, length us, event | category | flops | bytes accessed | tf_op | source)
XLA Modules:
  0.0 137.3 jit_solution(6794632100309833883)
XLA Ops:
  3.1 1.1 copy-done.12
  4.3 3.6 %embed.2 = (bf16[4,4,64,384]{3,2,1,0:T(8,128)(2,1)S(1)}, bf16[4,64,384]{2,1,0:T(8,128)(2,1)S(1)}, bf16[4,64,384]{2,1,0:T(8,128)(2,1)S(1)}, f32[16,32,384]{2,1,0:...) custom-call(s32[8,1,512]{2,1,0:T(1,128)S(1)} %reshape.14.ids, ...), custom_call_target="tpu_custom_call" | custom-call | flops 1000 | bytes 1000 | tf_op jit(solution)/shard_map/embed/pallas_call | solution.py:270
  7.9 3.8 %collective-permute-start = (bf16[4,64,384]{2,1,0:T(8,128)(2,1)S(1)}, bf16[4,64,384]{2,1,0:T(8,128)(2,1)S(1)}, u32[]{:S(2)}, u32[]{:S(2)}) collective-permute-start(bf16[4,64,384]{2,1,0:T(8,128)(2,1)S(1)} %get-tuple-element.27), channel_id=1, source_target_pairs={{0,1},{1,2},{2,3},{4,5},{5,6},{6,7},{8,9},{9,10},{10,11},{12,13},{... | collective-permute-start | bytes 589832 | tf_op jit(solution)/shard_map/ppermute | solution.py:373
  11.7 1.9 %collective-permute-start.1 = (bf16[4,64,384]{2,1,0:T(8,128)(2,1)S(1)}, bf16[4,64,384]{2,1,0:T(8,128)(2,1)S(1)}, u32[]{:S(2)}, u32[]{:S(2)}) collective-permute-start(bf16[4,64,384]{2,1,0:T(8,128)(2,1)S(1)} %get-tuple-element.28), channel_id=1, source_target_pairs={{1,0},{2,1},{3,2},{5,4},{6,5},{7,6},{9,8},{10,9},{11,10},{13,12},{... | collective-permute-start | bytes 589832 | tf_op jit(solution)/shard_map/ppermute | solution.py:373
  14.3 4.4 %collective-permute-done.1.after = bf16[4,64,384]{2,1,0:T(8,128)(2,1)S(1)} collective-permute-done((bf16[4,64,384]{2,1,0:T(8,128)(2,1)S(1)}, bf16[4,64,384]{2,1,0:T(8,128)(2,1)S(1)}, u32[]{:S(2)}, u32[]{:S(2)}) %collective-permute-start.1) | collective-permute-done | bytes 196640 | tf_op jit(solution)/shard_map/ppermute | solution.py:373
  18.7 1.1 edge.2
  21.4 3.1 %collective-permute-start.4 = (bf16[32,32,384]{2,1,0:T(8,128)(2,1)S(1)}, bf16[32,32,384]{2,1,0:T(8,128)(2,1)S(1)}, u32[]{:S(2)}, u32[]{:S(2)}) collective-permute-start(bf16[32,32,384]{2,1,0:T(8,128)(2,1)S(1)} %constant_dynamic-update-slice_fusion.own_lo), channel_id=1, source_target_pairs={{0,4},{4,8},{8,12},{12,16},{16,20},{20,24},{24,28},{1,5},{5,9},{9,... | collective-permute-start | bytes 2359304 | tf_op jit(solution)/shard_map/ppermute | solution.py:352
  24.6 9.7 %embed.3 = (bf16[12,4,64,384]{3,2,1,0:T(8,128)(2,1)}, bf16[12,64,384]{2,1,0:T(8,128)(2,1)}, bf16[12,64,384]{2,1,0:T(8,128)(2,1)}, f32[16,96,384]{2,1,0:T(8,128)}...) custom-call(s32[8,1,512]{2,1,0:T(1,128)S(1)} %reshape.14.ids, bf16[16,4,64,384]{3,2,1,0:T(8,128)(2,1)} %frames.3, ...), custom_call_target="tpu_custom_call" | custom-call | flops 1000 | bytes 1000 | tf_op jit(solution)/shard_map/embed/pallas_call | solution.py:270
  34.3 1.0 copy-done.4
  36.3 3.1 %collective-permute-start.5 = (bf16[8,96,384]{2,1,0:T(8,128)(2,1)}, bf16[8,96,384]{2,1,0:T(8,128)(2,1)S(1)}, u32[]{:S(2)}, u32[]{:S(2)}) collective-permute-start(bf16[8,96,384]{2,1,0:T(8,128)(2,1)} %slice.12), channel_id=1, source_target_pairs={{0,4},{4,8},{8,12},{12,16},{16,20},{20,24},{24,28},{1,5},{5,9},{9,... | collective-permute-start | bytes 1769480 | tf_op jit(solution)/shard_map/ppermute | solution.py:352
  39.4 12.6 %collective-permute-done.5.hi = bf16[8,96,384]{2,1,0:T(8,128)(2,1)S(1)} collective-permute-done((bf16[8,96,384]{2,1,0:T(8,128)(2,1)}, bf16[8,96,384]{2,1,0:T(8,128)(2,1)S(1)}, u32[]{:S(2)}, u32[]{:S(2)}) %collective-permute-start.5) | collective-permute-done | bytes 589856 | tf_op jit(solution)/shard_map/ppermute | solution.py:352
  52.0 1.1 broadcast_select_fusion.2
  53.2 1.5 %collective-permute-start.6 = (bf16[32,32,384]{2,1,0:T(8,128)(2,1)}, bf16[32,32,384]{2,1,0:T(8,128)(2,1)}, u32[]{:S(2)}, u32[]{:S(2)}) collective-permute-start(bf16[32,32,384]{2,1,0:T(8,128)(2,1)} %broadcast_select_fusion.2), channel_id=1, source_target_pairs={{0,16},{4,20},{1,17},{5,21},{2,18},{6,22},{3,19},{7,23}} | collective-permute-start | bytes 2359304 | tf_op jit(solution)/shard_map/ppermute | solution.py:362
  54.7 1.9 %collective-permute-start.2 = (bf16[12,64,384]{2,1,0:T(8,128)(2,1)}, bf16[12,64,384]{2,1,0:T(8,128)(2,1)}, u32[]{:S(2)}, u32[]{:S(2)}) collective-permute-start(bf16[12,64,384]{2,1,0:T(8,128)(2,1)} %get-tuple-element.31), channel_id=1, source_target_pairs={{0,1},{1,2},{2,3},{4,5},{5,6},{6,7},{8,9},{9,10},{10,11},{12,13},{... | collective-permute-start | bytes 1769480 | tf_op jit(solution)/shard_map/ppermute | solution.py:373
  56.6 3.2 %collective-permute-start.3 = (bf16[12,64,384]{2,1,0:T(8,128)(2,1)}, bf16[12,64,384]{2,1,0:T(8,128)(2,1)}, u32[]{:S(2)}, u32[]{:S(2)}) collective-permute-start(bf16[12,64,384]{2,1,0:T(8,128)(2,1)} %get-tuple-element.32), channel_id=1, source_target_pairs={{1,0},{2,1},{3,2},{5,4},{6,5},{7,6},{9,8},{10,9},{11,10},{13,12},{... | collective-permute-start | bytes 1769480 | tf_op jit(solution)/shard_map/ppermute | solution.py:373
  60.7 3.8 %collective-permute-start.7 = (bf16[8,96,384]{2,1,0:T(8,128)(2,1)}, bf16[8,96,384]{2,1,0:T(8,128)(2,1)}, u32[]{:S(2)}, u32[]{:S(2)}) collective-permute-start(bf16[8,96,384]{2,1,0:T(8,128)(2,1)} %slice.13), channel_id=1, source_target_pairs={{0,4},{4,8},{8,12},{12,16},{16,20},{20,24},{24,28},{1,5},{5,9},{9,... | collective-permute-start | bytes 1769480 | tf_op jit(solution)/shard_map/ppermute | solution.py:352
  64.6 2.1 %broadcast_select_fusion = bf16[32,32,384]{2,1,0:T(8,128)(2,1)} fusion(bf16[32,32,384]{2,1,0:T(8,128)(2,1)} %collective-permute-done.6, bf16[32,32,384]{2,1,0:T(8,128)(2,1)} %broadcast_select_fusion.2, pred[]{:T(512)S(6)} %or.7), kind=kLoop, calls=%fused_computation | loop fusion | flops 393216 | bytes 2359297 | tf_op jit(solution)/shard_map/jit(_where)/select_n | solution.py:365
  66.7 1.3 collective-permute-start.9
  68.5 5.4 %edge.3 = (f32[16,96,384]{2,1,0:T(8,128)S(1)}, bf16[16,96,384]{2,1,0:T(8,128)(2,1)S(1)}, bf16[16,96,384]{2,1,0:T(8,128)(2,1)S(1)}) custom-call(bf16[12,4,64,384]{3,2,1,0:T(8,128)(2,1)} %get-tuple-element.30.emb, bf16[12,64,384]{2,1,0:T(8,128)(2,1)} %collective-permute-done.2.before, bf16[12,64,384]{2,1,0:T(8,128)(2,1)} %collective-permute-done.3.after, ...), custom_call_target="tpu_custom_call" | custom-call | flops 1000 | bytes 1000 | tf_op jit(solution)/shard_map/edge/pallas_call | solution.py:299
  73.9 1.4 %copy-done.3 = f32[16,96,384]{2,1,0:T(8,128)} copy-done((f32[16,96,384]{2,1,0:T(8,128)}, f32[16,96,384]{2,1,0:T(8,128)S(1)}, u32[]{:S(2)}) %copy-start.3) | copy-done | bytes 2359320
  75.3 1.1 copy-done.5
  76.5 10.8 %collective-permute-done.7.hi = bf16[8,96,384]{2,1,0:T(8,128)(2,1)} collective-permute-done((bf16[8,96,384]{2,1,0:T(8,128)(2,1)}, bf16[8,96,384]{2,1,0:T(8,128)(2,1)}, u32[]{:S(2)}, u32[]{:S(2)}) %collective-permute-start.7) | collective-permute-done | bytes 589856 | tf_op jit(solution)/shard_map/ppermute | solution.py:352
  87.3 1.1 fusion.2
  88.4 5.0 %collective-permute-start.10 = (bf16[8,96,384]{2,1,0:T(8,128)(2,1)}, bf16[8,96,384]{2,1,0:T(8,128)(2,1)}, u32[]{:S(2)}, u32[]{:S(2)}) collective-permute-start(bf16[8,96,384]{2,1,0:T(8,128)(2,1)} %get-tuple-element.47), channel_id=1, source_target_pairs={{0,4},{4,8},{8,12},{12,16},{16,20},{20,24},{24,28},{1,5},{5,9},{9,... | collective-permute-start | bytes 1769480 | tf_op jit(solution)/shard_map/ppermute | solution.py:352
  93.4 2.3 %collective-permute-start.8 = (bf16[8,96,384]{2,1,0:T(8,128)(2,1)}, bf16[8,96,384]{2,1,0:T(8,128)(2,1)}, u32[]{:S(2)}, u32[]{:S(2)}) collective-permute-start(bf16[8,96,384]{2,1,0:T(8,128)(2,1)} %get-tuple-element.48), channel_id=1, source_target_pairs={{0,4},{4,8},{8,12},{12,16},{16,20},{20,24},{24,28},{1,5},{5,9},{9,... | collective-permute-start | bytes 1769480 | tf_op jit(solution)/shard_map/ppermute | solution.py:352
  96.0 1.2 copy.16
  97.2 8.3 %collective-permute-done.9 = bf16[32,32,384]{2,1,0:T(8,128)(2,1)} collective-permute-done((bf16[32,32,384]{2,1,0:T(8,128)(2,1)}, bf16[32,32,384]{2,1,0:T(8,128)(2,1)}, u32[]{:S(2)}, u32[]{:S(2)}) %collective-permute-start.9) | collective-permute-done | bytes 786464 | tf_op jit(solution)/shard_map/ppermute | solution.py:362
  105.5 1.2 broadcast_select_fusion.1.anchors
  106.8 7.5 %attend.4.rest_0_ = bf16[16,4,64,384]{3,2,1,0:T(8,128)(2,1)} custom-call(s32[1]{0:T(128)} %bitcast.tm_ref, bf16[16,32,384]{2,1,0:T(8,128)(2,1)S(1)} %copy-done.15, bf16[16,96,384]{2,1,0:T(8,128)(2,1)} %copy-done.4, bf16[32,32,384]{2,1,0:T(8,128)(2,1)S(1)} %constant_dynamic-update-slice_fusion.own_lo, bf16[16,96,384]{2,1,0:T(8,128)(2,1)} %copy-done.1, ...), custom_call_target="tpu_custom_call" | custom-call | flops 1000 | bytes 1000 | tf_op jit(solution)/shard_map/attend/pallas_call | solution.py:328
  114.3 7.7 %attend.5.rest_0_ = bf16[16,4,64,384]{3,2,1,0:T(8,128)(2,1)} custom-call(s32[1]{0:T(128)} %bitcast.tm_ref, bf16[16,32,384]{2,1,0:T(8,128)(2,1)S(1)} %copy-done.15, bf16[16,96,384]{2,1,0:T(8,128)(2,1)} %copy-done.4, bf16[32,32,384]{2,1,0:T(8,128)(2,1)S(1)} %constant_dynamic-update-slice_fusion.own_lo, ...), custom_call_target="tpu_custom_call", output_to_operand_aliasing={{}: (14, {})} | custom-call | flops 1000 | bytes 1000 | tf_op jit(solution)/shard_map/attend/pallas_call | solution.py:328
  122.1 7.6 %attend.6.rest_0_ = bf16[16,4,64,384]{3,2,1,0:T(8,128)(2,1)} custom-call(s32[1]{0:T(128)} %bitcast.tm_ref, bf16[16,32,384]{2,1,0:T(8,128)(2,1)S(1)} %copy-done.17, bf16[16,96,384]{2,1,0:T(8,128)(2,1)} %copy-done.5, bf16[32,32,384]{2,1,0:T(8,128)(2,1)S(1)} %constant_dynamic-update-slice_fusion.own_lo, ...), custom_call_target="tpu_custom_call", output_to_operand_aliasing={{}: (14, {})} | custom-call | flops 1000 | bytes 1000 | tf_op jit(solution)/shard_map/attend/pallas_call | solution.py:328
  129.7 7.6 %attend.7 = bf16[16,4,64,384]{3,2,1,0:T(8,128)(2,1)} custom-call(s32[1]{0:T(128)} %bitcast.tm_ref, bf16[16,32,384]{2,1,0:T(8,128)(2,1)S(1)} %copy-done.17, bf16[16,96,384]{2,1,0:T(8,128)(2,1)} %copy-done.5, bf16[32,32,384]{2,1,0:T(8,128)(2,1)S(1)} %constant_dynamic-update-slice_fusion.own_lo, ...), custom_call_target="tpu_custom_call", output_to_operand_aliasing={{}: (14, {})} | custom-call | flops 1000 | bytes 1000 | tf_op jit(solution)/shard_map/attend/pallas_call | solution.py:328
  (54 shorter events, 8.0 us)
Async XLA Ops:
  0.0 2.3 %copy-start = (bf16[8,384]{1,0:T(8,128)(2,1)S(1)}, bf16[8,384]{1,0:T(8,128)(2,1)}, u32[]{:S(2)}) copy-start(bf16[8,384]{1,0:T(8,128)(2,1)} %param.15) | copy-start | bytes 18436
  3.1 1.1 copy-start.12
  7.9 10.8 %copy-start.10 = (f32[16,32,384]{2,1,0:T(8,128)}, f32[16,32,384]{2,1,0:T(8,128)S(1)}, u32[]{:S(2)}) copy-start(f32[16,32,384]{2,1,0:T(8,128)S(1)} %get-tuple-element.45.m_lo) | copy-start | bytes 2359300
  7.9 12.7 %copy-start.14 = (bf16[16,32,384]{2,1,0:T(8,128)(2,1)}, bf16[16,32,384]{2,1,0:T(8,128)(2,1)S(1)}, u32[]{:S(2)}) copy-start(bf16[16,32,384]{2,1,0:T(8,128)(2,1)S(1)} %get-tuple-element.43.x_lo) | copy-start | bytes 1179652
  7.9 16.7 %copy-start.13 = (bf16[1024,384]{1,0:T(8,128)(2,1)S(1)}, bf16[1024,384]{1,0:T(8,128)(2,1)}, u32[]{:S(2)}) copy-start(bf16[1024,384]{1,0:T(8,128)(2,1)} %table.3) | copy-start | bytes 2359300
  7.9 6.4 %collective-permute-start = (bf16[4,64,384]{2,1,0:T(8,128)(2,1)S(1)}, bf16[4,64,384]{2,1,0:T(8,128)(2,1)S(1)}, u32[]{:S(2)}, u32[]{:S(2)}) collective-permute-start(bf16[4,64,384]{2,1,0:T(8,128)(2,1)S(1)} %get-tuple-element.27), channel_id=1, source_target_pairs={{0,1},{1,2},{2,3},{4,5},{5,6},{6,7},{8,9},{9,10},{10,11},{12,13},{... | collective-permute-start | bytes 589832 | tf_op jit(solution)/shard_map/ppermute | solution.py:373
  11.7 7.0 %collective-permute-start.1 = (bf16[4,64,384]{2,1,0:T(8,128)(2,1)S(1)}, bf16[4,64,384]{2,1,0:T(8,128)(2,1)S(1)}, u32[]{:S(2)}, u32[]{:S(2)}) collective-permute-start(bf16[4,64,384]{2,1,0:T(8,128)(2,1)S(1)} %get-tuple-element.28), channel_id=1, source_target_pairs={{1,0},{2,1},{3,2},{5,4},{6,5},{7,6},{9,8},{10,9},{11,10},{13,12},{... | collective-permute-start | bytes 589832 | tf_op jit(solution)/shard_map/ppermute | solution.py:373
  19.8 0.7 copy-start.16
  20.5 0.9 copy-start.8
  21.4 30.6 %collective-permute-start.4 = (bf16[32,32,384]{2,1,0:T(8,128)(2,1)S(1)}, bf16[32,32,384]{2,1,0:T(8,128)(2,1)S(1)}, u32[]{:S(2)}, u32[]{:S(2)}) collective-permute-start(bf16[32,32,384]{2,1,0:T(8,128)(2,1)S(1)} %constant_dynamic-update-slice_fusion.own_lo), channel_id=1, source_target_pairs={{0,4},{4,8},{8,12},{12,16},{16,20},{20,24},{24,28},{1,5},{5,9},{9,... | collective-permute-start | bytes 2359304 | tf_op jit(solution)/shard_map/ppermute | solution.py:352
  34.3 1.0 copy-start.4
  35.3 25.4 %copy-start.1 = (bf16[16,96,384]{2,1,0:T(8,128)(2,1)}, bf16[16,96,384]{2,1,0:T(8,128)(2,1)S(1)}, u32[]{:S(2)}) copy-start(bf16[16,96,384]{2,1,0:T(8,128)(2,1)S(1)} %get-tuple-element.39.own_hi) | copy-start | bytes 3538948
  36.3 15.8 %collective-permute-start.5 = (bf16[8,96,384]{2,1,0:T(8,128)(2,1)}, bf16[8,96,384]{2,1,0:T(8,128)(2,1)S(1)}, u32[]{:S(2)}, u32[]{:S(2)}) collective-permute-start(bf16[8,96,384]{2,1,0:T(8,128)(2,1)} %slice.12), channel_id=1, source_target_pairs={{0,4},{4,8},{8,12},{12,16},{16,20},{20,24},{24,28},{1,5},{5,9},{9,... | collective-permute-start | bytes 1769480 | tf_op jit(solution)/shard_map/ppermute | solution.py:352
  52.0 14.7 %copy-start.18 = (bf16[8,96,384]{2,1,0:T(8,128)(2,1)}, bf16[8,96,384]{2,1,0:T(8,128)(2,1)S(1)}, u32[]{:S(2)}) copy-start(bf16[8,96,384]{2,1,0:T(8,128)(2,1)S(1)} %collective-permute-done.5.hi) | copy-start | bytes 1769476
  53.2 11.4 %collective-permute-start.6 = (bf16[32,32,384]{2,1,0:T(8,128)(2,1)}, bf16[32,32,384]{2,1,0:T(8,128)(2,1)}, u32[]{:S(2)}, u32[]{:S(2)}) collective-permute-start(bf16[32,32,384]{2,1,0:T(8,128)(2,1)} %broadcast_select_fusion.2), channel_id=1, source_target_pairs={{0,16},{4,20},{1,17},{5,21},{2,18},{6,22},{3,19},{7,23}} | collective-permute-start | bytes 2359304 | tf_op jit(solution)/shard_map/ppermute | solution.py:362
  54.7 13.3 %collective-permute-start.2 = (bf16[12,64,384]{2,1,0:T(8,128)(2,1)}, bf16[12,64,384]{2,1,0:T(8,128)(2,1)}, u32[]{:S(2)}, u32[]{:S(2)}) collective-permute-start(bf16[12,64,384]{2,1,0:T(8,128)(2,1)} %get-tuple-element.31), channel_id=1, source_target_pairs={{0,1},{1,2},{2,3},{4,5},{5,6},{6,7},{8,9},{9,10},{10,11},{12,13},{... | collective-permute-start | bytes 1769480 | tf_op jit(solution)/shard_map/ppermute | solution.py:373
  56.6 11.8 %collective-permute-start.3 = (bf16[12,64,384]{2,1,0:T(8,128)(2,1)}, bf16[12,64,384]{2,1,0:T(8,128)(2,1)}, u32[]{:S(2)}, u32[]{:S(2)}) collective-permute-start(bf16[12,64,384]{2,1,0:T(8,128)(2,1)} %get-tuple-element.32), channel_id=1, source_target_pairs={{1,0},{2,1},{3,2},{5,4},{6,5},{7,6},{9,8},{10,9},{11,10},{13,12},{... | collective-permute-start | bytes 1769480 | tf_op jit(solution)/shard_map/ppermute | solution.py:373
  60.7 26.6 %collective-permute-start.7 = (bf16[8,96,384]{2,1,0:T(8,128)(2,1)}, bf16[8,96,384]{2,1,0:T(8,128)(2,1)}, u32[]{:S(2)}, u32[]{:S(2)}) collective-permute-start(bf16[8,96,384]{2,1,0:T(8,128)(2,1)} %slice.13), channel_id=1, source_target_pairs={{0,4},{4,8},{8,12},{12,16},{16,20},{20,24},{24,28},{1,5},{5,9},{9,... | collective-permute-start | bytes 1769480 | tf_op jit(solution)/shard_map/ppermute | solution.py:352
  66.7 38.8 %collective-permute-start.9 = (bf16[32,32,384]{2,1,0:T(8,128)(2,1)}, bf16[32,32,384]{2,1,0:T(8,128)(2,1)}, u32[]{:S(2)}, u32[]{:S(2)}) collective-permute-start(bf16[32,32,384]{2,1,0:T(8,128)(2,1)} %broadcast_select_fusion), channel_id=1, source_target_pairs={{0,8},{4,12},{16,24},{20,28},{1,9},{5,13},{17,25},{21,29},{2,10},{... | collective-permute-start | bytes 2359304 | tf_op jit(solution)/shard_map/ppermute | solution.py:362
  68.5 27.3 %copy-start.20 = (bf16[384,384]{1,0:T(8,128)(2,1)S(1)}, bf16[384,384]{1,0:T(8,128)(2,1)}, u32[]{:S(2)}) copy-start(bf16[384,384]{1,0:T(8,128)(2,1)} %param.18) | copy-start | bytes 884740
  73.9 1.4 %copy-start.3 = (f32[16,96,384]{2,1,0:T(8,128)}, f32[16,96,384]{2,1,0:T(8,128)S(1)}, u32[]{:S(2)}) copy-start(f32[16,96,384]{2,1,0:T(8,128)S(1)} %get-tuple-element.42.m_hi) | copy-start | bytes 7077892
  75.3 1.1 copy-start.5
  76.5 30.3 %copy-start.2 = (bf16[16,96,384]{2,1,0:T(8,128)(2,1)}, bf16[16,96,384]{2,1,0:T(8,128)(2,1)S(1)}, u32[]{:S(2)}) copy-start(bf16[16,96,384]{2,1,0:T(8,128)(2,1)S(1)} %get-tuple-element.40.own_hi) | copy-start | bytes 3538948
  88.4 33.6 %collective-permute-start.10 = (bf16[8,96,384]{2,1,0:T(8,128)(2,1)}, bf16[8,96,384]{2,1,0:T(8,128)(2,1)}, u32[]{:S(2)}, u32[]{:S(2)}) collective-permute-start(bf16[8,96,384]{2,1,0:T(8,128)(2,1)} %get-tuple-element.47), channel_id=1, source_target_pairs={{0,4},{4,8},{8,12},{12,16},{16,20},{20,24},{24,28},{1,5},{5,9},{9,... | collective-permute-start | bytes 1769480 | tf_op jit(solution)/shard_map/ppermute | solution.py:352
  93.4 36.3 %collective-permute-start.8 = (bf16[8,96,384]{2,1,0:T(8,128)(2,1)}, bf16[8,96,384]{2,1,0:T(8,128)(2,1)}, u32[]{:S(2)}, u32[]{:S(2)}) collective-permute-start(bf16[8,96,384]{2,1,0:T(8,128)(2,1)} %get-tuple-element.48), channel_id=1, source_target_pairs={{0,4},{4,8},{8,12},{12,16},{16,20},{20,24},{24,28},{1,5},{5,9},{9,... | collective-permute-start | bytes 1769480 | tf_op jit(solution)/shard_map/ppermute | solution.py:352
  97.2 9.6 %copy-start.6 = (bf16[384,384]{1,0:T(8,128)(2,1)S(1)}, bf16[384,384]{1,0:T(8,128)(2,1)}, u32[]{:S(2)}) copy-start(bf16[384,384]{1,0:T(8,128)(2,1)} %wk.7) | copy-start | bytes 884740
  97.2 9.6 %copy-start.7 = (bf16[384,384]{1,0:T(8,128)(2,1)S(1)}, bf16[384,384]{1,0:T(8,128)(2,1)}, u32[]{:S(2)}) copy-start(bf16[384,384]{1,0:T(8,128)(2,1)} %w_out.7) | copy-start | bytes 884740
  97.2 9.6 %copy-start.11 = (f32[16,32,384]{2,1,0:T(8,128)S(1)}, f32[16,32,384]{2,1,0:T(8,128)}, u32[]{:S(2)}) copy-start(f32[16,32,384]{2,1,0:T(8,128)} %copy-done.10) | copy-start | bytes 2359300
  97.2 9.6 %copy-start.15 = (bf16[16,32,384]{2,1,0:T(8,128)(2,1)S(1)}, bf16[16,32,384]{2,1,0:T(8,128)(2,1)}, u32[]{:S(2)}) copy-start(bf16[16,32,384]{2,1,0:T(8,128)(2,1)} %copy-done.14) | copy-start | bytes 1179652
  97.2 9.6 %copy-start.19 = (bf16[8,96,384]{2,1,0:T(8,128)(2,1)S(1)}, bf16[8,96,384]{2,1,0:T(8,128)(2,1)}, u32[]{:S(2)}) copy-start(bf16[8,96,384]{2,1,0:T(8,128)(2,1)} %copy-done.18) | copy-start | bytes 1769476
  114.3 7.7 %copy-start.9 = (f32[16,32,384]{2,1,0:T(8,128)S(1)}, f32[16,32,384]{2,1,0:T(8,128)}, u32[]{:S(2)}) copy-start(f32[16,32,384]{2,1,0:T(8,128)} %copy-done.8) | copy-start | bytes 2359300
  114.3 7.7 %copy-start.17 = (bf16[16,32,384]{2,1,0:T(8,128)(2,1)S(1)}, bf16[16,32,384]{2,1,0:T(8,128)(2,1)}, u32[]{:S(2)}) copy-start(bf16[16,32,384]{2,1,0:T(8,128)(2,1)} %copy-done.16) | copy-start | bytes 1179652

commit v5 on v3

--- a/solution.py
+++ b/solution.py
@@ -408,6 +408,7 @@
     lo, _ = lax.optimization_barrier((lo, rolled_c))
     anchors = anchors_of(first, lo, tm)
     hi = [send(rolled_c[r * row : (r + 1) * row], 1) for r in range(inner // row)]
+    top, bottom, _ = lax.optimization_barrier((top, bottom, hi[0]))
     mixed_d, normed_d, rolled_d = edge(ANCHORS, emb, *halo(top, bottom), conv, gain)
 
     def blocks(x_lo, x_hi, own_hi, hi, m_lo, m_hi, start, at, hi_at):

time: 138 us -> 148 us (1.072)
  waiting for transfers between devices: 36.1 us -> 50.7 us
  starting transfers between devices: 31.2 us -> 26.3 us
    ppermute x5, waiting for transfers between devices: 31.1 us -> 41.8 us  [send(): return lax.ppermute(x, 'tm', [(i, i + by) for i in range(count - by)])]
    ppermute x5, starting transfers between devices: 17.5 us -> 13.4 us  [send(): return lax.ppermute(x, 'tm', [(i, i + by) for i in range(count - by)])]
    ppermute x2, waiting for transfers between devices: 4.4 us -> 8.34 us  [halo(): lax.ppermute(top, 'space', [(j, i) for i, j in up])]
    unnamed x43 -> x49, local copies, waits for them, and re-layouts: 9.08 us -> 10 us
  transfers between devices with their start and end apart: 11 -> 11, of which waited for: 7 -> 7; matrix products, arithmetic and copies ran while one was open for 6% -> 5% of each run, Pallas kernels for 28% -> 26%
where the time goes in v5:
time: 148 us; the launch traced here: 147 us
  waiting for transfers between devices  50.7 us (34%)
  Pallas kernels  49.9 us (34%)
  starting transfers between devices  26.3 us (18%)
  local copies, waits for them, and re-layouts  14.5 us (10%)
  other arithmetic  4.57 us (3%)
    ppermute x5, waiting for transfers between devices, send(): return lax.ppermute(x, 'tm', [(i, i + by) for i in range(count - by)])  41.8 us
    pallas_call x4, Pallas kernels, attend(): pl.pallas_call(attend_kernel, grid=(positions // (STEP * GROUP),), in_spe...  30.4 us
    ppermute x5, starting transfers between devices, send(): return lax.ppermute(x, 'tm', [(i, i + by) for i in range(count - by)])  13.4 us
    pallas_call x2, Pallas kernels, embed(): pl.pallas_call(functools.partial(embed_kernel, first), grid=(count // 2,)...  13.3 us
    unnamed x49, local copies, waits for them, and re-layouts  10 us
    ppermute x2, waiting for transfers between devices, halo(): lax.ppermute(top, 'space', [(j, i) for i, j in up])  8.34 us
    pallas_call x2, Pallas kernels, edge(): pl.pallas_call(functools.partial(edge_kernel, first), grid=(count // 2,),...  6.2 us
    ppermute x2, starting transfers between devices, halo(): lax.ppermute(bottom, 'space', up)  5.72 us
  transfers between devices with their start and end apart: 11, of which 7 were waited for; matrix products, arithmetic and copies ran while one was open for 5% of the time, Pallas kernels for 26%

profile of v5, /device:TPU:9, one launch (start us, length us, event | category | flops | bytes accessed | tf_op | source)
XLA Modules:
  0.0 147.2 jit_solution(8341339922000264735)
XLA Ops:
  3.1 1.1 copy-done.12
  4.3 3.6 %embed.2 = (bf16[4,4,64,384]{3,2,1,0:T(8,128)(2,1)S(1)}, bf16[4,64,384]{2,1,0:T(8,128)(2,1)S(1)}, bf16[4,64,384]{2,1,0:T(8,128)(2,1)S(1)}, f32[16,32,384]{2,1,0:...) custom-call(s32[8,1,512]{2,1,0:T(1,128)S(1)} %reshape.14.ids, ...), custom_call_target="tpu_custom_call" | custom-call | flops 1000 | bytes 1000 | tf_op jit(solution)/shard_map/embed/pallas_call | solution.py:270
  7.9 3.8 %collective-permute-start = (bf16[4,64,384]{2,1,0:T(8,128)(2,1)S(1)}, bf16[4,64,384]{2,1,0:T(8,128)(2,1)S(1)}, u32[]{:S(2)}, u32[]{:S(2)}) collective-permute-start(bf16[4,64,384]{2,1,0:T(8,128)(2,1)S(1)} %get-tuple-element.28), channel_id=1, source_target_pairs={{0,1},{1,2},{2,3},{4,5},{5,6},{6,7},{8,9},{9,10},{10,11},{12,13},{... | collective-permute-start | bytes 589832 | tf_op jit(solution)/shard_map/ppermute | solution.py:371
  11.7 1.9 %collective-permute-start.1 = (bf16[4,64,384]{2,1,0:T(8,128)(2,1)S(1)}, bf16[4,64,384]{2,1,0:T(8,128)(2,1)S(1)}, u32[]{:S(2)}, u32[]{:S(2)}) collective-permute-start(bf16[4,64,384]{2,1,0:T(8,128)(2,1)S(1)} %get-tuple-element.29), channel_id=1, source_target_pairs={{1,0},{2,1},{3,2},{5,4},{6,5},{7,6},{9,8},{10,9},{11,10},{13,12},{... | collective-permute-start | bytes 589832 | tf_op jit(solution)/shard_map/ppermute | solution.py:371
  14.3 4.4 %collective-permute-done.1.after = bf16[4,64,384]{2,1,0:T(8,128)(2,1)S(1)} collective-permute-done((bf16[4,64,384]{2,1,0:T(8,128)(2,1)S(1)}, bf16[4,64,384]{2,1,0:T(8,128)(2,1)S(1)}, u32[]{:S(2)}, u32[]{:S(2)}) %collective-permute-start.1) | collective-permute-done | bytes 196640 | tf_op jit(solution)/shard_map/ppermute | solution.py:371
  18.7 1.1 edge.2
  21.4 3.1 %collective-permute-start.5 = (bf16[32,32,384]{2,1,0:T(8,128)(2,1)S(1)}, bf16[32,32,384]{2,1,0:T(8,128)(2,1)S(1)}, u32[]{:S(2)}, u32[]{:S(2)}) collective-permute-start(bf16[32,32,384]{2,1,0:T(8,128)(2,1)S(1)} %constant_dynamic-update-slice_fusion.own_lo), channel_id=1, source_target_pairs={{0,4},{4,8},{8,12},{12,16},{16,20},{20,24},{24,28},{1,5},{5,9},{9,... | collective-permute-start | bytes 2359304 | tf_op jit(solution)/shard_map/ppermute | solution.py:352
  24.6 9.7 %embed.3 = (bf16[12,4,64,384]{3,2,1,0:T(8,128)(2,1)}, bf16[12,64,384]{2,1,0:T(8,128)(2,1)}, bf16[12,64,384]{2,1,0:T(8,128)(2,1)}, f32[16,96,384]{2,1,0:T(8,128)}...) custom-call(s32[8,1,512]{2,1,0:T(1,128)S(1)} %reshape.14.ids, bf16[16,4,64,384]{3,2,1,0:T(8,128)(2,1)} %frames.3, ...), custom_call_target="tpu_custom_call" | custom-call | flops 1000 | bytes 1000 | tf_op jit(solution)/shard_map/embed/pallas_call | solution.py:270
  35.3 5.0 %collective-permute-done.5.lo = bf16[32,32,384]{2,1,0:T(8,128)(2,1)S(1)} collective-permute-done((bf16[32,32,384]{2,1,0:T(8,128)(2,1)S(1)}, bf16[32,32,384]{2,1,0:T(8,128)(2,1)S(1)}, u32[]{:S(2)}, u32[]{:S(2)}) %collective-permute-start.5) | collective-permute-done | bytes 786464 | tf_op jit(solution)/shard_map/ppermute | solution.py:352
  41.3 1.5 %collective-permute-start.7 = (bf16[32,32,384]{2,1,0:T(8,128)(2,1)}, bf16[32,32,384]{2,1,0:T(8,128)(2,1)}, u32[]{:S(2)}, u32[]{:S(2)}) collective-permute-start(bf16[32,32,384]{2,1,0:T(8,128)(2,1)} %broadcast_select_fusion), channel_id=1, source_target_pairs={{0,16},{4,20},{1,17},{5,21},{2,18},{6,22},{3,19},{7,23}} | collective-permute-start | bytes 2359304 | tf_op jit(solution)/shard_map/ppermute | solution.py:361
  43.8 2.2 %collective-permute-start.2 = (bf16[8,96,384]{2,1,0:T(8,128)(2,1)S(1)}, bf16[8,96,384]{2,1,0:T(8,128)(2,1)S(1)}, u32[]{:S(2)}, u32[]{:S(2)}) collective-permute-start(bf16[8,96,384]{2,1,0:T(8,128)(2,1)S(1)} %get-tuple-element.50), channel_id=1, source_target_pairs={{0,4},{4,8},{8,12},{12,16},{16,20},{20,24},{24,28},{1,5},{5,9},{9,... | collective-permute-start | bytes 1769480 | tf_op jit(solution)/shard_map/ppermute | solution.py:352
  46.1 28.3 %collective-permute-done.2.hi = bf16[8,96,384]{2,1,0:T(8,128)(2,1)S(1)} collective-permute-done((bf16[8,96,384]{2,1,0:T(8,128)(2,1)S(1)}, bf16[8,96,384]{2,1,0:T(8,128)(2,1)S(1)}, u32[]{:S(2)}, u32[]{:S(2)}) %collective-permute-start.2) | collective-permute-done | bytes 589856 | tf_op jit(solution)/shard_map/ppermute | solution.py:352
  74.3 1.9 %collective-permute-start.3 = (bf16[12,64,384]{2,1,0:T(8,128)(2,1)}, bf16[12,64,384]{2,1,0:T(8,128)(2,1)S(1)}, u32[]{:S(2)}, u32[]{:S(2)}) collective-permute-start(bf16[12,64,384]{2,1,0:T(8,128)(2,1)} %get-tuple-element.35), channel_id=1, source_target_pairs={{0,1},{1,2},{2,3},{4,5},{5,6},{6,7},{8,9},{9,10},{10,11},{12,13},{... | collective-permute-start | bytes 1769480 | tf_op jit(solution)/shard_map/ppermute | solution.py:371
  76.3 2.4 %collective-permute-start.4 = (bf16[12,64,384]{2,1,0:T(8,128)(2,1)}, bf16[12,64,384]{2,1,0:T(8,128)(2,1)S(1)}, u32[]{:S(2)}, u32[]{:S(2)}) collective-permute-start(bf16[12,64,384]{2,1,0:T(8,128)(2,1)} %get-tuple-element.36), channel_id=1, source_target_pairs={{1,0},{2,1},{3,2},{5,4},{6,5},{7,6},{9,8},{10,9},{11,10},{13,12},{... | collective-permute-start | bytes 1769480 | tf_op jit(solution)/shard_map/ppermute | solution.py:371
  78.7 2.2 %broadcast_select_fusion.1 = bf16[32,32,384]{2,1,0:T(8,128)(2,1)} fusion(bf16[32,32,384]{2,1,0:T(8,128)(2,1)} %collective-permute-done.7, bf16[32,32,384]{2,1,0:T(8,128)(2,1)} %broadcast_select_fusion, pred[]{:T(512)S(6)} %or.7), kind=kLoop, calls=%fused_computation.1 | loop fusion | flops 393216 | bytes 2359297 | tf_op jit(solution)/shard_map/jit(_where)/select_n | solution.py:363
  80.9 1.3 collective-permute-start.8
  82.2 1.9 %collective-permute-start.10 = (bf16[8,96,384]{2,1,0:T(8,128)(2,1)}, bf16[8,96,384]{2,1,0:T(8,128)(2,1)}, u32[]{:S(2)}, u32[]{:S(2)}) collective-permute-start(bf16[8,96,384]{2,1,0:T(8,128)(2,1)} %get-tuple-element.49), channel_id=1, source_target_pairs={{0,4},{4,8},{8,12},{12,16},{16,20},{20,24},{24,28},{1,5},{5,9},{9,... | collective-permute-start | bytes 1769480 | tf_op jit(solution)/shard_map/ppermute | solution.py:352
  84.1 3.9 %collective-permute-done.4.after = bf16[12,64,384]{2,1,0:T(8,128)(2,1)S(1)} collective-permute-done((bf16[12,64,384]{2,1,0:T(8,128)(2,1)}, bf16[12,64,384]{2,1,0:T(8,128)(2,1)S(1)}, u32[]{:S(2)}, u32[]{:S(2)}) %collective-permute-start.4) | collective-permute-done | bytes 589856 | tf_op jit(solution)/shard_map/ppermute | solution.py:371
  90.0 5.1 %edge.3 = (f32[16,96,384]{2,1,0:T(8,128)S(1)}, bf16[16,96,384]{2,1,0:T(8,128)(2,1)S(1)}, bf16[16,96,384]{2,1,0:T(8,128)(2,1)S(1)}) custom-call(bf16[12,4,64,384]{3,2,1,0:T(8,128)(2,1)} %get-tuple-element.31.emb, bf16[12,64,384]{2,1,0:T(8,128)(2,1)S(1)} %collective-permute-done.3.before, bf16[12,64,384]{2,1,0:T(8,128)(2,1)S(1)} %copy-done.21, ...), custom_call_target="tpu_custom_call" | custom-call | flops 1000 | bytes 1000 | tf_op jit(solution)/shard_map/edge/pallas_call | solution.py:299
  95.1 1.4 copy-done.3
  96.5 1.1 copy-done.5
  97.6 1.1 fusion.3
  98.8 1.9 %collective-permute-start.9 = (bf16[8,96,384]{2,1,0:T(8,128)(2,1)}, bf16[8,96,384]{2,1,0:T(8,128)(2,1)}, u32[]{:S(2)}, u32[]{:S(2)}) collective-permute-start(bf16[8,96,384]{2,1,0:T(8,128)(2,1)} %get-tuple-element.51), channel_id=1, source_target_pairs={{0,4},{4,8},{8,12},{12,16},{16,20},{20,24},{24,28},{1,5},{5,9},{9,... | collective-permute-start | bytes 1769480 | tf_op jit(solution)/shard_map/ppermute | solution.py:352
  100.7 4.2 %collective-permute-start.6 = (bf16[8,96,384]{2,1,0:T(8,128)(2,1)}, bf16[8,96,384]{2,1,0:T(8,128)(2,1)}, u32[]{:S(2)}, u32[]{:S(2)}) collective-permute-start(bf16[8,96,384]{2,1,0:T(8,128)(2,1)} %get-tuple-element.52), channel_id=1, source_target_pairs={{0,4},{4,8},{8,12},{12,16},{16,20},{20,24},{24,28},{1,5},{5,9},{9,... | collective-permute-start | bytes 1769480 | tf_op jit(solution)/shard_map/ppermute | solution.py:352
  105.2 1.2 copy.16
  106.4 1.4 broadcast_select_fusion.2.anchors
  108.2 7.5 %attend.4.rest_0_ = bf16[16,4,64,384]{3,2,1,0:T(8,128)(2,1)} custom-call(s32[1]{0:T(128)} %bitcast.tm_ref, bf16[16,32,384]{2,1,0:T(8,128)(2,1)S(1)} %copy-done.15, bf16[16,96,384]{2,1,0:T(8,128)(2,1)} %copy-done.4, bf16[32,32,384]{2,1,0:T(8,128)(2,1)S(1)} %constant_dynamic-update-slice_fusion.own_lo, bf16[16,96,384]{2,1,0:T(8,128)(2,1)} %copy-done.1, ...), custom_call_target="tpu_custom_call" | custom-call | flops 1000 | bytes 1000 | tf_op jit(solution)/shard_map/attend/pallas_call | solution.py:328
  115.7 7.7 %attend.5.rest_0_ = bf16[16,4,64,384]{3,2,1,0:T(8,128)(2,1)} custom-call(s32[1]{0:T(128)} %bitcast.tm_ref, bf16[16,32,384]{2,1,0:T(8,128)(2,1)S(1)} %copy-done.15, bf16[16,96,384]{2,1,0:T(8,128)(2,1)} %copy-done.4, bf16[32,32,384]{2,1,0:T(8,128)(2,1)S(1)} %constant_dynamic-update-slice_fusion.own_lo, ...), custom_call_target="tpu_custom_call", output_to_operand_aliasing={{}: (14, {})} | custom-call | flops 1000 | bytes 1000 | tf_op jit(solution)/shard_map/attend/pallas_call | solution.py:328
  123.4 3.8 %collective-permute-done.9.hi = bf16[8,96,384]{2,1,0:T(8,128)(2,1)} collective-permute-done((bf16[8,96,384]{2,1,0:T(8,128)(2,1)}, bf16[8,96,384]{2,1,0:T(8,128)(2,1)}, u32[]{:S(2)}, u32[]{:S(2)}) %collective-permute-start.9) | collective-permute-done | bytes 589856 | tf_op jit(solution)/shard_map/ppermute | solution.py:352
  127.3 7.6 %attend.6.rest_0_ = bf16[16,4,64,384]{3,2,1,0:T(8,128)(2,1)} custom-call(s32[1]{0:T(128)} %bitcast.tm_ref, bf16[16,32,384]{2,1,0:T(8,128)(2,1)S(1)} %copy-done.17, bf16[16,96,384]{2,1,0:T(8,128)(2,1)} %copy-done.5, bf16[32,32,384]{2,1,0:T(8,128)(2,1)S(1)} %constant_dynamic-update-slice_fusion.own_lo, ...), custom_call_target="tpu_custom_call", output_to_operand_aliasing={{}: (14, {})} | custom-call | flops 1000 | bytes 1000 | tf_op jit(solution)/shard_map/attend/pallas_call | solution.py:328
  134.9 4.7 %collective-permute-done.6.hi = bf16[8,96,384]{2,1,0:T(8,128)(2,1)} collective-permute-done((bf16[8,96,384]{2,1,0:T(8,128)(2,1)}, bf16[8,96,384]{2,1,0:T(8,128)(2,1)}, u32[]{:S(2)}, u32[]{:S(2)}) %collective-permute-start.6) | collective-permute-done | bytes 589856 | tf_op jit(solution)/shard_map/ppermute | solution.py:352
  139.6 7.6 %attend.7 = bf16[16,4,64,384]{3,2,1,0:T(8,128)(2,1)} custom-call(s32[1]{0:T(128)} %bitcast.tm_ref, bf16[16,32,384]{2,1,0:T(8,128)(2,1)S(1)} %copy-done.17, bf16[16,96,384]{2,1,0:T(8,128)(2,1)} %copy-done.5, bf16[32,32,384]{2,1,0:T(8,128)(2,1)S(1)} %constant_dynamic-update-slice_fusion.own_lo, ...), custom_call_target="tpu_custom_call", output_to_operand_aliasing={{}: (14, {})} | custom-call | flops 1000 | bytes 1000 | tf_op jit(solution)/shard_map/attend/pallas_call | solution.py:328
  (57 shorter events, 11.0 us)
Async XLA Ops:
  0.0 2.3 %copy-start = (bf16[8,384]{1,0:T(8,128)(2,1)S(1)}, bf16[8,384]{1,0:T(8,128)(2,1)}, u32[]{:S(2)}) copy-start(bf16[8,384]{1,0:T(8,128)(2,1)} %param.15) | copy-start | bytes 18436
  3.1 1.1 copy-start.12
  7.9 10.8 %copy-start.10 = (f32[16,32,384]{2,1,0:T(8,128)}, f32[16,32,384]{2,1,0:T(8,128)S(1)}, u32[]{:S(2)}) copy-start(f32[16,32,384]{2,1,0:T(8,128)S(1)} %get-tuple-element.47.m_lo) | copy-start | bytes 2359300
  7.9 12.7 %copy-start.14 = (bf16[16,32,384]{2,1,0:T(8,128)(2,1)}, bf16[16,32,384]{2,1,0:T(8,128)(2,1)S(1)}, u32[]{:S(2)}) copy-start(bf16[16,32,384]{2,1,0:T(8,128)(2,1)S(1)} %get-tuple-element.45.x_lo) | copy-start | bytes 1179652
  7.9 16.7 %copy-start.13 = (bf16[1024,384]{1,0:T(8,128)(2,1)S(1)}, bf16[1024,384]{1,0:T(8,128)(2,1)}, u32[]{:S(2)}) copy-start(bf16[1024,384]{1,0:T(8,128)(2,1)} %table.3) | copy-start | bytes 2359300
  7.9 6.4 %collective-permute-start = (bf16[4,64,384]{2,1,0:T(8,128)(2,1)S(1)}, bf16[4,64,384]{2,1,0:T(8,128)(2,1)S(1)}, u32[]{:S(2)}, u32[]{:S(2)}) collective-permute-start(bf16[4,64,384]{2,1,0:T(8,128)(2,1)S(1)} %get-tuple-element.28), channel_id=1, source_target_pairs={{0,1},{1,2},{2,3},{4,5},{5,6},{6,7},{8,9},{9,10},{10,11},{12,13},{... | collective-permute-start | bytes 589832 | tf_op jit(solution)/shard_map/ppermute | solution.py:371
  11.7 7.0 %collective-permute-start.1 = (bf16[4,64,384]{2,1,0:T(8,128)(2,1)S(1)}, bf16[4,64,384]{2,1,0:T(8,128)(2,1)S(1)}, u32[]{:S(2)}, u32[]{:S(2)}) collective-permute-start(bf16[4,64,384]{2,1,0:T(8,128)(2,1)S(1)} %get-tuple-element.29), channel_id=1, source_target_pairs={{1,0},{2,1},{3,2},{5,4},{6,5},{7,6},{9,8},{10,9},{11,10},{13,12},{... | collective-permute-start | bytes 589832 | tf_op jit(solution)/shard_map/ppermute | solution.py:371
  20.5 0.9 copy-start.8
  21.4 18.9 %collective-permute-start.5 = (bf16[32,32,384]{2,1,0:T(8,128)(2,1)S(1)}, bf16[32,32,384]{2,1,0:T(8,128)(2,1)S(1)}, u32[]{:S(2)}, u32[]{:S(2)}) collective-permute-start(bf16[32,32,384]{2,1,0:T(8,128)(2,1)S(1)} %constant_dynamic-update-slice_fusion.own_lo), channel_id=1, source_target_pairs={{0,4},{4,8},{8,12},{12,16},{16,20},{20,24},{24,28},{1,5},{5,9},{9,... | collective-permute-start | bytes 2359304 | tf_op jit(solution)/shard_map/ppermute | solution.py:352
  34.3 1.1 copy-start.4
  35.3 8.5 %copy-start.1 = (bf16[16,96,384]{2,1,0:T(8,128)(2,1)}, bf16[16,96,384]{2,1,0:T(8,128)(2,1)S(1)}, u32[]{:S(2)}) copy-start(bf16[16,96,384]{2,1,0:T(8,128)(2,1)S(1)} %get-tuple-element.34.own_hi) | copy-start | bytes 3538948
  41.3 37.4 %collective-permute-start.7 = (bf16[32,32,384]{2,1,0:T(8,128)(2,1)}, bf16[32,32,384]{2,1,0:T(8,128)(2,1)}, u32[]{:S(2)}, u32[]{:S(2)}) collective-permute-start(bf16[32,32,384]{2,1,0:T(8,128)(2,1)} %broadcast_select_fusion), channel_id=1, source_target_pairs={{0,16},{4,20},{1,17},{5,21},{2,18},{6,22},{3,19},{7,23}} | collective-permute-start | bytes 2359304 | tf_op jit(solution)/shard_map/ppermute | solution.py:361
  43.8 30.5 %collective-permute-start.2 = (bf16[8,96,384]{2,1,0:T(8,128)(2,1)S(1)}, bf16[8,96,384]{2,1,0:T(8,128)(2,1)S(1)}, u32[]{:S(2)}, u32[]{:S(2)}) collective-permute-start(bf16[8,96,384]{2,1,0:T(8,128)(2,1)S(1)} %get-tuple-element.50), channel_id=1, source_target_pairs={{0,4},{4,8},{8,12},{12,16},{16,20},{20,24},{24,28},{1,5},{5,9},{9,... | collective-permute-start | bytes 1769480 | tf_op jit(solution)/shard_map/ppermute | solution.py:352
  74.3 13.7 %copy-start.18 = (bf16[8,96,384]{2,1,0:T(8,128)(2,1)}, bf16[8,96,384]{2,1,0:T(8,128)(2,1)S(1)}, u32[]{:S(2)}) copy-start(bf16[8,96,384]{2,1,0:T(8,128)(2,1)S(1)} %collective-permute-done.2.hi) | copy-start | bytes 1769476
  74.3 9.8 %collective-permute-start.3 = (bf16[12,64,384]{2,1,0:T(8,128)(2,1)}, bf16[12,64,384]{2,1,0:T(8,128)(2,1)S(1)}, u32[]{:S(2)}, u32[]{:S(2)}) collective-permute-start(bf16[12,64,384]{2,1,0:T(8,128)(2,1)} %get-tuple-element.35), channel_id=1, source_target_pairs={{0,1},{1,2},{2,3},{4,5},{5,6},{6,7},{8,9},{9,10},{10,11},{12,13},{... | collective-permute-start | bytes 1769480 | tf_op jit(solution)/shard_map/ppermute | solution.py:371
  76.3 11.8 %collective-permute-start.4 = (bf16[12,64,384]{2,1,0:T(8,128)(2,1)}, bf16[12,64,384]{2,1,0:T(8,128)(2,1)S(1)}, u32[]{:S(2)}, u32[]{:S(2)}) collective-permute-start(bf16[12,64,384]{2,1,0:T(8,128)(2,1)} %get-tuple-element.36), channel_id=1, source_target_pairs={{1,0},{2,1},{3,2},{5,4},{6,5},{7,6},{9,8},{10,9},{11,10},{13,12},{... | collective-permute-start | bytes 1769480 | tf_op jit(solution)/shard_map/ppermute | solution.py:371
  80.9 25.5 %collective-permute-start.8 = (bf16[32,32,384]{2,1,0:T(8,128)(2,1)}, bf16[32,32,384]{2,1,0:T(8,128)(2,1)}, u32[]{:S(2)}, u32[]{:S(2)}) collective-permute-start(bf16[32,32,384]{2,1,0:T(8,128)(2,1)} %broadcast_select_fusion.1), channel_id=1, source_target_pairs={{0,8},{4,12},{16,24},{20,28},{1,9},{5,13},{17,25},{21,29},{2,10},{... | collective-permute-start | bytes 2359304 | tf_op jit(solution)/shard_map/ppermute | solution.py:361
  82.2 33.5 %collective-permute-start.10 = (bf16[8,96,384]{2,1,0:T(8,128)(2,1)}, bf16[8,96,384]{2,1,0:T(8,128)(2,1)}, u32[]{:S(2)}, u32[]{:S(2)}) collective-permute-start(bf16[8,96,384]{2,1,0:T(8,128)(2,1)} %get-tuple-element.49), channel_id=1, source_target_pairs={{0,4},{4,8},{8,12},{12,16},{16,20},{20,24},{24,28},{1,5},{5,9},{9,... | collective-permute-start | bytes 1769480 | tf_op jit(solution)/shard_map/ppermute | solution.py:352
  88.9 1.1 copy-start.21
  95.1 1.4 copy-start.3
  96.5 1.1 copy-start.5
  97.6 10.2 %copy-start.2 = (bf16[16,96,384]{2,1,0:T(8,128)(2,1)}, bf16[16,96,384]{2,1,0:T(8,128)(2,1)S(1)}, u32[]{:S(2)}) copy-start(bf16[16,96,384]{2,1,0:T(8,128)(2,1)S(1)} %get-tuple-element.42.own_hi) | copy-start | bytes 3538948
  97.6 7.3 %copy-start.22 = (bf16[384,384]{1,0:T(8,128)(2,1)S(1)}, bf16[384,384]{1,0:T(8,128)(2,1)}, u32[]{:S(2)}) copy-start(bf16[384,384]{1,0:T(8,128)(2,1)} %param.18) | copy-start | bytes 884740
  98.8 28.5 %collective-permute-start.9 = (bf16[8,96,384]{2,1,0:T(8,128)(2,1)}, bf16[8,96,384]{2,1,0:T(8,128)(2,1)}, u32[]{:S(2)}, u32[]{:S(2)}) collective-permute-start(bf16[8,96,384]{2,1,0:T(8,128)(2,1)} %get-tuple-element.51), channel_id=1, source_target_pairs={{0,4},{4,8},{8,12},{12,16},{16,20},{20,24},{24,28},{1,5},{5,9},{9,... | collective-permute-start | bytes 1769480 | tf_op jit(solution)/shard_map/ppermute | solution.py:352
  100.7 38.9 %collective-permute-start.6 = (bf16[8,96,384]{2,1,0:T(8,128)(2,1)}, bf16[8,96,384]{2,1,0:T(8,128)(2,1)}, u32[]{:S(2)}, u32[]{:S(2)}) collective-permute-start(bf16[8,96,384]{2,1,0:T(8,128)(2,1)} %get-tuple-element.52), channel_id=1, source_target_pairs={{0,4},{4,8},{8,12},{12,16},{16,20},{20,24},{24,28},{1,5},{5,9},{9,... | collective-permute-start | bytes 1769480 | tf_op jit(solution)/shard_map/ppermute | solution.py:352
  106.3 1.5 copy-start.6
  106.4 1.5 copy-start.7
  106.4 1.5 %copy-start.11 = (f32[16,32,384]{2,1,0:T(8,128)S(1)}, f32[16,32,384]{2,1,0:T(8,128)}, u32[]{:S(2)}) copy-start(f32[16,32,384]{2,1,0:T(8,128)} %copy-done.10) | copy-start | bytes 2359300
  106.4 1.6 %copy-start.15 = (bf16[16,32,384]{2,1,0:T(8,128)(2,1)S(1)}, bf16[16,32,384]{2,1,0:T(8,128)(2,1)}, u32[]{:S(2)}) copy-start(bf16[16,32,384]{2,1,0:T(8,128)(2,1)} %copy-done.14) | copy-start | bytes 1179652
  106.4 1.8 %copy-start.19 = (bf16[8,96,384]{2,1,0:T(8,128)(2,1)S(1)}, bf16[8,96,384]{2,1,0:T(8,128)(2,1)}, u32[]{:S(2)}) copy-start(bf16[8,96,384]{2,1,0:T(8,128)(2,1)} %copy-done.18) | copy-start | bytes 1769476
  115.7 11.6 %copy-start.9 = (f32[16,32,384]{2,1,0:T(8,128)S(1)}, f32[16,32,384]{2,1,0:T(8,128)}, u32[]{:S(2)}) copy-start(f32[16,32,384]{2,1,0:T(8,128)} %copy-done.8) | copy-start | bytes 2359300
  115.7 11.6 %copy-start.17 = (bf16[16,32,384]{2,1,0:T(8,128)(2,1)S(1)}, bf16[16,32,384]{2,1,0:T(8,128)(2,1)}, u32[]{:S(2)}) copy-start(bf16[16,32,384]{2,1,0:T(8,128)(2,1)} %copy-done.16) | copy-start | bytes 1179652
  (2 other events, 1.6 us)
